TPU v7x, 128 devices: a whole 4x4x4 slice. The times are simulated.
128 devices in a mesh: dp: 16 (over z, y), grp: 8 (over x, core).
Axes of the slice: x: 4, y: 4, z: 4, core: 2. Of those that a mesh axis runs over, the one named last changes fastest.
Arguments:
- frames: bfloat16 [384, 256, 1024], P(('dp', 'grp')), may hold values from -6 to 6
- episode_len: int32 [48], replicated, may hold values from 1 to 64, 384 in all
- norm_spatial: float32 [1024], replicated, may hold values from 0.25 to 1.75
- w_sqkv: bfloat16 [1024, 3072], replicated
- w_so: bfloat16 [1024, 1024], replicated, may hold values from -0.1875 to 0.1875
- norm_temporal: float32 [1024], replicated, may hold values from 0.25 to 1.75
- w_tqkv: bfloat16 [1024, 3072], P(('dp', 'grp'))
- w_to: bfloat16 [1024, 1024], P(('dp', 'grp')), may hold values from -0.1875 to 0.1875
Outputs:
- block_out: bfloat16 [384, 256, 1024], P(('dp', 'grp'))
Inputs may be any that keep to these rules, and one draw needn't show every extreme that they name: episode_len lists consecutive episodes that together cover all 384 frames; the longest has exactly 64 frames.
All inputs are finite; a program needn't handle non-finite values.
Results may differ from a plain program's by a relative error of at most 0.029.
The roundings to bfloat16 on the way count: a program that leaves them out, or rounds other values in their place, can miss the bound.
Values may be sent and summed in bfloat16 or wider, within the bound.
No kernel may reach another device: no remote copies, remote signals or barrier semaphores. Data moves between devices by JAX's collectives and lax.ppermute only.
A program may use at most 128 MiB of HBM per device.

v0:
```python
import jax
import jax.numpy as jnp
from jax import lax
from jax.sharding import PartitionSpec as P

HEADS = 16


def normed(values, gain):
    wide = values.astype(jnp.float32)
    scale = lax.rsqrt(jnp.mean(wide * wide, axis=-1, keepdims=True) + 1e-06)
    return (wide * scale * gain).astype(jnp.bfloat16)


def softmax_rows(scores):
    top = jnp.max(scores, axis=-1, keepdims=True)
    weights = jnp.exp(scores - top)
    return (weights / jnp.sum(weights, axis=-1, keepdims=True)).astype(jnp.bfloat16)


def local(frames, episode_len, norm_spatial, w_sqkv, w_so, norm_temporal, w_tqkv, w_to):
    count, tokens, width = frames.shape
    head_dim = width // HEADS
    scale = head_dim ** (-0.5)
    full_tqkv, full_to = (
        lax.all_gather(w_tqkv, ("dp", "grp"), axis=0, tiled=True),
        lax.all_gather(w_to, ("dp", "grp"), axis=0, tiled=True),
    )
    hidden = normed(frames, norm_spatial).reshape(count * tokens, width)
    sqkv = jnp.dot(hidden, w_sqkv, preferred_element_type=jnp.float32).astype(jnp.bfloat16)
    sqkv = sqkv.reshape(count, tokens, 3 * width)

    def spatial_frame(block):
        queries = block[:, :width].reshape(tokens, HEADS, head_dim)
        keys_part = block[:, width : 2 * width].reshape(tokens, HEADS, head_dim)
        values_part = block[:, 2 * width :].reshape(tokens, HEADS, head_dim)
        scores = (
            jnp.einsum("phd,qhd->hpq", queries, keys_part, preferred_element_type=jnp.float32)
            * scale
        )
        probs = softmax_rows(scores)
        heads = jnp.einsum("hpq,qhd->phd", probs, values_part, preferred_element_type=jnp.float32)
        return heads.astype(jnp.bfloat16).reshape(tokens, width)

    spatial_heads = lax.map(spatial_frame, sqkv).reshape(count * tokens, width)
    update = jnp.dot(spatial_heads, w_so, preferred_element_type=jnp.float32).reshape(
        count, tokens, width
    )
    mixed = (frames.astype(jnp.float32) + update).astype(jnp.bfloat16)
    temporal_in = normed(mixed, norm_temporal)
    columns = lax.all_to_all(temporal_in, ("dp", "grp"), split_axis=1, concat_axis=0, tiled=True)
    total, local_pos, _ = columns.shape
    tqkv = jnp.dot(
        columns.reshape(total * local_pos, width), full_tqkv, preferred_element_type=jnp.float32
    )
    tqkv = tqkv.astype(jnp.bfloat16).reshape(total, local_pos, 3 * width)
    ends = jnp.cumsum(episode_len)
    position = jnp.arange(total, dtype=jnp.int32)
    episode = jnp.sum((position[:, None] >= ends[None, :]).astype(jnp.int32), axis=1)
    allowed = (position[None, :] <= position[:, None]) & (episode[None, :] == episode[:, None])
    outputs = []
    for slot_index in range(local_pos):
        block = tqkv[:, slot_index]
        queries = block[:, :width].reshape(total, HEADS, head_dim)
        keys_part = block[:, width : 2 * width].reshape(total, HEADS, head_dim)
        values_part = block[:, 2 * width :].reshape(total, HEADS, head_dim)
        scores = (
            jnp.einsum("fhd,ghd->hfg", queries, keys_part, preferred_element_type=jnp.float32)
            * scale
        )
        scores = jnp.where(allowed[None], scores, -1e30)
        probs = softmax_rows(scores)
        heads = jnp.einsum("hfg,ghd->fhd", probs, values_part, preferred_element_type=jnp.float32)
        outputs.append(heads.astype(jnp.bfloat16).reshape(total, width))
    temporal_heads = jnp.stack(outputs, axis=1).reshape(total * local_pos, width)
    temporal_update = jnp.dot(temporal_heads, full_to, preferred_element_type=jnp.float32).astype(
        jnp.bfloat16
    )
    temporal_update = temporal_update.reshape(total, local_pos, width)
    returned = lax.all_to_all(
        temporal_update, ("dp", "grp"), split_axis=0, concat_axis=1, tiled=True
    )
    return (mixed.astype(jnp.float32) + returned.astype(jnp.float32)).astype(jnp.bfloat16)


def solution(mesh):
    placed = (
        P(("dp", "grp"), None, None),
        P(),
        P(),
        P(),
        P(),
        P(),
        P(("dp", "grp"), None),
        P(("dp", "grp"), None),
    )
    return jax.shard_map(
        local, mesh=mesh, in_specs=placed, out_specs=P(("dp", "grp"), None, None), check_vma=False
    )
```

profile of v0, /device:TPU:1, one launch (start us, length us, event | category | flops | bytes accessed | tf_op | source)
XLA Modules:
  0.0 261.2 jit_solution(18136565001263562111)
XLA Ops:
  10.9 9.5 %convolution_convert_fusion.1 = bf16[768,3072]{1,0:T(8,128)(2,1)} fusion(bf16[768,1024]{1,0:T(8,128)(2,1)S(1)} %bitcast.88, bf16[1024,3072]{1,0:T(8,128)(2,1)} %param.13), kind=kOutput, calls=%fused_computation.23 | convolution fusion | flops 4834197504 | bytes 12582912 | tf_op jit(solution)/shard_map/dot_general | solution.py:30
  20.4 47.2 %while.10 = (s32[]{:T(128)}, bf16[3,256,1024]{1,2,0:T(8,128)(2,1)}, bf16[3,256,3072]{2,1,0:T(8,128)(2,1)}, s32[]{:T(128)}) while((s32[]{:T(128)}, bf16[3,256,1024]{1,2,0:T(8,128)(2,1)}, bf16[3,256,3072]{2,1,0:T(8,128)(2,1)}, s32[]{:T(128)}) %tuple.45), condition=%wide.region_4.5_spmd, body=%wide.region_1.4_spmd.sunk | while | flops 273940736 | bytes 21004356 | solution.py:45
  20.4 2.7 %constant_dynamic-slice_fusion.2 = bf16[1,256,3072]{2,1,0:T(8,128)(2,1)} fusion(bf16[3,256,3072]{2,1,0:T(8,128)(2,1)} %get-tuple-element.101, s32[]{:T(128)S(6)} %copy.93), kind=kLoop, calls=%fused_computation.10.clone.1 | loop fusion | bytes 3145732 | tf_op jit(solution)/shard_map/while/body/jit(dynamic_index_in_dim)/dynamic_slice | solution.py:45
  23.1 2.6 copy.89
  28.0 4.6 %fusion.84 = (f32[16,256]{1,0:T(8,128)S(1)}, f32[16,256,256]{1,2,0:T(8,128)}) fusion(bf16[256,16,64]{0,2,1:T(8,128)(2,1)} %bitcast.84, bf16[256,16,64]{0,2,1:T(8,128)(2,1)S(1)} %bitcast.83), kind=kOutput, calls=%fused_computation.69.clone.1 | convolution fusion | flops 137363712 | bytes 5259264 | tf_op jit(solution)/shard_map/while/body/eval_jaxpr/sub | solution.py:17
  32.6 2.7 %fusion.85 = bf16[16,64,256]{2,1,0:T(8,128)(2,1)S(1)} fusion(bf16[256,16,64]{0,2,1:T(8,128)(2,1)S(1)} %bitcast.82, f32[16,256,256]{1,2,0:T(8,128)} %get-tuple-element.89, f32[16,256]{1,0:T(8,128)S(1)} %get-tuple-element.90), kind=kOutput, calls=%fused_computation.7.clone.1 | convolution fusion | flops 136577024 | bytes 5259264 | tf_op jit(solution)/shard_map/while/body/eval_jaxpr/hpq,qhd->phd/dot_general | solution.py:42
  36.1 2.7 %constant_dynamic-slice_fusion.2 = bf16[1,256,3072]{2,1,0:T(8,128)(2,1)} fusion(bf16[3,256,3072]{2,1,0:T(8,128)(2,1)} %get-tuple-element.101, s32[]{:T(128)S(6)} %copy.93), kind=kLoop, calls=%fused_computation.10.clone.1 | loop fusion | bytes 3145732 | tf_op jit(solution)/shard_map/while/body/jit(dynamic_index_in_dim)/dynamic_slice | solution.py:45
  43.7 4.7 %fusion.84 = (f32[16,256]{1,0:T(8,128)S(1)}, f32[16,256,256]{1,2,0:T(8,128)}) fusion(bf16[256,16,64]{0,2,1:T(8,128)(2,1)} %bitcast.84, bf16[256,16,64]{0,2,1:T(8,128)(2,1)S(1)} %bitcast.83), kind=kOutput, calls=%fused_computation.69.clone.1 | convolution fusion | flops 137363712 | bytes 5259264 | tf_op jit(solution)/shard_map/while/body/eval_jaxpr/sub | solution.py:17
  48.3 2.7 %fusion.85 = bf16[16,64,256]{2,1,0:T(8,128)(2,1)S(1)} fusion(bf16[256,16,64]{0,2,1:T(8,128)(2,1)S(1)} %bitcast.82, f32[16,256,256]{1,2,0:T(8,128)} %get-tuple-element.89, f32[16,256]{1,0:T(8,128)S(1)} %get-tuple-element.90), kind=kOutput, calls=%fused_computation.7.clone.1 | convolution fusion | flops 136577024 | bytes 5259264 | tf_op jit(solution)/shard_map/while/body/eval_jaxpr/hpq,qhd->phd/dot_general | solution.py:42
  51.9 2.7 %constant_dynamic-slice_fusion.2 = bf16[1,256,3072]{2,1,0:T(8,128)(2,1)} fusion(bf16[3,256,3072]{2,1,0:T(8,128)(2,1)} %get-tuple-element.101, s32[]{:T(128)S(6)} %copy.93), kind=kLoop, calls=%fused_computation.10.clone.1 | loop fusion | bytes 3145732 | tf_op jit(solution)/shard_map/while/body/jit(dynamic_index_in_dim)/dynamic_slice | solution.py:45
  59.5 4.6 %fusion.84 = (f32[16,256]{1,0:T(8,128)S(1)}, f32[16,256,256]{1,2,0:T(8,128)}) fusion(bf16[256,16,64]{0,2,1:T(8,128)(2,1)} %bitcast.84, bf16[256,16,64]{0,2,1:T(8,128)(2,1)S(1)} %bitcast.83), kind=kOutput, calls=%fused_computation.69.clone.1 | convolution fusion | flops 137363712 | bytes 5259264 | tf_op jit(solution)/shard_map/while/body/eval_jaxpr/sub | solution.py:17
  64.1 2.7 %fusion.85 = bf16[16,64,256]{2,1,0:T(8,128)(2,1)S(1)} fusion(bf16[256,16,64]{0,2,1:T(8,128)(2,1)S(1)} %bitcast.82, f32[16,256,256]{1,2,0:T(8,128)} %get-tuple-element.89, f32[16,256]{1,0:T(8,128)S(1)} %get-tuple-element.90), kind=kOutput, calls=%fused_computation.7.clone.1 | convolution fusion | flops 136577024 | bytes 5259264 | tf_op jit(solution)/shard_map/while/body/eval_jaxpr/hpq,qhd->phd/dot_general | solution.py:42
  67.6 4.1 %fusion.26 = (f32[3,256]{1,0:T(4,128)S(1)}, bf16[3,256,1024]{2,1,0:T(8,128)(2,1)S(1)}) fusion(bf16[3,256,1024]{1,2,0:T(8,128)(2,1)} %get-tuple-element.22, bf16[1024,1024]{1,0:T(8,128)(2,1)S(1)} %copy-done, bf16[3,256,1024]{2,1,0:T(8,128)(2,1)} %param.10), kind=kOutput, calls=%fused_computation.42 | convolution fusion | flops 1615330560 | bytes 6818816 | tf_op jit(solution)/shard_map/dot_general | solution.py:46
  73.3 2.7 %copy.61 = bf16[3,256,1024]{2,0,1:T(4,128)(2,1)} copy(bf16[3,256,1024]{2,1,0:T(8,128)(2,1)S(1)} %fusion.28) | data formatting | bytes 3145728 | tf_op jit(solution)/shard_map/convert_element_type | solution.py:12
  76.0 11.6 %all-to-all-start = ((bf16[3,256,1024]{2,0,1:T(4,128)(2,1)}), bf16[3,256,1024]{2,0,1:T(4,128)(2,1)S(1)}, u32[]{:S(2)}, u32[]{:S(2)}) async-start(bf16[3,256,1024]{2,0,1:T(4,128)(2,1)} %copy.61), calls=%async_computation | async-start | bytes 4194304 | tf_op jit(solution)/shard_map/all_to_all | solution.py:51
  88.9 29.4 %all-to-all-done = bf16[3,256,1024]{2,0,1:T(4,128)(2,1)S(1)} async-done(((bf16[3,256,1024]{2,0,1:T(4,128)(2,1)}), bf16[3,256,1024]{2,0,1:T(4,128)(2,1)S(1)}, u32[]{:S(2)}, u32[]{:S(2)}) %all-to-all-start) | async-done | bytes 1572896 | tf_op jit(solution)/shard_map/all_to_all | solution.py:51
  123.3 9.5 %convolution_convert_fusion = bf16[768,3072]{1,0:T(8,128)(2,1)} fusion(bf16[768,1024]{1,0:T(8,128)(2,1)S(1)} %reshape.146, bf16[1024,3072]{1,0:T(8,128)(2,1)} %all-gather.3.cloned.1.call-done), kind=kOutput, calls=%fused_computation.22 | convolution fusion | flops 4834197504 | bytes 12582912 | tf_op jit(solution)/shard_map/dot_general | solution.py:53
  132.8 10.3 %reshape.147 = bf16[384,2,3072]{2,1,0:T(2,128)(2,1)} reshape(bf16[768,3072]{1,0:T(8,128)(2,1)} %convolution_convert_fusion) | data formatting | bytes 9437184 | tf_op jit(solution)/shard_map/reshape | solution.py:56
  143.1 9.8 %fusion.47 = (bf16[384,1,3072]{2,1,0:T(2,128)(2,1)S(1)}, bf16[384,1,3072]{2,1,0:T(2,128)(2,1)S(1)}) fusion(bf16[384,2,3072]{2,1,0:T(2,128)(2,1)} %reshape.147), kind=kLoop, calls=%fused_computation.70 | loop fusion | bytes 9437184 | tf_op jit(solution)/shard_map/slice | solution.py:63
  153.0 3.1 %copy_bitcast_fusion = (bf16[384,3072]{1,0:T(8,128)(2,1)S(1)}, bf16[384,3072]{1,0:T(8,128)(2,1)}) fusion(bf16[384,1,3072]{2,1,0:T(2,128)(2,1)S(1)} %get-tuple-element.47, bf16[384,1,3072]{2,1,0:T(2,128)(2,1)S(1)} %get-tuple-element.46), kind=kLoop, calls=%fused_computation.47 | loop fusion | bytes 9437184 | tf_op jit(solution)/shard_map/squeeze | solution.py:63
  158.2 5.6 %fusion.50 = (f32[16,384]{1,0:T(8,128)S(1)}, f32[16,384,384]{1,2,0:T(8,128)}) fusion(pred[384,384]{0,1:T(8,128)(4,1)S(1)} %fusion.40, bf16[384,16,64]{0,2,1:T(8,128)(2,1)S(1)} %bitcast.92, bf16[384,16,64]{0,2,1:T(8,128)(2,1)S(1)} %bitcast.94), kind=kOutput, calls=%fused_computation.73 | convolution fusion | flops 311427456 | bytes 11182080 | tf_op jit(solution)/shard_map/sub | solution.py:17
  163.8 4.5 %fusion.34 = bf16[16,64,384]{2,1,0:T(8,128)(2,1)S(1)} fusion(bf16[384,16,64]{0,2,1:T(8,128)(2,1)S(1)} %bitcast.90, f32[16,384,384]{1,2,0:T(8,128)} %get-tuple-element.57, f32[16,384]{1,0:T(8,128)S(1)} %get-tuple-element.56), kind=kOutput, calls=%fused_computation.54 | convolution fusion | flops 307101696 | bytes 11034624 | tf_op jit(solution)/shard_map/hfg,ghd->fhd/dot_general | solution.py:73
  170.0 3.0 %fusion.48 = (bf16[384,1024]{1,0:T(8,128)(2,1)S(1)}, bf16[384,1024]{1,0:T(8,128)(2,1)}, bf16[384,1024]{1,0:T(8,128)(2,1)}) fusion(bf16[384,3072]{1,0:T(8,128)(2,1)} %get-tuple-element.61), kind=kLoop, calls=%fused_computation.71 | loop fusion | bytes 4718592 | tf_op jit(solution)/shard_map/slice | solution.py:65
  178.8 8.2 %fusion.51 = (f32[16,384]{1,0:T(8,128)S(1)}, f32[16,384,384]{1,2,0:T(8,128)}) fusion(pred[384,384]{0,1:T(8,128)(4,1)S(1)} %fusion.40, bf16[384,16,64]{0,2,1:T(8,128)(2,1)} %bitcast.91, bf16[384,16,64]{0,2,1:T(8,128)(2,1)} %bitcast.93), kind=kOutput, calls=%fused_computation.74 | convolution fusion | flops 311427456 | bytes 11182080 | tf_op jit(solution)/shard_map/sub | solution.py:17
  187.0 5.4 %fusion.35 = bf16[16,64,384]{2,1,0:T(8,128)(2,1)} fusion(bf16[384,16,64]{0,2,1:T(8,128)(2,1)S(1)} %bitcast.89, f32[16,384,384]{1,2,0:T(8,128)} %get-tuple-element.59, f32[16,384]{1,0:T(8,128)S(1)} %get-tuple-element.58), kind=kOutput, calls=%fused_computation.55 | convolution fusion | flops 307101696 | bytes 11034624 | tf_op jit(solution)/shard_map/hfg,ghd->fhd/dot_general | solution.py:73
  192.4 4.8 %copy.74 = bf16[384,1,1024]{2,1,0:T(2,128)(2,1)} copy(bf16[384,1,1024]{0,2,1:T(8,128)(2,1)} %bitcast.96) | data formatting | bytes 1572864 | tf_op jit(solution)/shard_map/stack;reshape | solution.py:75
  197.1 5.5 %pad_maximum_fusion = bf16[384,2,1024]{2,1,0:T(2,128)(2,1)} fusion(bf16[384,1,1024]{2,1,0:T(2,128)(2,1)S(1)} %copy.75, bf16[384,1,1024]{2,1,0:T(2,128)(2,1)} %copy.74), kind=kLoop, calls=%fused_computation.52 | loop fusion | flops 3145728 | bytes 3145728 | tf_op jit(solution)/shard_map/stack | solution.py:75
  205.2 4.5 %convolution_convert_fusion.2 = bf16[768,1024]{1,0:T(8,128)(2,1)} fusion(bf16[768,1024]{1,0:T(8,128)(2,1)S(1)} %reshape.156, bf16[1024,1024]{1,0:T(8,128)(2,1)} %all-gather.5.cloned.1.call-done), kind=kOutput, calls=%fused_computation.51 | convolution fusion | flops 1611399168 | bytes 5242880 | tf_op jit(solution)/shard_map/dot_general | solution.py:76
  212.2 28.8 %all_to_all.24 = bf16[384,2,1024]{2,1,0:T(2,128)(2,1)S(1)} all-to-all(bf16[384,2,1024]{2,1,0:T(2,128)(2,1)S(1)} %reshape.157), channel_id=1, replica_groups=mesh['dp'=16,'grp'=8] {'dp','grp'}, dimensions={0} | all-to-all | bytes 3145728 | tf_op jit(solution)/shard_map/all_to_all | solution.py:80
  242.0 2.9 %copy.76 = f32[3,128,2,1024]{3,2,1,0:T(2,128)} copy(f32[3,128,2,1024]{3,2,0,1:T(2,128)S(1)} %convert_bitcast_fusion) | data formatting | bytes 6291456 | tf_op jit(solution)/shard_map/convert_element_type | solution.py:83
  244.9 5.4 %reshape.158 = f32[3,256,1024]{2,1,0:T(8,128)} reshape(f32[3,128,2,1024]{3,2,1,0:T(2,128)} %copy.76) | data formatting | bytes 6291456 | tf_op jit(solution)/shard_map/convert_element_type | solution.py:83
  250.3 4.1 %fusion.29 = bf16[3,256,1024]{2,1,0:T(8,128)(2,1)} fusion(f32[3,256,1024]{2,1,0:T(8,128)} %reshape.158, bf16[3,256,1024]{2,1,0:T(8,128)(2,1)} %copy-done.2), kind=kLoop, calls=%fused_computation.45 | loop fusion | flops 2359296 | bytes 6291456 | tf_op jit(solution)/shard_map/convert_element_type | solution.py:83
  (52 shorter events, 42.3 us)
Async XLA Ops:
  6.5 61.1 %copy-start = (bf16[1024,1024]{1,0:T(8,128)(2,1)S(1)}, bf16[1024,1024]{1,0:T(8,128)(2,1)}, u32[]{:S(2)}) copy-start(bf16[1024,1024]{1,0:T(8,128)(2,1)} %param.14) | copy-start | bytes 6291460
  6.5 116.8 %all-gather.3.cloned.1.call-start = ((), (), s32[]{:S(2)}) async-start(), calls=%async_computation.2 | async-start | bytes 6340608 | tf_op jit(solution)/shard_map/all_gather | solution.py:26
  67.6 5.3 %copy-start.5 = (f32[1024]{0:T(1024)S(1)}, f32[1024]{0:T(1024)}, u32[]{:S(2)}) copy-start(f32[1024]{0:T(1024)} %param.15) | copy-start | bytes 12292
  71.7 1.2 copy-start.2
  73.3 15.1 %copy-start.6 = (s32[48]{0:T(128)S(1)}, s32[48]{0:T(128)}, u32[]{:S(2)}) copy-start(s32[48]{0:T(128)} %param.11) | copy-start | bytes 580
  76.0 42.3 %all-to-all-start = ((bf16[3,256,1024]{2,0,1:T(4,128)(2,1)}), bf16[3,256,1024]{2,0,1:T(4,128)(2,1)S(1)}, u32[]{:S(2)}, u32[]{:S(2)}) async-start(bf16[3,256,1024]{2,0,1:T(4,128)(2,1)} %copy.61), calls=%async_computation | async-start | bytes 4194304 | tf_op jit(solution)/shard_map/all_to_all | solution.py:51
  87.6 117.5 %all-gather.5.cloned.1.call-start = ((), (), s32[]{:S(2)}) async-start(), calls=%async_computation.3 | async-start | bytes 2113536 | tf_op jit(solution)/shard_map/all_gather | solution.py:27
  158.2 5.6 %copy-start.4 = (bf16[384,1024]{0,1:T(8,128)(2,1)S(1)}, bf16[384,1024]{0,1:T(8,128)(2,1)}, u32[]{:S(2)}) copy-start(bf16[384,1024]{0,1:T(8,128)(2,1)} %copy.70) | copy-start | bytes 2359300
  178.8 8.2 %copy-start.3 = (bf16[384,1024]{0,1:T(8,128)(2,1)S(1)}, bf16[384,1024]{0,1:T(8,128)(2,1)}, u32[]{:S(2)}) copy-start(bf16[384,1024]{0,1:T(8,128)(2,1)} %copy.64) | copy-start | bytes 2359300
  244.9 9.5 %copy-start.1 = (bf16[1024,1024]{1,0:T(8,128)(2,1)S(1)}, bf16[1024,1024]{1,0:T(8,128)(2,1)}, u32[]{:S(2)}) copy-start(bf16[1024,1024]{1,0:T(8,128)(2,1)} %param.14) | copy-start | bytes 6291460
Sparse Core Ops, SparseCore 0:
  10.5 71.8 all-gather.2
  91.6 70.2 all-gather.4
where the time goes:
time: 263 us; the launch traced here: 261 us
  local copies, waits for them, and re-layouts  88 us (33%)
  matrix products  73.3 us (28%)
  waiting for transfers between devices  30.7 us (12%)
  blocking collectives  28.8 us (11%)
  other arithmetic  15.1 us (6%)
  between operations  13.6 us (5%)
  starting transfers between devices  11.8 us (4%)
    all_to_all x1, waiting for transfers between devices, local(): lax.all_to_all(temporal_in, ('dp', 'grp'), split_axis=1, concat_axis=0, t...  29.4 us
    all_to_all x1, blocking collectives, local(): lax.all_to_all(temporal_update, ('dp', 'grp'), split_axis=0, concat_axis=...  28.8 us
    sub x5, matrix products, softmax_rows(): weights = jnp.exp(scores - top)  27.6 us
    dynamic_slice x6, local copies, waits for them, and re-layouts, local(): spatial_heads = lax.map(spatial_frame, sqkv).reshape(count * tokens, width)  15.9 us
    all_to_all x1, starting transfers between devices, local(): lax.all_to_all(temporal_in, ('dp', 'grp'), split_axis=1, concat_axis=0, t...  11.6 us
    reshape x1, local copies, waits for them, and re-layouts, local(): tqkv = tqkv.astype(jnp.bfloat16).reshape(total, local_pos, 3 * width)  10.3 us
    dot_general x2, matrix products, local(): jnp.einsum('hfg,ghd->fhd', probs, values_part, preferred_element_type=jnp...  9.95 us
    slice x1, local copies, waits for them, and re-layouts, local(): block = tqkv[:, slot_index]  9.83 us
  transfers between devices with their start and end apart: 3, of which 1 were waited for; matrix products, arithmetic and copies ran while one was open for 59% of the time, Pallas kernels for 0%

commit v1 on v0

v1 whole, which is shorter than its diff:
```python
import functools

import jax
import jax.numpy as jnp
from jax import lax
from jax.experimental import pallas as pl
from jax.experimental.pallas import tpu as pltpu
from jax.sharding import PartitionSpec as P

HEADS = 16
LANES = 128
CHUNK = 256
LOG2E = 1.4426950408889634
F32 = jnp.float32
BF16 = jnp.bfloat16


def normed(wide, gain):
    scale = lax.rsqrt(jnp.mean(wide * wide, axis=-1, keepdims=True) + 1e-06)
    return wide * scale * gain


def head_pair(q2, k2, v2, scale, cap=None):
    lane = lax.broadcasted_iota(jnp.int32, q2.shape, 1)
    zero = jnp.zeros_like(q2)
    outs = []
    for side in range(2):
        mine = lane < 64 if side == 0 else lane >= 64
        q = jnp.where(mine, q2, zero)
        scores = lax.dot_general(q, k2, (((1,), (1,)), ((), ())), preferred_element_type=F32)
        if cap is not None:
            scores = jnp.minimum(scores, cap)
        top = jnp.max(scores, axis=-1, keepdims=True)
        weights = jnp.exp2((scores - top) * (scale * LOG2E))
        total = jnp.sum(weights, axis=-1, keepdims=True)
        out = jnp.dot(weights.astype(BF16), v2, preferred_element_type=F32)
        outs.append(out * (1.0 / total))
    return jnp.where(lane < 64, outs[0], outs[1]).astype(BF16)


def spatial_kernel(
    tokens,
    frames_ref,
    gain_s_ref,
    gain_t_ref,
    w_qkv_hbm,
    w_o_hbm,
    mixed_ref,
    send_ref,
    w_qkv,
    w_o,
    hidden,
    qkv,
    heads,
    stage,
    qkv_sem,
    o_sem,
):
    rows, width = frames_ref.shape
    count = rows // tokens
    parts = 3 * width // CHUNK
    scale = (width // HEADS) ** (-0.5)
    groups = width // LANES
    owners = tokens // 2
    block = count * 2 * groups

    def fetch(c):
        return pltpu.make_async_copy(
            w_qkv_hbm.at[:, pl.ds(pl.multiple_of(c * CHUNK, CHUNK), CHUNK)], w_qkv.at[c], qkv_sem.at[c]
        )

    fetch_o = pltpu.make_async_copy(w_o_hbm, w_o, o_sem)
    for c in range(parts):
        fetch(c).start()
    fetch_o.start()

    @pl.loop(0, count)
    def _(f):
        at = pl.ds(pl.multiple_of(f * tokens, tokens), tokens)
        hidden[at, :] = normed(frames_ref[at, :].astype(F32), gain_s_ref[...]).astype(BF16)

    @pl.loop(0, parts)
    def _(c):
        fetch(c).wait()
        qkv[c] = jnp.dot(hidden[...], w_qkv[c], preferred_element_type=F32).astype(BF16)

    fetch_o.wait()
    third = parts // 3
    per = CHUNK // LANES

    @pl.loop(0, count)
    def _(f):
        at = pl.ds(pl.multiple_of(f * tokens, tokens), tokens)
        for pair in range(HEADS // 2):
            c, cols = pair // per, pl.ds((pair % per) * LANES, LANES)
            heads[:, pair * LANES : (pair + 1) * LANES] = head_pair(
                qkv[c, at, cols], qkv[third + c, at, cols], qkv[2 * third + c, at, cols], scale
            )
        update = jnp.dot(heads[...], w_o[...], preferred_element_type=F32)
        mixed = (frames_ref[at, :].astype(F32) + update).astype(BF16)
        mixed_ref[at, :] = mixed
        inner = normed(mixed.astype(F32), gain_t_ref[...])
        for i in range(2):
            for j in range(groups):
                stage[pl.ds(f * 2 * groups + i * groups + j, owners, stride=block), :] = inner[
                    i * owners : (i + 1) * owners, j * LANES : (j + 1) * LANES
                ]

    send_ref[...] = stage[...].astype(BF16)


def spatial(frames, gain_s, gain_t, w_qkv, w_o):
    count, tokens, width = frames.shape
    rows = count * tokens
    parts = 3 * width // CHUNK
    vmem = pl.BlockSpec(memory_space=pltpu.VMEM)
    hbm = pl.BlockSpec(memory_space=pl.ANY)
    return pl.pallas_call(
        functools.partial(spatial_kernel, tokens),
        out_shape=(
            jax.ShapeDtypeStruct((rows, width), BF16),
            jax.ShapeDtypeStruct((rows * width // LANES, LANES), BF16),
        ),
        in_specs=[vmem, vmem, vmem, hbm, hbm],
        out_specs=(vmem, vmem),
        scratch_shapes=[
            pltpu.VMEM((parts, width, CHUNK), BF16),
            pltpu.VMEM((width, width), BF16),
            pltpu.VMEM((rows, width), BF16),
            pltpu.VMEM((parts, rows, CHUNK), BF16),
            pltpu.VMEM((tokens, width), BF16),
            pltpu.VMEM((rows * width // LANES, LANES), F32),
            pltpu.SemaphoreType.DMA((parts,)),
            pltpu.SemaphoreType.DMA,
        ],
        compiler_params=pltpu.CompilerParams(vmem_limit_bytes=44 * 2**20),
        cost_estimate=pl.CostEstimate(flops=16 * 10**9, bytes_accessed=14 * 2**20, transcendentals=0),
        name="spatial",
    )(frames.reshape(rows, width), gain_s.reshape(1, width), gain_t.reshape(1, width), w_qkv, w_o)


def temporal_kernel(
    local_pos,
    len_ref,
    recv_ref,
    w_qkv_hbm,
    w_o_hbm,
    send_ref,
    w_qkv,
    w_o,
    hidden,
    qkv,
    heads,
    stage,
    cap,
    qkv_sem,
    o_sem,
):
    total = hidden.shape[0] // local_pos
    width = hidden.shape[1]
    parts = 3 * width // CHUNK
    scale = (width // HEADS) ** (-0.5)
    groups = width // LANES
    block = local_pos * groups
    span = cap.shape[1]

    def fetch(c):
        return pltpu.make_async_copy(
            w_qkv_hbm.at[:, pl.ds(pl.multiple_of(c * CHUNK, CHUNK), CHUNK)], w_qkv.at[c], qkv_sem.at[c]
        )

    fetch_o = pltpu.make_async_copy(w_o_hbm, w_o, o_sem)
    for c in range(parts):
        fetch(c).start()
    fetch_o.start()

    position = lax.broadcasted_iota(jnp.int32, (total, LANES), 0)

    def first(e, carry):
        end, begin = carry
        end = end + len_ref[e]
        return end, jnp.where(position >= end, end, begin)

    _, begin = lax.fori_loop(0, len_ref.shape[0], first, (jnp.int32(0), jnp.zeros((total, LANES), jnp.int32)))
    lane = lax.broadcasted_iota(jnp.int32, (span, LANES), 1)
    for b in range(total // span):
        rows = slice(b * span, (b + 1) * span)
        for side in range(2):
            other = lane + (b - 1 + side) * span
            fine = (other <= position[rows]) & (other >= begin[rows])
            cap[b, :, side * span : (side + 1) * span] = jnp.where(fine, jnp.inf, -1e30)

    stage[...] = recv_ref[...].astype(F32)
    for i in range(local_pos):
        for j in range(groups):
            hidden[i * total : (i + 1) * total, j * LANES : (j + 1) * LANES] = stage[
                pl.ds(i * groups + j, total, stride=block), :
            ].astype(BF16)

    @pl.loop(0, parts)
    def _(c):
        fetch(c).wait()
        qkv[c] = jnp.dot(hidden[...], w_qkv[c], preferred_element_type=F32).astype(BF16)

    fetch_o.wait()
    third = parts // 3
    per = CHUNK // LANES

    for i in range(local_pos):
        for b in range(total // span):
            at = pl.ds(i * total + b * span, span)
            low = max(b - 1, 0)
            seen = pl.ds(i * total + low * span, (b + 1 - low) * span)
            limit = cap[b] if b else cap[b, :, span:]
            for pair in range(HEADS // 2):
                c, cols = pair // per, pl.ds((pair % per) * LANES, LANES)
                heads[b * span : (b + 1) * span, pair * LANES : (pair + 1) * LANES] = head_pair(
                    qkv[c, at, cols], qkv[third + c, seen, cols], qkv[2 * third + c, seen, cols], scale, limit
                )
        update = jnp.dot(heads[...], w_o[...], preferred_element_type=F32)
        for j in range(groups):
            stage[pl.ds(i * groups + j, total, stride=block), :] = update[:, j * LANES : (j + 1) * LANES]

    send_ref[...] = stage[...].astype(BF16)


def temporal(episode_len, recv, w_qkv, w_o, total, local_pos):
    width = w_o.shape[0]
    rows = total * local_pos
    parts = 3 * width // CHUNK
    span = LANES
    vmem = pl.BlockSpec(memory_space=pltpu.VMEM)
    hbm = pl.BlockSpec(memory_space=pl.ANY)
    return pl.pallas_call(
        functools.partial(temporal_kernel, local_pos),
        out_shape=jax.ShapeDtypeStruct(recv.shape, BF16),
        in_specs=[pl.BlockSpec(memory_space=pltpu.SMEM), vmem, hbm, hbm],
        out_specs=vmem,
        scratch_shapes=[
            pltpu.VMEM((parts, width, CHUNK), BF16),
            pltpu.VMEM((width, width), BF16),
            pltpu.VMEM((rows, width), BF16),
            pltpu.VMEM((parts, rows, CHUNK), BF16),
            pltpu.VMEM((total, width), BF16),
            pltpu.VMEM((rows * width // LANES, LANES), F32),
            pltpu.VMEM((total // span, span, 2 * span), F32),
            pltpu.SemaphoreType.DMA((parts,)),
            pltpu.SemaphoreType.DMA,
        ],
        compiler_params=pltpu.CompilerParams(vmem_limit_bytes=44 * 2**20),
        cost_estimate=pl.CostEstimate(flops=16 * 10**9, bytes_accessed=14 * 2**20, transcendentals=0),
        name="temporal",
    )(episode_len, recv, w_qkv, w_o)


def finish_kernel(tokens, mixed_ref, recv_ref, out_ref, stage):
    rows, width = mixed_ref.shape
    count = rows // tokens
    groups = width // LANES
    owners = tokens // 2
    block = count * 2 * groups
    stage[...] = recv_ref[...].astype(F32)
    for f in range(count):
        for i in range(2):
            for j in range(groups):
                at = (pl.ds(f * tokens + i * owners, owners), pl.ds(j * LANES, LANES))
                back = stage[pl.ds(f * 2 * groups + i * groups + j, owners, stride=block), :]
                out_ref[at] = (mixed_ref[at].astype(F32) + back).astype(BF16)


def finish(mixed, recv, tokens):
    vmem = pl.BlockSpec(memory_space=pltpu.VMEM)
    return pl.pallas_call(
        functools.partial(finish_kernel, tokens),
        out_shape=jax.ShapeDtypeStruct(mixed.shape, BF16),
        in_specs=[vmem, vmem],
        out_specs=vmem,
        scratch_shapes=[pltpu.VMEM(recv.shape, F32)],
        compiler_params=pltpu.CompilerParams(vmem_limit_bytes=32 * 2**20),
        name="finish",
    )(mixed, recv)


def local(frames, episode_len, norm_spatial, w_sqkv, w_so, norm_temporal, w_tqkv, w_to):
    axes = ("dp", "grp")
    count, tokens, width = frames.shape
    shards = lax.axis_size(axes)
    full_tqkv = lax.all_gather(w_tqkv, axes, axis=0, tiled=True)
    full_to = lax.all_gather(w_to, axes, axis=0, tiled=True)
    mixed, send = spatial(frames, norm_spatial, norm_temporal, w_sqkv, w_so)
    block = (shards, -1, LANES)
    recv = lax.all_to_all(send.reshape(block), axes, split_axis=0, concat_axis=0, tiled=True)
    back = temporal(
        episode_len, recv.reshape(-1, LANES), full_tqkv, full_to, count * shards, tokens // shards
    )
    returned = lax.all_to_all(back.reshape(block), axes, split_axis=0, concat_axis=0, tiled=True)
    return finish(mixed, returned.reshape(-1, LANES), tokens).reshape(frames.shape)


def solution(mesh):
    placed = (
        P(("dp", "grp"), None, None),
        P(),
        P(),
        P(),
        P(),
        P(),
        P(("dp", "grp"), None),
        P(("dp", "grp"), None),
    )
    return jax.shard_map(
        local, mesh=mesh, in_specs=placed, out_specs=P(("dp", "grp"), None, None), check_vma=False
    )
```

time: 263 us -> 222 us (0.84)
  local copies, waits for them, and re-layouts: 88 us -> 5.96 us
  matrix products: 73.3 us -> 0 us
  waiting for transfers between devices: 30.7 us -> 91.8 us
  Pallas kernels: 0 us -> 43.3 us
  blocking collectives: 28.8 us -> 67.2 us
  other arithmetic: 15.1 us -> 0 us
  starting transfers between devices: 11.8 us -> 0.04 us
    all_gather x2, waiting for transfers between devices: 0.04 us -> 90.4 us  [the longest x1 68.8 us: local(): full_tqkv = lax.all_gather(w_tqkv, axes, axis=0, tiled=True)]
    dot_general x9 -> x0, matrix products: 45.7 us -> none  [the longest x2 9.95 us: local(): jnp.einsum('hfg,ghd->fhd', probs, values_part, preferred_element_type=jnp...]
    pallas_call x0 -> x3, Pallas kernels: none -> 43.3 us  [the longest x1 24.3 us: temporal(): pl.pallas_call(functools.partial(temporal_kernel, local_pos), out_shape=j...]
    all_to_all x1 -> x2, blocking collectives: 28.8 us -> 67.2 us  [the longest x1 36.9 us: local(): lax.all_to_all(send.reshape(block), axes, split_axis=0, concat_axis=0, ti...]
    all_to_all x1 -> x0, waiting for transfers between devices: 29.4 us -> none  [local(): lax.all_to_all(temporal_in, ('dp', 'grp'), split_axis=1, concat_axis=0, t...]
    sub x5 -> x0, matrix products: 27.6 us -> none  [softmax_rows(): weights = jnp.exp(scores - top)]
    slice x12 -> x0, local copies, waits for them, and re-layouts: 27.4 us -> none  [the longest x1 9.83 us: local(): block = tqkv[:, slot_index]]
    reshape x4 -> x0, local copies, waits for them, and re-layouts: 17.8 us -> none  [the longest x1 10.3 us: local(): tqkv = tqkv.astype(jnp.bfloat16).reshape(total, local_pos, 3 * width)]
  transfers between devices with their start and end apart: 3 -> 2, of which waited for: 1 -> 2; matrix products, arithmetic and copies ran while one was open for 59% -> 0% of each run, Pallas kernels for 0% -> 7%
where the time goes in v1:
time: 222 us
  waiting for transfers between devices  91.8 us (41%)
  blocking collectives  67.2 us (30%)
  Pallas kernels  43.3 us (20%)
  between operations  13.4 us (6%)
  local copies, waits for them, and re-layouts  5.96 us (3%)
    all_gather x1, waiting for transfers between devices, local(): full_tqkv = lax.all_gather(w_tqkv, axes, axis=0, tiled=True)  68.8 us
    all_to_all x1, blocking collectives, local(): lax.all_to_all(send.reshape(block), axes, split_axis=0, concat_axis=0, ti...  36.9 us
    all_to_all x1, blocking collectives, local(): lax.all_to_all(back.reshape(block), axes, split_axis=0, concat_axis=0, ti...  30.2 us
    pallas_call x1, Pallas kernels, temporal(): pl.pallas_call(functools.partial(temporal_kernel, local_pos), out_shape=j...  24.3 us
    all_gather x1, waiting for transfers between devices, local(): full_to = lax.all_gather(w_to, axes, axis=0, tiled=True)  21.6 us
    pallas_call x1, Pallas kernels, spatial(): pl.pallas_call(functools.partial(spatial_kernel, tokens), out_shape=(jax....  16.3 us
    unnamed x12, local copies, waits for them, and re-layouts  5.96 us
  transfers between devices with their start and end apart: 2, of which 2 were waited for; matrix products, arithmetic and copies ran while one was open for 0% of the time, Pallas kernels for 7%

profile of v1, /device:TPU:1, one launch (start us, length us, event | category | flops | bytes accessed | tf_op | source)
XLA Modules:
  0.0 221.7 jit_solution(4718418090895387295)
XLA Ops:
  6.5 0.0 all-gather.5.cloned.1.call-start
  6.5 0.7 all-gather.5.cloned.1.call-update
  7.3 0.0 all-gather.3.cloned.1.call-start
  7.3 0.7 all-gather.3.cloned.1.call-update
  8.0 0.0 copy-start
  8.0 1.6 copy-done
  9.6 0.0 copy-start.2
  9.6 1.4 copy-done.2
  11.0 0.0 copy-start.3
  11.0 0.7 copy-done.3
  11.7 0.0 copy-start.4
  11.7 0.7 copy-done.4
  12.4 16.3 %spatial.1 = (bf16[768,1024]{1,0:T(8,128)(2,1)S(1)}, bf16[6144,128]{1,0:T(8,128)(2,1)S(1)}) custom-call(bf16[768,1024]{1,0:T(8,128)(2,1)S(1)} %bitcast.12, f32[1,1024]{1,0:T(1,128)S(1)} %bitcast.13, f32[1,1024]{1,0:T(1,128)S(1)} %bitcast.14, bf16[1024,3072]{1,0:T(8,128)(2,1)} %w_qkv_hbm.1, bf16[1024,1024]{1,0:T(8,128)(2,1)S(1)} %copy-done), custom_call_target="tpu_custom_call" | custom-call | flops 16000000000 | bytes 14680064 | tf_op jit(solution)/shard_map/spatial/pallas_call | solution.py:118
  28.6 0.0 copy-start.5
  28.7 36.9 %all_to_all.10 = bf16[128,48,128]{2,1,0:T(8,128)(2,1)S(1)} all-to-all(bf16[128,48,128]{2,1,0:T(8,128)(2,1)S(1)} %bitcast.11), channel_id=1, replica_groups=mesh['dp'=16,'grp'=8] {'dp','grp'}, dimensions={0} | all-to-all | bytes 3145728 | tf_op jit(solution)/shard_map/all_to_all | solution.py:292
  65.6 21.6 %all-gather.5.cloned.1.call-done.w_o_hbm = bf16[1024,1024]{1,0:T(8,128)(2,1)} async-done(((bf16[8,1024]{1,0:T(8,128)(2,1)}), bf16[1024,1024]{1,0:T(8,128)(2,1)}) %all-gather.5.cloned.1.call-update) | async-done | bytes 2097168 | tf_op jit(solution)/shard_map/all_gather | solution.py:289
  87.2 68.8 %all-gather.3.cloned.1.call-done.w_qkv_hbm = bf16[1024,3072]{1,0:T(8,128)(2,1)} async-done(((bf16[8,3072]{1,0:T(8,128)(2,1)}), bf16[1024,3072]{1,0:T(8,128)(2,1)}) %all-gather.3.cloned.1.call-update) | async-done | bytes 6291472 | tf_op jit(solution)/shard_map/all_gather | solution.py:288
  156.0 0.0 copy-done.5
  156.0 0.0 copy-start.1
  156.0 1.6 copy-done.1
  157.6 24.3 %temporal.1 = bf16[6144,128]{1,0:T(8,128)(2,1)S(1)} custom-call(s32[48]{0:T(128)S(1)} %copy-done.5, bf16[6144,128]{1,0:T(8,128)(2,1)S(1)} %bitcast.9, bf16[1024,3072]{1,0:T(8,128)(2,1)} %all-gather.3.cloned.1.call-done.w_qkv_hbm, bf16[1024,1024]{1,0:T(8,128)(2,1)S(1)} %copy-done.1), custom_call_target="tpu_custom_call" | custom-call | flops 16000000000 | bytes 14680064 | tf_op jit(solution)/shard_map/temporal/pallas_call | solution.py:234
  181.9 30.2 %all_to_all.11 = bf16[128,48,128]{2,1,0:T(8,128)(2,1)S(1)} all-to-all(bf16[128,48,128]{2,1,0:T(8,128)(2,1)S(1)} %bitcast.10), channel_id=1, replica_groups=mesh['dp'=16,'grp'=8] {'dp','grp'}, dimensions={0} | all-to-all | bytes 3145728 | tf_op jit(solution)/shard_map/all_to_all | solution.py:296
  212.1 2.8 %finish.1 = bf16[768,1024]{1,0:T(8,128)(2,1)} custom-call(bf16[768,1024]{1,0:T(8,128)(2,1)S(1)} %get-tuple-element.7.mixed_ref, bf16[6144,128]{1,0:T(8,128)(2,1)S(1)} %bitcast.8), custom_call_target="tpu_custom_call" | custom-call | tf_op jit(solution)/shard_map/finish/pallas_call | solution.py:273
Async XLA Ops:
  6.5 80.7 %all-gather.5.cloned.1.call-start = ((), (), s32[]{:S(2)}) async-start(), calls=%async_computation.3 | async-start | bytes 2113536 | tf_op jit(solution)/shard_map/all_gather | solution.py:289
  7.3 148.7 %all-gather.3.cloned.1.call-start = ((), (), s32[]{:S(2)}) async-start(), calls=%async_computation.2 | async-start | bytes 6340608 | tf_op jit(solution)/shard_map/all_gather | solution.py:288
  8.0 1.6 copy-start
  9.6 1.4 copy-start.2
  11.0 0.7 copy-start.3
  11.7 0.7 copy-start.4
  28.6 127.3 %copy-start.5 = (s32[48]{0:T(128)S(1)}, s32[48]{0:T(128)}, u32[]{:S(2)}) copy-start(s32[48]{0:T(128)} %len_ref.1) | copy-start | bytes 580
  156.0 1.6 copy-start.1
Sparse Core Ops, SparseCore 0:
  10.5 76.6 all-gather.4
  90.3 65.6 all-gather.2

commit v2 on v1

--- a/solution.py
+++ b/solution.py
@@ -40,19 +40,21 @@
 
 def spatial_kernel(
     tokens,
-    frames_ref,
+    frames_hbm,
     gain_s_ref,
     gain_t_ref,
     w_qkv_hbm,
     w_o_hbm,
     mixed_ref,
     send_ref,
+    frames_ref,
     w_qkv,
     w_o,
     hidden,
     qkv,
     heads,
     stage,
+    frame_sem,
     qkv_sem,
     o_sem,
 ):
@@ -70,6 +72,13 @@
         )
 
     fetch_o = pltpu.make_async_copy(w_o_hbm, w_o, o_sem)
+
+    def fetch_frame(f):
+        at = pl.ds(pl.multiple_of(f * tokens, tokens), tokens)
+        return pltpu.make_async_copy(frames_hbm.at[at, :], frames_ref.at[at, :], frame_sem.at[f])
+
+    for f in range(count):
+        fetch_frame(f).start()
     for c in range(parts):
         fetch(c).start()
     fetch_o.start()
@@ -77,6 +86,7 @@
     @pl.loop(0, count)
     def _(f):
         at = pl.ds(pl.multiple_of(f * tokens, tokens), tokens)
+        fetch_frame(f).wait()
         hidden[at, :] = normed(frames_ref[at, :].astype(F32), gain_s_ref[...]).astype(BF16)
 
     @pl.loop(0, parts)
@@ -121,15 +131,17 @@
             jax.ShapeDtypeStruct((rows, width), BF16),
             jax.ShapeDtypeStruct((rows * width // LANES, LANES), BF16),
         ),
-        in_specs=[vmem, vmem, vmem, hbm, hbm],
+        in_specs=[hbm, vmem, vmem, hbm, hbm],
         out_specs=(vmem, vmem),
         scratch_shapes=[
+            pltpu.VMEM((rows, width), BF16),
             pltpu.VMEM((parts, width, CHUNK), BF16),
             pltpu.VMEM((width, width), BF16),
             pltpu.VMEM((rows, width), BF16),
             pltpu.VMEM((parts, rows, CHUNK), BF16),
             pltpu.VMEM((tokens, width), BF16),
             pltpu.VMEM((rows * width // LANES, LANES), F32),
+            pltpu.SemaphoreType.DMA((count,)),
             pltpu.SemaphoreType.DMA((parts,)),
             pltpu.SemaphoreType.DMA,
         ],
@@ -143,8 +155,7 @@
     local_pos,
     len_ref,
     recv_ref,
-    w_qkv_hbm,
-    w_o_hbm,
+    w_hbm,
     send_ref,
     w_qkv,
     w_o,
@@ -166,10 +177,10 @@
 
     def fetch(c):
         return pltpu.make_async_copy(
-            w_qkv_hbm.at[:, pl.ds(pl.multiple_of(c * CHUNK, CHUNK), CHUNK)], w_qkv.at[c], qkv_sem.at[c]
+            w_hbm.at[:, pl.ds(pl.multiple_of(c * CHUNK, CHUNK), CHUNK)], w_qkv.at[c], qkv_sem.at[c]
         )
 
-    fetch_o = pltpu.make_async_copy(w_o_hbm, w_o, o_sem)
+    fetch_o = pltpu.make_async_copy(w_hbm.at[:, pl.ds(3 * width, width)], w_o, o_sem)
     for c in range(parts):
         fetch(c).start()
     fetch_o.start()
@@ -224,8 +235,8 @@
     send_ref[...] = stage[...].astype(BF16)
 
 
-def temporal(episode_len, recv, w_qkv, w_o, total, local_pos):
-    width = w_o.shape[0]
+def temporal(episode_len, recv, weights, total, local_pos):
+    width = weights.shape[0]
     rows = total * local_pos
     parts = 3 * width // CHUNK
     span = LANES
@@ -234,7 +245,7 @@
     return pl.pallas_call(
         functools.partial(temporal_kernel, local_pos),
         out_shape=jax.ShapeDtypeStruct(recv.shape, BF16),
-        in_specs=[pl.BlockSpec(memory_space=pltpu.SMEM), vmem, hbm, hbm],
+        in_specs=[pl.BlockSpec(memory_space=pltpu.SMEM), vmem, hbm],
         out_specs=vmem,
         scratch_shapes=[
             pltpu.VMEM((parts, width, CHUNK), BF16),
@@ -250,7 +261,7 @@
         compiler_params=pltpu.CompilerParams(vmem_limit_bytes=44 * 2**20),
         cost_estimate=pl.CostEstimate(flops=16 * 10**9, bytes_accessed=14 * 2**20, transcendentals=0),
         name="temporal",
-    )(episode_len, recv, w_qkv, w_o)
+    )(episode_len, recv, weights)
 
 
 def finish_kernel(tokens, mixed_ref, recv_ref, out_ref, stage):
@@ -285,13 +296,12 @@
     axes = ("dp", "grp")
     count, tokens, width = frames.shape
     shards = lax.axis_size(axes)
-    full_tqkv = lax.all_gather(w_tqkv, axes, axis=0, tiled=True)
-    full_to = lax.all_gather(w_to, axes, axis=0, tiled=True)
+    whole = lax.all_gather(jnp.concatenate([w_tqkv, w_to], axis=1), axes, axis=0, tiled=True)
     mixed, send = spatial(frames, norm_spatial, norm_temporal, w_sqkv, w_so)
     block = (shards, -1, LANES)
     recv = lax.all_to_all(send.reshape(block), axes, split_axis=0, concat_axis=0, tiled=True)
     back = temporal(
-        episode_len, recv.reshape(-1, LANES), full_tqkv, full_to, count * shards, tokens // shards
+        episode_len, recv.reshape(-1, LANES), whole, count * shards, tokens // shards
     )
     returned = lax.all_to_all(back.reshape(block), axes, split_axis=0, concat_axis=0, tiled=True)
     return finish(mixed, returned.reshape(-1, LANES), tokens).reshape(frames.shape)

time: 222 us -> 158 us (0.71)
  waiting for transfers between devices: 91.8 us -> 25.9 us
    all_gather x2 -> x1, waiting for transfers between devices: 90.4 us -> 25.9 us  [local(): lax.all_gather(jnp.concatenate([w_tqkv, w_to], axis=1), axes, axis=0, til...]
    unnamed x12 -> x10, local copies, waits for them, and re-layouts: 5.96 us -> 4.37 us
  transfers between devices with their start and end apart: 2 -> 1, of which waited for: 2 -> 1; matrix products, arithmetic and copies ran while one was open for 0% -> 0% of each run, Pallas kernels for 7% -> 10%
where the time goes in v2:
time: 158 us; the launch traced here: 157 us
  blocking collectives  68.9 us (44%)
  Pallas kernels  43.3 us (27%)
  waiting for transfers between devices  25.9 us (16%)
  between operations  13.4 us (8%)
  local copies, waits for them, and re-layouts  4.37 us (3%)
    all_to_all x1, blocking collectives, local(): lax.all_to_all(send.reshape(block), axes, split_axis=0, concat_axis=0, ti...  38.8 us
    all_to_all x1, blocking collectives, local(): lax.all_to_all(back.reshape(block), axes, split_axis=0, concat_axis=0, ti...  30.1 us
    all_gather x1, waiting for transfers between devices, local(): lax.all_gather(jnp.concatenate([w_tqkv, w_to], axis=1), axes, axis=0, til...  25.9 us
    pallas_call x1, Pallas kernels, temporal(): pl.pallas_call(functools.partial(temporal_kernel, local_pos), out_shape=j...  24.1 us
    pallas_call x1, Pallas kernels, spatial(): pl.pallas_call(functools.partial(spatial_kernel, tokens), out_shape=(jax....  16.4 us
    unnamed x10, local copies, waits for them, and re-layouts  4.37 us
  transfers between devices with their start and end apart: 1, of which 1 were waited for; matrix products, arithmetic and copies ran while one was open for 0% of the time, Pallas kernels for 10%

profile of v2, /device:TPU:1, one launch (start us, length us, event | category | flops | bytes accessed | tf_op | source)
XLA Modules:
  0.0 157.4 jit_solution(15078145735282673291)
XLA Ops:
  6.5 0.0 all-gather.2.cloned.1.call-start
  6.5 1.4 pad_maximum_fusion
  8.0 0.0 all-gather.2.cloned.1.call-update
  8.0 0.0 copy-start
  8.0 1.6 %copy-done = bf16[1024,1024]{1,0:T(8,128)(2,1)S(1)} copy-done((bf16[1024,1024]{1,0:T(8,128)(2,1)S(1)}, bf16[1024,1024]{1,0:T(8,128)(2,1)}, u32[]{:S(2)}) %copy-start) | copy-done | bytes 2097176
  9.6 0.0 copy-start.1
  9.6 1.4 copy-done.1
  11.0 0.0 copy-start.2
  11.0 0.7 copy-done.2
  11.7 0.0 copy-start.3
  11.7 0.7 copy-done.3
  12.4 16.4 %spatial.1 = (bf16[768,1024]{1,0:T(8,128)(2,1)S(1)}, bf16[6144,128]{1,0:T(8,128)(2,1)S(1)}) custom-call(bf16[768,1024]{1,0:T(8,128)(2,1)S(1)} %bitcast.12, f32[1,1024]{1,0:T(1,128)S(1)} %bitcast.13, f32[1,1024]{1,0:T(1,128)S(1)} %bitcast.14, bf16[1024,3072]{1,0:T(8,128)(2,1)} %w_qkv_hbm.1, bf16[1024,1024]{1,0:T(8,128)(2,1)S(1)} %copy-done), custom_call_target="tpu_custom_call" | custom-call | flops 16000000000 | bytes 14680064 | tf_op jit(solution)/shard_map/spatial/pallas_call | solution.py:128
  28.8 0.0 copy-start.4
  28.8 38.8 %all_to_all.10 = bf16[128,48,128]{2,1,0:T(8,128)(2,1)S(1)} all-to-all(bf16[128,48,128]{2,1,0:T(8,128)(2,1)S(1)} %bitcast.10), channel_id=1, replica_groups=mesh['dp'=16,'grp'=8] {'dp','grp'}, dimensions={0} | all-to-all | bytes 3145728 | tf_op jit(solution)/shard_map/all_to_all | solution.py:302
  67.6 25.9 %all-gather.2.cloned.1.call-done.w_hbm = bf16[1024,4096]{1,0:T(8,128)(2,1)} async-done(((bf16[8,4096]{1,0:T(8,128)(2,1)}), bf16[1024,4096]{1,0:T(8,128)(2,1)}) %all-gather.2.cloned.1.call-update) | async-done | bytes 8388624 | tf_op jit(solution)/shard_map/all_gather | solution.py:299
  93.5 0.0 copy-done.4
  93.5 24.1 %temporal.1 = bf16[6144,128]{1,0:T(8,128)(2,1)S(1)} custom-call(s32[48]{0:T(128)S(1)} %copy-done.4, bf16[6144,128]{1,0:T(8,128)(2,1)S(1)} %bitcast.9, bf16[1024,4096]{1,0:T(8,128)(2,1)} %all-gather.2.cloned.1.call-done.w_hbm), custom_call_target="tpu_custom_call" | custom-call | flops 16000000000 | bytes 14680064 | tf_op jit(solution)/shard_map/temporal/pallas_call | solution.py:245
  117.6 30.1 %all_to_all.11 = bf16[128,48,128]{2,1,0:T(8,128)(2,1)S(1)} all-to-all(bf16[128,48,128]{2,1,0:T(8,128)(2,1)S(1)} %bitcast.11), channel_id=1, replica_groups=mesh['dp'=16,'grp'=8] {'dp','grp'}, dimensions={0} | all-to-all | bytes 3145728 | tf_op jit(solution)/shard_map/all_to_all | solution.py:306
  147.8 2.8 %finish.1 = bf16[768,1024]{1,0:T(8,128)(2,1)} custom-call(bf16[768,1024]{1,0:T(8,128)(2,1)S(1)} %get-tuple-element.7.mixed_ref, bf16[6144,128]{1,0:T(8,128)(2,1)S(1)} %bitcast.8), custom_call_target="tpu_custom_call" | custom-call | tf_op jit(solution)/shard_map/finish/pallas_call | solution.py:284
Async XLA Ops:
  6.5 86.9 %all-gather.2.cloned.1.call-start = ((), (), s32[]{:S(2)}) async-start(), calls=%async_computation.2 | async-start | bytes 8454144 | tf_op jit(solution)/shard_map/all_gather | solution.py:299
  8.0 1.6 %copy-start = (bf16[1024,1024]{1,0:T(8,128)(2,1)S(1)}, bf16[1024,1024]{1,0:T(8,128)(2,1)}, u32[]{:S(2)}) copy-start(bf16[1024,1024]{1,0:T(8,128)(2,1)} %w_o_hbm.1) | copy-start | bytes 6291460
  9.6 1.4 copy-start.1
  11.0 0.7 copy-start.2
  11.7 0.7 copy-start.3
  28.8 64.7 %copy-start.4 = (s32[48]{0:T(128)S(1)}, s32[48]{0:T(128)}, u32[]{:S(2)}) copy-start(s32[48]{0:T(128)} %len_ref.1) | copy-start | bytes 580
Sparse Core Ops, SparseCore 0:
  10.3 83.0 all-gather.1

commit v3 on v2

--- a/solution.py
+++ b/solution.py
@@ -10,6 +10,7 @@
 HEADS = 16
 LANES = 128
 CHUNK = 256
+TOGETHER = 3
 LOG2E = 1.4426950408889634
 F32 = jnp.float32
 BF16 = jnp.bfloat16
@@ -41,19 +42,22 @@
 def spatial_kernel(
     tokens,
     frames_hbm,
-    gain_s_ref,
-    gain_t_ref,
+    gain_s_hbm,
+    gain_t_hbm,
     w_qkv_hbm,
     w_o_hbm,
     mixed_ref,
     send_ref,
     frames_ref,
+    gain_s_ref,
+    gain_t_ref,
     w_qkv,
     w_o,
     hidden,
     qkv,
     heads,
     stage,
+    gain_sem,
     frame_sem,
     qkv_sem,
     o_sem,
@@ -77,11 +81,19 @@
         at = pl.ds(pl.multiple_of(f * tokens, tokens), tokens)
         return pltpu.make_async_copy(frames_hbm.at[at, :], frames_ref.at[at, :], frame_sem.at[f])
 
+    gains = (
+        pltpu.make_async_copy(gain_s_hbm, gain_s_ref, gain_sem.at[0]),
+        pltpu.make_async_copy(gain_t_hbm, gain_t_ref, gain_sem.at[1]),
+    )
+    for copy in gains:
+        copy.start()
     for f in range(count):
         fetch_frame(f).start()
     for c in range(parts):
         fetch(c).start()
     fetch_o.start()
+    for copy in gains:
+        copy.wait()
 
     @pl.loop(0, count)
     def _(f):
@@ -89,10 +101,12 @@
         fetch_frame(f).wait()
         hidden[at, :] = normed(frames_ref[at, :].astype(F32), gain_s_ref[...]).astype(BF16)
 
-    @pl.loop(0, parts)
-    def _(c):
-        fetch(c).wait()
-        qkv[c] = jnp.dot(hidden[...], w_qkv[c], preferred_element_type=F32).astype(BF16)
+    @pl.loop(0, parts, step=TOGETHER)
+    def _(first):
+        for c in range(TOGETHER):
+            fetch(first + c).wait()
+        for c in range(TOGETHER):
+            qkv[first + c] = jnp.dot(hidden[...], w_qkv[first + c], preferred_element_type=F32).astype(BF16)
 
     fetch_o.wait()
     third = parts // 3
@@ -124,23 +138,26 @@
     rows = count * tokens
     parts = 3 * width // CHUNK
     vmem = pl.BlockSpec(memory_space=pltpu.VMEM)
-    hbm = pl.BlockSpec(memory_space=pl.ANY)
+    hbm = pl.BlockSpec(memory_space=pltpu.HBM)
     return pl.pallas_call(
         functools.partial(spatial_kernel, tokens),
         out_shape=(
             jax.ShapeDtypeStruct((rows, width), BF16),
             jax.ShapeDtypeStruct((rows * width // LANES, LANES), BF16),
         ),
-        in_specs=[hbm, vmem, vmem, hbm, hbm],
+        in_specs=[hbm] * 5,
         out_specs=(vmem, vmem),
         scratch_shapes=[
             pltpu.VMEM((rows, width), BF16),
+            pltpu.VMEM((1, width), F32),
+            pltpu.VMEM((1, width), F32),
             pltpu.VMEM((parts, width, CHUNK), BF16),
             pltpu.VMEM((width, width), BF16),
             pltpu.VMEM((rows, width), BF16),
             pltpu.VMEM((parts, rows, CHUNK), BF16),
             pltpu.VMEM((tokens, width), BF16),
             pltpu.VMEM((rows * width // LANES, LANES), F32),
+            pltpu.SemaphoreType.DMA((2,)),
             pltpu.SemaphoreType.DMA((count,)),
             pltpu.SemaphoreType.DMA((parts,)),
             pltpu.SemaphoreType.DMA,
@@ -173,7 +190,8 @@
     scale = (width // HEADS) ** (-0.5)
     groups = width // LANES
     block = local_pos * groups
-    span = cap.shape[1]
+    span, seen = cap.shape[1:]
+    back = total - seen
 
     def fetch(c):
         return pltpu.make_async_copy(
@@ -196,10 +214,10 @@
     lane = lax.broadcasted_iota(jnp.int32, (span, LANES), 1)
     for b in range(total // span):
         rows = slice(b * span, (b + 1) * span)
-        for side in range(2):
-            other = lane + (b - 1 + side) * span
+        for side in range(seen // LANES):
+            other = lane + b * back + side * LANES
             fine = (other <= position[rows]) & (other >= begin[rows])
-            cap[b, :, side * span : (side + 1) * span] = jnp.where(fine, jnp.inf, -1e30)
+            cap[b, :, side * LANES : (side + 1) * LANES] = jnp.where(fine, jnp.inf, -1e30)
 
     stage[...] = recv_ref[...].astype(F32)
     for i in range(local_pos):
@@ -208,26 +226,30 @@
                 pl.ds(i * groups + j, total, stride=block), :
             ].astype(BF16)
 
-    @pl.loop(0, parts)
-    def _(c):
-        fetch(c).wait()
-        qkv[c] = jnp.dot(hidden[...], w_qkv[c], preferred_element_type=F32).astype(BF16)
+    @pl.loop(0, parts, step=TOGETHER)
+    def _(first):
+        for c in range(TOGETHER):
+            fetch(first + c).wait()
+        for c in range(TOGETHER):
+            qkv[first + c] = jnp.dot(hidden[...], w_qkv[first + c], preferred_element_type=F32).astype(BF16)
 
     fetch_o.wait()
     third = parts // 3
     per = CHUNK // LANES
 
-    for i in range(local_pos):
-        for b in range(total // span):
-            at = pl.ds(i * total + b * span, span)
-            low = max(b - 1, 0)
-            seen = pl.ds(i * total + low * span, (b + 1 - low) * span)
-            limit = cap[b] if b else cap[b, :, span:]
+    @pl.loop(0, local_pos)
+    def _(i):
+        @pl.loop(0, total // span)
+        def _(b):
+            at = pl.ds(pl.multiple_of(i * total + b * span, LANES // 2), span)
+            near = pl.ds(pl.multiple_of(i * total + b * back, LANES), seen)
+            limit = cap[b]
             for pair in range(HEADS // 2):
                 c, cols = pair // per, pl.ds((pair % per) * LANES, LANES)
-                heads[b * span : (b + 1) * span, pair * LANES : (pair + 1) * LANES] = head_pair(
-                    qkv[c, at, cols], qkv[third + c, seen, cols], qkv[2 * third + c, seen, cols], scale, limit
+                heads[pl.ds(pl.multiple_of(b * span, LANES // 2), span), pl.ds(pair * LANES, LANES)] = head_pair(
+                    qkv[c, at, cols], qkv[third + c, near, cols], qkv[2 * third + c, near, cols], scale, limit
                 )
+
         update = jnp.dot(heads[...], w_o[...], preferred_element_type=F32)
         for j in range(groups):
             stage[pl.ds(i * groups + j, total, stride=block), :] = update[:, j * LANES : (j + 1) * LANES]
@@ -239,7 +261,7 @@
     width = weights.shape[0]
     rows = total * local_pos
     parts = 3 * width // CHUNK
-    span = LANES
+    span, seen = total // 2, 2 * LANES
     vmem = pl.BlockSpec(memory_space=pltpu.VMEM)
     hbm = pl.BlockSpec(memory_space=pl.ANY)
     return pl.pallas_call(
@@ -254,7 +276,7 @@
             pltpu.VMEM((parts, rows, CHUNK), BF16),
             pltpu.VMEM((total, width), BF16),
             pltpu.VMEM((rows * width // LANES, LANES), F32),
-            pltpu.VMEM((total // span, span, 2 * span), F32),
+            pltpu.VMEM((total // span, span, seen), F32),
             pltpu.SemaphoreType.DMA((parts,)),
             pltpu.SemaphoreType.DMA,
         ],

time: 158 us -> 151 us (0.956)
  Pallas kernels: 43.3 us -> 37.1 us
    pallas_call x1, Pallas kernels: 24.1 us -> 18.5 us  [temporal(): pl.pallas_call(functools.partial(temporal_kernel, local_pos), out_shape=j...]
where the time goes in v3:
time: 151 us
  blocking collectives  68.7 us (45%)
  Pallas kernels  37.1 us (25%)
  waiting for transfers between devices  26.1 us (17%)
  between operations  13.4 us (9%)
  local copies, waits for them, and re-layouts  4.37 us (3%)
    all_to_all x1, blocking collectives, local(): lax.all_to_all(send.reshape(block), axes, split_axis=0, concat_axis=0, ti...  38.6 us
    all_to_all x1, blocking collectives, local(): lax.all_to_all(back.reshape(block), axes, split_axis=0, concat_axis=0, ti...  30.1 us
    all_gather x1, waiting for transfers between devices, local(): lax.all_gather(jnp.concatenate([w_tqkv, w_to], axis=1), axes, axis=0, til...  26.1 us
    pallas_call x1, Pallas kernels, temporal(): pl.pallas_call(functools.partial(temporal_kernel, local_pos), out_shape=j...  18.5 us
    pallas_call x1, Pallas kernels, spatial(): pl.pallas_call(functools.partial(spatial_kernel, tokens), out_shape=(jax....  15.8 us
    unnamed x10, local copies, waits for them, and re-layouts  4.37 us
  transfers between devices with their start and end apart: 1, of which 1 were waited for; matrix products, arithmetic and copies ran while one was open for 0% of the time, Pallas kernels for 10%

profile of v3, /device:TPU:1, one launch (start us, length us, event | category | flops | bytes accessed | tf_op | source)
XLA Modules:
  0.0 151.1 jit_solution(2848206569048600020)
XLA Ops:
  6.5 0.0 all-gather.2.cloned.1.call-start
  6.5 1.4 pad_maximum_fusion
  8.0 0.0 all-gather.2.cloned.1.call-update
  8.0 0.0 copy-start
  8.0 1.6 %copy-done = bf16[1024,1024]{1,0:T(8,128)(2,1)S(1)} copy-done((bf16[1024,1024]{1,0:T(8,128)(2,1)S(1)}, bf16[1024,1024]{1,0:T(8,128)(2,1)}, u32[]{:S(2)}) %copy-start) | copy-done | bytes 2097176
  9.6 0.0 copy-start.1
  9.6 1.4 copy-done.1
  11.0 0.0 copy-start.2
  11.0 0.7 copy-done.2
  11.7 0.0 copy-start.3
  11.7 0.7 copy-done.3
  12.4 15.8 %spatial.1 = (bf16[768,1024]{1,0:T(8,128)(2,1)S(1)}, bf16[6144,128]{1,0:T(8,128)(2,1)S(1)}) custom-call(bf16[768,1024]{1,0:T(8,128)(2,1)S(1)} %bitcast.12, f32[1,1024]{1,0:T(1,128)S(1)} %bitcast.13, f32[1,1024]{1,0:T(1,128)S(1)} %bitcast.14, bf16[1024,3072]{1,0:T(8,128)(2,1)} %w_qkv_hbm.1, bf16[1024,1024]{1,0:T(8,128)(2,1)S(1)} %copy-done), custom_call_target="tpu_custom_call" | custom-call | flops 16000000000 | bytes 14680064 | tf_op jit(solution)/shard_map/spatial/pallas_call | solution.py:142
  28.2 0.0 copy-start.4
  28.2 38.6 %all_to_all.10 = bf16[128,48,128]{2,1,0:T(8,128)(2,1)S(1)} all-to-all(bf16[128,48,128]{2,1,0:T(8,128)(2,1)S(1)} %bitcast.10), channel_id=1, replica_groups=mesh['dp'=16,'grp'=8] {'dp','grp'}, dimensions={0} | all-to-all | bytes 3145728 | tf_op jit(solution)/shard_map/all_to_all | solution.py:324
  66.8 26.1 %all-gather.2.cloned.1.call-done.w_hbm = bf16[1024,4096]{1,0:T(8,128)(2,1)} async-done(((bf16[8,4096]{1,0:T(8,128)(2,1)}), bf16[1024,4096]{1,0:T(8,128)(2,1)}) %all-gather.2.cloned.1.call-update) | async-done | bytes 8388624 | tf_op jit(solution)/shard_map/all_gather | solution.py:321
  92.8 0.0 copy-done.4
  92.8 18.5 %temporal.1 = bf16[6144,128]{1,0:T(8,128)(2,1)S(1)} custom-call(s32[48]{0:T(128)S(1)} %copy-done.4, bf16[6144,128]{1,0:T(8,128)(2,1)S(1)} %bitcast.9, bf16[1024,4096]{1,0:T(8,128)(2,1)} %all-gather.2.cloned.1.call-done.w_hbm), custom_call_target="tpu_custom_call" | custom-call | flops 16000000000 | bytes 14680064 | tf_op jit(solution)/shard_map/temporal/pallas_call | solution.py:267
  111.3 30.1 %all_to_all.11 = bf16[128,48,128]{2,1,0:T(8,128)(2,1)S(1)} all-to-all(bf16[128,48,128]{2,1,0:T(8,128)(2,1)S(1)} %bitcast.11), channel_id=1, replica_groups=mesh['dp'=16,'grp'=8] {'dp','grp'}, dimensions={0} | all-to-all | bytes 3145728 | tf_op jit(solution)/shard_map/all_to_all | solution.py:328
  141.5 2.8 %finish.1 = bf16[768,1024]{1,0:T(8,128)(2,1)} custom-call(bf16[768,1024]{1,0:T(8,128)(2,1)S(1)} %get-tuple-element.7.mixed_ref, bf16[6144,128]{1,0:T(8,128)(2,1)S(1)} %bitcast.8), custom_call_target="tpu_custom_call" | custom-call | tf_op jit(solution)/shard_map/finish/pallas_call | solution.py:306
Async XLA Ops:
  6.5 86.3 %all-gather.2.cloned.1.call-start = ((), (), s32[]{:S(2)}) async-start(), calls=%async_computation.2 | async-start | bytes 8454144 | tf_op jit(solution)/shard_map/all_gather | solution.py:321
  8.0 1.6 %copy-start = (bf16[1024,1024]{1,0:T(8,128)(2,1)S(1)}, bf16[1024,1024]{1,0:T(8,128)(2,1)}, u32[]{:S(2)}) copy-start(bf16[1024,1024]{1,0:T(8,128)(2,1)} %w_o_hbm.1) | copy-start | bytes 6291460
  9.6 1.4 copy-start.1
  11.0 0.7 copy-start.2
  11.7 0.7 copy-start.3
  28.2 64.7 %copy-start.4 = (s32[48]{0:T(128)S(1)}, s32[48]{0:T(128)}, u32[]{:S(2)}) copy-start(s32[48]{0:T(128)} %len_ref.1) | copy-start | bytes 580
Sparse Core Ops, SparseCore 0:
  10.3 82.4 all-gather.1

commit v4 on v3

--- a/solution.py
+++ b/solution.py
@@ -56,7 +56,6 @@
     hidden,
     qkv,
     heads,
-    stage,
     gain_sem,
     frame_sem,
     qkv_sem,
@@ -68,7 +67,6 @@
     scale = (width // HEADS) ** (-0.5)
     groups = width // LANES
     owners = tokens // 2
-    block = count * 2 * groups
 
     def fetch(c):
         return pltpu.make_async_copy(
@@ -124,13 +122,9 @@
         mixed = (frames_ref[at, :].astype(F32) + update).astype(BF16)
         mixed_ref[at, :] = mixed
         inner = normed(mixed.astype(F32), gain_t_ref[...])
-        for i in range(2):
-            for j in range(groups):
-                stage[pl.ds(f * 2 * groups + i * groups + j, owners, stride=block), :] = inner[
-                    i * owners : (i + 1) * owners, j * LANES : (j + 1) * LANES
-                ]
-
-    send_ref[...] = stage[...].astype(BF16)
+        both = [inner[i * owners : (i + 1) * owners].reshape(owners, groups, LANES) for i in range(2)]
+        rows_out = pl.ds(pl.multiple_of(f * 2 * groups, 2 * groups), 2 * groups)
+        send_ref[:, rows_out, :] = jnp.concatenate(both, axis=1).astype(BF16)
 
 
 def spatial(frames, gain_s, gain_t, w_qkv, w_o):
@@ -143,7 +137,7 @@
         functools.partial(spatial_kernel, tokens),
         out_shape=(
             jax.ShapeDtypeStruct((rows, width), BF16),
-            jax.ShapeDtypeStruct((rows * width // LANES, LANES), BF16),
+            jax.ShapeDtypeStruct((tokens // 2, count * 2 * width // LANES, LANES), BF16),
         ),
         in_specs=[hbm] * 5,
         out_specs=(vmem, vmem),
@@ -156,7 +150,6 @@
             pltpu.VMEM((rows, width), BF16),
             pltpu.VMEM((parts, rows, CHUNK), BF16),
             pltpu.VMEM((tokens, width), BF16),
-            pltpu.VMEM((rows * width // LANES, LANES), F32),
             pltpu.SemaphoreType.DMA((2,)),
             pltpu.SemaphoreType.DMA((count,)),
             pltpu.SemaphoreType.DMA((parts,)),
@@ -172,18 +165,9 @@
     local_pos,
     len_ref,
     recv_ref,
-    w_hbm,
-    send_ref,
-    w_qkv,
-    w_o,
-    hidden,
-    qkv,
-    heads,
-    stage,
-    cap,
-    qkv_sem,
-    o_sem,
+    *refs,
 ):
+    parts_in, (send_ref, w_qkv, hidden, qkv, heads, cap) = refs[:-6], refs[-6:]
     total = hidden.shape[0] // local_pos
     width = hidden.shape[1]
     parts = 3 * width // CHUNK
@@ -193,16 +177,6 @@
     span, seen = cap.shape[1:]
     back = total - seen
 
-    def fetch(c):
-        return pltpu.make_async_copy(
-            w_hbm.at[:, pl.ds(pl.multiple_of(c * CHUNK, CHUNK), CHUNK)], w_qkv.at[c], qkv_sem.at[c]
-        )
-
-    fetch_o = pltpu.make_async_copy(w_hbm.at[:, pl.ds(3 * width, width)], w_o, o_sem)
-    for c in range(parts):
-        fetch(c).start()
-    fetch_o.start()
-
     position = lax.broadcasted_iota(jnp.int32, (total, LANES), 0)
 
     def first(e, carry):
@@ -219,21 +193,23 @@
             fine = (other <= position[rows]) & (other >= begin[rows])
             cap[b, :, side * LANES : (side + 1) * LANES] = jnp.where(fine, jnp.inf, -1e30)
 
-    stage[...] = recv_ref[...].astype(F32)
-    for i in range(local_pos):
-        for j in range(groups):
-            hidden[i * total : (i + 1) * total, j * LANES : (j + 1) * LANES] = stage[
-                pl.ds(i * groups + j, total, stride=block), :
-            ].astype(BF16)
+    step = 4 * groups
+    for k in range(total // step):
+        wide = recv_ref[pl.ds(k * step * block, step * block), :].astype(F32)
+        wide = wide.reshape(step, local_pos, groups, LANES)
+        for i in range(local_pos):
+            at = i * total + k * step
+            hidden[at : at + step, :] = wide[:, i].reshape(step, width).astype(BF16)
+
+    lines = w_qkv.shape[1]
+    put_rows(parts_in, (0, 1, 3, 2, 2), (0, 0, 0, 0, lines // 2), w_qkv)
 
     @pl.loop(0, parts, step=TOGETHER)
     def _(first):
         for c in range(TOGETHER):
-            fetch(first + c).wait()
-        for c in range(TOGETHER):
-            qkv[first + c] = jnp.dot(hidden[...], w_qkv[first + c], preferred_element_type=F32).astype(BF16)
-
-    fetch_o.wait()
+            weights = w_qkv[first + c].reshape(width, CHUNK)
+            qkv[first + c] = jnp.dot(hidden[...], weights, preferred_element_type=F32).astype(BF16)
+
     third = parts // 3
     per = CHUNK // LANES
 
@@ -246,87 +222,155 @@
             limit = cap[b]
             for pair in range(HEADS // 2):
                 c, cols = pair // per, pl.ds((pair % per) * LANES, LANES)
-                heads[pl.ds(pl.multiple_of(b * span, LANES // 2), span), pl.ds(pair * LANES, LANES)] = head_pair(
+                heads[at, pl.ds(pair * LANES, LANES)] = head_pair(
                     qkv[c, at, cols], qkv[third + c, near, cols], qkv[2 * third + c, near, cols], scale, limit
                 )
 
-        update = jnp.dot(heads[...], w_o[...], preferred_element_type=F32)
-        for j in range(groups):
-            stage[pl.ds(i * groups + j, total, stride=block), :] = update[:, j * LANES : (j + 1) * LANES]
-
-    send_ref[...] = stage[...].astype(BF16)
+    for k in range(total // step):
+        both = [
+            heads[i * total + k * step : i * total + (k + 1) * step, :].astype(F32).reshape(step, groups, LANES)
+            for i in range(local_pos)
+        ]
+        wide = jnp.stack(both, axis=1).reshape(step * block, LANES)
+        send_ref[pl.ds(k * step * block, step * block), :] = wide.astype(BF16)
 
 
 def temporal(episode_len, recv, weights, total, local_pos):
-    width = weights.shape[0]
-    rows = total * local_pos
+    lines, rows, cols = weights[0].shape
+    width = lines * SIDE * rows
+    tokens = total * local_pos
     parts = 3 * width // CHUNK
     span, seen = total // 2, 2 * LANES
     vmem = pl.BlockSpec(memory_space=pltpu.VMEM)
-    hbm = pl.BlockSpec(memory_space=pl.ANY)
     return pl.pallas_call(
         functools.partial(temporal_kernel, local_pos),
         out_shape=jax.ShapeDtypeStruct(recv.shape, BF16),
-        in_specs=[pl.BlockSpec(memory_space=pltpu.SMEM), vmem, hbm],
+        in_specs=[pl.BlockSpec(memory_space=pltpu.SMEM)] + [vmem] * (1 + len(weights)),
         out_specs=vmem,
         scratch_shapes=[
-            pltpu.VMEM((parts, width, CHUNK), BF16),
-            pltpu.VMEM((width, width), BF16),
-            pltpu.VMEM((rows, width), BF16),
-            pltpu.VMEM((parts, rows, CHUNK), BF16),
-            pltpu.VMEM((total, width), BF16),
-            pltpu.VMEM((rows * width // LANES, LANES), F32),
+            pltpu.VMEM((parts, lines, SIDE, rows, CHUNK), BF16),
+            pltpu.VMEM((tokens, width), BF16),
+            pltpu.VMEM((parts, tokens, CHUNK), BF16),
+            pltpu.VMEM((tokens, width), BF16),
             pltpu.VMEM((total // span, span, seen), F32),
-            pltpu.SemaphoreType.DMA((parts,)),
-            pltpu.SemaphoreType.DMA,
         ],
-        compiler_params=pltpu.CompilerParams(vmem_limit_bytes=44 * 2**20),
+        compiler_params=pltpu.CompilerParams(vmem_limit_bytes=32 * 2**20),
         cost_estimate=pl.CostEstimate(flops=16 * 10**9, bytes_accessed=14 * 2**20, transcendentals=0),
         name="temporal",
-    )(episode_len, recv, weights)
-
-
-def finish_kernel(tokens, mixed_ref, recv_ref, out_ref, stage):
+    )(episode_len, recv, *weights)
+
+
+def finish_kernel(tokens, mixed_ref, recv_ref, *refs):
+    parts_in, (out_ref, w_o, heads) = refs[:-3], refs[-3:]
     rows, width = mixed_ref.shape
     count = rows // tokens
     groups = width // LANES
     owners = tokens // 2
-    block = count * 2 * groups
-    stage[...] = recv_ref[...].astype(F32)
+    put_rows(parts_in, (0, 1, 3, 2), (0, 0, 0, 0), w_o)
     for f in range(count):
+        wide = recv_ref[:, f * 2 * groups : (f + 1) * 2 * groups, :].astype(F32)
+        wide = wide.reshape(owners, 2, groups, LANES)
         for i in range(2):
-            for j in range(groups):
-                at = (pl.ds(f * tokens + i * owners, owners), pl.ds(j * LANES, LANES))
-                back = stage[pl.ds(f * 2 * groups + i * groups + j, owners, stride=block), :]
-                out_ref[at] = (mixed_ref[at].astype(F32) + back).astype(BF16)
-
-
-def finish(mixed, recv, tokens):
+            at = f * tokens + i * owners
+            heads[at : at + owners, :] = wide[:, i].reshape(owners, width).astype(BF16)
+    for c in range(width // CHUNK):
+        cols = pl.ds(c * CHUNK, CHUNK)
+        weights = w_o[c].reshape(width, CHUNK)
+        update = jnp.dot(heads[...], weights, preferred_element_type=F32).astype(BF16)
+        out_ref[:, cols] = (mixed_ref[:, cols].astype(F32) + update.astype(F32)).astype(BF16)
+
+
+def finish(mixed, recv, weights, tokens):
+    lines, rows, cols = weights[0].shape
     vmem = pl.BlockSpec(memory_space=pltpu.VMEM)
     return pl.pallas_call(
         functools.partial(finish_kernel, tokens),
         out_shape=jax.ShapeDtypeStruct(mixed.shape, BF16),
-        in_specs=[vmem, vmem],
+        in_specs=[vmem] * (2 + len(weights)),
         out_specs=vmem,
-        scratch_shapes=[pltpu.VMEM(recv.shape, F32)],
-        compiler_params=pltpu.CompilerParams(vmem_limit_bytes=32 * 2**20),
+        scratch_shapes=[
+            pltpu.VMEM((2 * cols // CHUNK, lines, SIDE, rows, CHUNK), BF16),
+            pltpu.VMEM(mixed.shape, BF16),
+        ],
+        compiler_params=pltpu.CompilerParams(vmem_limit_bytes=24 * 2**20),
+        cost_estimate=pl.CostEstimate(flops=2 * 10**9, bytes_accessed=6 * 2**20, transcendentals=0),
         name="finish",
-    )(mixed, recv)
+    )(mixed, recv, *weights)
+
+
+AXES = ("dp", "grp")
+SIDE = 4
+
+
+def device(z, y, x, core):
+    return ((z * SIDE + y) * SIDE + x % SIDE) * 2 + core
+
+
+def swap_halves(shard):
+    span = range(SIDE)
+    pairs = [[device(z, y, x, 0), device(z, y, x, 1)] for z in span for y in span for x in span]
+    return lax.all_to_all(shard, AXES, split_axis=1, concat_axis=0, tiled=True, axis_index_groups=pairs)
+
+
+def spread(block):
+    span = range(SIDE)
+    planes = [[device(z, y, x, core) for z in span for y in span] for x in span for core in range(2)]
+    copies = jnp.broadcast_to(block[None], (len(planes[0]),) + block.shape)
+    return lax.all_to_all(copies, AXES, split_axis=0, concat_axis=0, tiled=True, axis_index_groups=planes)
+
+
+def along_x(part, step):
+    span = range(SIDE)
+    places = [(z, y, x, core) for z in span for y in span for x in span for core in range(2)]
+    pairs = [(device(z, y, x, core), device(z, y, x + step, core)) for z, y, x, core in places]
+    return lax.ppermute(part, AXES, pairs)
+
+
+def from_sibling(part):
+    count = lax.axis_size(AXES)
+    return lax.ppermute(part, AXES, [(k, k ^ 1) for k in range(count)])
+
+
+def put_rows(parts, shifts, lows, blocks):
+    x = lax.axis_index("grp") // 2
+    core = lax.rem(lax.axis_index("grp"), 2)
+    half = blocks.shape[0] // 2
+    count = len(shifts)
+    for k, part in enumerate(parts):
+        side = core if k < count else 1 - core
+        origin = lax.rem(x + SIDE - shifts[k % count], SIDE)
+        low = lows[k % count]
+        for line in range(part.shape[0]):
+            for c in range(half):
+                blocks[side * half + c, low + line, origin] = part[line, :, c * CHUNK : (c + 1) * CHUNK]
+
+
+def exchange(array, shards):
+    blocks = array.reshape(shards, -1, LANES)
+    return lax.all_to_all(blocks, AXES, split_axis=0, concat_axis=0, tiled=True)
 
 
 def local(frames, episode_len, norm_spatial, w_sqkv, w_so, norm_temporal, w_tqkv, w_to):
-    axes = ("dp", "grp")
     count, tokens, width = frames.shape
-    shards = lax.axis_size(axes)
-    whole = lax.all_gather(jnp.concatenate([w_tqkv, w_to], axis=1), axes, axis=0, tiled=True)
+    shards = lax.axis_size(AXES)
+    cut = 3 * width // 2
+    halves = [w_tqkv[:, :cut], w_to[:, : width // 2], w_tqkv[:, cut:], w_to[:, width // 2 :]]
+    plane = spread(swap_halves(jnp.concatenate(halves, axis=1)))
     mixed, send = spatial(frames, norm_spatial, norm_temporal, w_sqkv, w_so)
-    block = (shards, -1, LANES)
-    recv = lax.all_to_all(send.reshape(block), axes, split_axis=0, concat_axis=0, tiled=True)
-    back = temporal(
-        episode_len, recv.reshape(-1, LANES), whole, count * shards, tokens // shards
-    )
-    returned = lax.all_to_all(back.reshape(block), axes, split_axis=0, concat_axis=0, tiled=True)
-    return finish(mixed, returned.reshape(-1, LANES), tokens).reshape(frames.shape)
+    plane, send = lax.optimization_barrier((plane, send))
+    own, own_o = plane[:, :, :cut], plane[:, :, cut:]
+    left, right = along_x(own, 1), along_x(own, -1)
+    lines = plane.shape[0]
+    mine = [own, left, right, along_x(left[: lines // 2], 1), along_x(right[lines // 2 :], -1)]
+    theirs = [from_sibling(part) for part in mine]
+    recv = exchange(send, shards)
+    recv, own_o = lax.optimization_barrier((recv, own_o))
+    mine_o = [own_o] + [along_x(own_o, step) for step in (1, -1, 2)]
+    back = temporal(episode_len, recv.reshape(-1, LANES), mine + theirs, count * shards, tokens // shards)
+    back, mine_o = lax.optimization_barrier((back, mine_o))
+    theirs_o = [from_sibling(part) for part in mine_o]
+    returned = exchange(back, shards)
+    return finish(mixed, returned, mine_o + theirs_o, tokens).reshape(frames.shape)
 
 
 def solution(mesh):

time: 151 us -> 148 us (0.980)
  blocking collectives: 68.7 us -> 4.86 us
  starting transfers between devices: 0.01 us -> 44.6 us
  waiting for transfers between devices: 26.1 us -> 46.2 us
  between operations: 13.4 us -> 0.18 us
  local copies, waits for them, and re-layouts: 4.37 us -> 12.8 us
  Pallas kernels: 37.1 us -> 38.8 us
    all_to_all x2 -> x1, blocking collectives: 68.7 us -> 4.86 us  [swap_halves(): lax.all_to_all(shard, AXES, split_axis=1, concat_axis=0, tiled=True, axis...]
    all_gather x1 -> x0, waiting for transfers between devices: 26.1 us -> none  [local(): lax.all_gather(jnp.concatenate([w_tqkv, w_to], axis=1), axes, axis=0, til...]
    all_to_all x0 -> x3, starting transfers between devices: none -> 26 us  [the longest x2 18.1 us: exchange(): return lax.all_to_all(blocks, AXES, split_axis=0, concat_axis=0, tiled=True)]
    ppermute x0 -> x16, waiting for transfers between devices: none -> 25.4 us  [the longest x7 23.8 us: along_x(): return lax.ppermute(part, AXES, pairs)]
    all_to_all x0 -> x3, waiting for transfers between devices: none -> 20.8 us  [the longest x2 20.8 us: exchange(): return lax.all_to_all(blocks, AXES, split_axis=0, concat_axis=0, tiled=True)]
    ppermute x0 -> x16, starting transfers between devices: none -> 18.6 us  [the longest x7 11.2 us: along_x(): return lax.ppermute(part, AXES, pairs)]
    unnamed x10 -> x32, local copies, waits for them, and re-layouts: 4.37 us -> 8.14 us
    slice x0 -> x6, local copies, waits for them, and re-layouts: none -> 3.55 us  [the longest x2 1.03 us: local(): own, own_o = (plane[:, :, :cut], plane[:, :, cut:])]
  transfers between devices with their start and end apart: 1 -> 19, of which waited for: 1 -> 7; matrix products, arithmetic and copies ran while one was open for 0% -> 1% of each run, Pallas kernels for 10% -> 24%
where the time goes in v4:
time: 148 us; the launch traced here: 147 us
  waiting for transfers between devices  46.2 us (31%)
  starting transfers between devices  44.6 us (30%)
  Pallas kernels  38.8 us (26%)
  local copies, waits for them, and re-layouts  12.8 us (9%)
  blocking collectives  4.86 us (3%)
    ppermute x7, waiting for transfers between devices, along_x(): return lax.ppermute(part, AXES, pairs)  23.8 us
    all_to_all x2, waiting for transfers between devices, exchange(): return lax.all_to_all(blocks, AXES, split_axis=0, concat_axis=0, tiled=True)  20.8 us
    pallas_call x1, Pallas kernels, temporal(): pl.pallas_call(functools.partial(temporal_kernel, local_pos), out_shape=j...  18.7 us
    all_to_all x2, starting transfers between devices, exchange(): return lax.all_to_all(blocks, AXES, split_axis=0, concat_axis=0, tiled=True)  18.1 us
    pallas_call x1, Pallas kernels, spatial(): pl.pallas_call(functools.partial(spatial_kernel, tokens), out_shape=(jax....  16.8 us
    ppermute x7, starting transfers between devices, along_x(): return lax.ppermute(part, AXES, pairs)  11.2 us
    unnamed x32, local copies, waits for them, and re-layouts  8.14 us
    all_to_all x1, starting transfers between devices, spread(): lax.all_to_all(copies, AXES, split_axis=0, concat_axis=0, tiled=True, axi...  7.85 us
  transfers between devices with their start and end apart: 19, of which 7 were waited for; matrix products, arithmetic and copies ran while one was open for 1% of the time, Pallas kernels for 24%

profile of v4, /device:TPU:1, one launch (start us, length us, event | category | flops | bytes accessed | tf_op | source)
XLA Modules:
  0.0 147.5 jit_solution(13687593192761103473)
XLA Ops:
  0.0 0.7 fusion.1
  0.7 0.8 fusion
  1.5 4.9 %all_to_all.31 = bf16[8,2,2048]{2,0,1:T(8,128)(2,1)S(1)} all-to-all(bf16[8,2,2048]{2,0,1:T(8,128)(2,1)S(1)} %bitcast.15), channel_id=1, replica_groups={{0,1},{2,3},{4,5},{6,7},{8,9},{10,11},{12,13},{14,15},{16,17},{18,19},{..., dimensions={1} | all-to-all | bytes 131072 | tf_op jit(solution)/shard_map/all_to_all | solution.py:312
  6.4 1.1 broadcast_in_dim.9
  7.5 7.9 %all-to-all-start.1 = ((bf16[16,16,2048]{2,1,0:T(8,128)(2,1)}), bf16[16,16,2048]{2,1,0:T(8,128)(2,1)S(1)}, u32[]{:S(2)}, u32[]{:S(2)}) async-start(bf16[16,16,2048]{2,1,0:T(8,128)(2,1)} %broadcast_in_dim.9), calls=%async_computation.1 | async-start | bytes 2097152 | tf_op jit(solution)/shard_map/all_to_all | solution.py:319
  15.4 1.4 copy-done.1
  16.8 16.8 %spatial.1 = (bf16[768,1024]{1,0:T(8,128)(2,1)S(1)}, bf16[128,48,128]{2,1,0:T(8,128)(2,1)}) custom-call(bf16[768,1024]{1,0:T(8,128)(2,1)S(1)} %bitcast.11, f32[1,1024]{1,0:T(1,128)S(1)} %bitcast.12, f32[1,1024]{1,0:T(1,128)S(1)} %bitcast.13, bf16[1024,3072]{1,0:T(8,128)(2,1)} %w_qkv_hbm.1, bf16[1024,1024]{1,0:T(8,128)(2,1)S(1)} %copy-done), custom_call_target="tpu_custom_call" | custom-call | flops 16000000000 | bytes 14680064 | tf_op jit(solution)/shard_map/spatial/pallas_call | solution.py:136
  33.5 1.2 copy-done.13
  34.7 1.0 copy-done.15
  35.8 1.3 collective-permute-start
  37.1 1.5 collective-permute-start.1
  38.5 9.1 %all-to-all-start.2 = ((bf16[128,48,128]{2,1,0:T(8,128)(2,1)}), bf16[128,48,128]{2,1,0:T(8,128)(2,1)S(1)}, u32[]{:S(2)}, u32[]{:S(2)}) async-start(bf16[128,48,128]{2,1,0:T(8,128)(2,1)} %get-tuple-element.18), calls=%async_computation.2 | async-start | bytes 3145728 | tf_op jit(solution)/shard_map/all_to_all | solution.py:350
  47.7 1.1 collective-permute-start.4
  48.8 6.7 %collective-permute-done.refs_1_ = bf16[16,16,1536]{2,1,0:T(8,128)(2,1)S(1)} collective-permute-done((bf16[16,16,1536]{2,1,0:T(8,128)(2,1)S(1)}, bf16[16,16,1536]{2,1,0:T(8,128)(2,1)S(1)}, u32[]{:S(2)}, u32[]{:S(2)}) %collective-permute-start) | collective-permute-done | bytes 786464 | tf_op jit(solution)/shard_map/ppermute | solution.py:326
  55.7 2.8 %collective-permute-start.5 = (bf16[16,16,1536]{2,1,0:T(8,128)(2,1)S(1)}, bf16[16,16,1536]{2,1,0:T(8,128)(2,1)}, u32[]{:S(2)}, u32[]{:S(2)}) collective-permute-start(bf16[16,16,1536]{2,1,0:T(8,128)(2,1)S(1)} %collective-permute-done.refs_1_), channel_id=1, source_target_pairs={{0,1},{1,0},{2,3},{3,2},{4,5},{5,4},{6,7},{7,6},{8,9},{9,8},{10,11... | collective-permute-start | bytes 2359304 | tf_op jit(solution)/shard_map/ppermute | solution.py:331
  58.7 1.0 slice.33
  59.8 4.1 %collective-permute-start.3 = (bf16[8,16,1536]{2,1,0:T(8,128)(2,1)S(1)}, bf16[8,16,1536]{2,1,0:T(8,128)(2,1)}, u32[]{:S(2)}, u32[]{:S(2)}) collective-permute-start(bf16[8,16,1536]{2,1,0:T(8,128)(2,1)S(1)} %slice.33), channel_id=1, source_target_pairs={{0,6},{1,7},{2,0},{3,1},{4,2},{5,3},{6,4},{7,5},{8,14},{9,15},{10,... | collective-permute-start | bytes 1179656 | tf_op jit(solution)/shard_map/ppermute | solution.py:326
  63.8 17.1 %collective-permute-done.2.refs_3_ = bf16[8,16,1536]{2,1,0:T(8,128)(2,1)} collective-permute-done((bf16[8,16,1536]{2,1,0:T(8,128)(2,1)S(1)}, bf16[8,16,1536]{2,1,0:T(8,128)(2,1)}, u32[]{:S(2)}, u32[]{:S(2)}) %collective-permute-start.2) | collective-permute-done | bytes 393248 | tf_op jit(solution)/shard_map/ppermute | solution.py:326
  80.9 1.5 %collective-permute-start.7 = (bf16[8,16,1536]{2,1,0:T(8,128)(2,1)}, bf16[8,16,1536]{2,1,0:T(8,128)(2,1)}, u32[]{:S(2)}, u32[]{:S(2)}) collective-permute-start(bf16[8,16,1536]{2,1,0:T(8,128)(2,1)} %collective-permute-done.2.refs_3_), channel_id=1, source_target_pairs={{0,1},{1,0},{2,3},{3,2},{4,5},{5,4},{6,7},{7,6},{8,9},{9,8},{10,11... | collective-permute-start | bytes 1179656 | tf_op jit(solution)/shard_map/ppermute | solution.py:331
  82.4 1.0 slice.28.refs_0_
  83.4 1.3 collective-permute-start.9
  84.7 1.6 %collective-permute-start.10 = (bf16[16,16,512]{2,1,0:T(8,128)(2,1)S(1)}, bf16[16,16,512]{2,1,0:T(8,128)(2,1)S(1)}, u32[]{:S(2)}, u32[]{:S(2)}) collective-permute-start(bf16[16,16,512]{2,1,0:T(8,128)(2,1)S(1)} %slice.28.refs_0_), channel_id=1, source_target_pairs={{0,6},{1,7},{2,0},{3,1},{4,2},{5,3},{6,4},{7,5},{8,14},{9,15},{10,... | collective-permute-start | bytes 786440 | tf_op jit(solution)/shard_map/ppermute | solution.py:326
  86.2 1.4 collective-permute-start.11
  87.6 18.7 %temporal.1 = bf16[6144,128]{1,0:T(8,128)(2,1)} custom-call(s32[48]{0:T(128)S(1)} %copy-done.12, bf16[6144,128]{1,0:T(8,128)(2,1)S(1)} %bitcast.10, bf16[16,16,1536]{2,1,0:T(8,128)(2,1)S(1)} %slice.29.refs_0_, bf16[16,16,1536]{2,1,0:T(8,128)(2,1)S(1)} %collective-permute-done.refs_1_, bf16[16,16,1536]{2,1,0:T(8,128)(2,1)} %collective-permute-done.1.refs_2_, ...), custom_call_target="tpu_custom_call" | custom-call | flops 16000000000 | bytes 14680064 | tf_op jit(solution)/shard_map/temporal/pallas_call | solution.py:245
  107.1 0.7 copy-done.6
  107.9 9.0 %all-to-all-start.3 = ((bf16[128,48,128]{2,1,0:T(8,128)(2,1)}), bf16[128,48,128]{2,1,0:T(8,128)(2,1)S(1)}, u32[]{:S(2)}, u32[]{:S(2)}) async-start(bf16[128,48,128]{2,1,0:T(8,128)(2,1)} %bitcast.7), calls=%async_computation.3 | async-start | bytes 3145728 | tf_op jit(solution)/shard_map/all_to_all | solution.py:350
  116.9 1.1 collective-permute-start.12
  120.3 0.7 copy-done.8
  121.0 20.8 %all-to-all-done.3.recv_ref = bf16[128,48,128]{2,1,0:T(8,128)(2,1)S(1)} async-done(((bf16[128,48,128]{2,1,0:T(8,128)(2,1)}), bf16[128,48,128]{2,1,0:T(8,128)(2,1)S(1)}, u32[]{:S(2)}, u32[]{:S(2)}) %all-to-all-start.3) | async-done | bytes 1572896 | tf_op jit(solution)/shard_map/all_to_all | solution.py:350
  141.8 0.9 copy-done.9
  142.7 1.4 copy-done.14
  144.2 3.3 %finish.1 = bf16[768,1024]{1,0:T(8,128)(2,1)} custom-call(bf16[768,1024]{1,0:T(8,128)(2,1)S(1)} %copy-done.14, bf16[128,48,128]{2,1,0:T(8,128)(2,1)S(1)} %all-to-all-done.3.recv_ref, bf16[16,16,512]{2,1,0:T(8,128)(2,1)S(1)} %slice.28.refs_0_, bf16[16,16,512]{2,1,0:T(8,128)(2,1)S(1)} %copy-done.3, bf16[16,16,512]{2,1,0:T(8,128)(2,1)S(1)} %copy-done.5, ...), custom_call_target="tpu_custom_call" | custom-call | flops 2000000000 | bytes 6291456 | tf_op jit(solution)/shard_map/finish/pallas_call | solution.py:286
  (50 shorter events, 3.6 us)
Async XLA Ops:
  6.3 9.0 %copy-start = (bf16[1024,1024]{1,0:T(8,128)(2,1)S(1)}, bf16[1024,1024]{1,0:T(8,128)(2,1)}, u32[]{:S(2)}) copy-start(bf16[1024,1024]{1,0:T(8,128)(2,1)} %w_o_hbm.1) | copy-start | bytes 6291460
  6.4 9.0 %copy-start.10 = (f32[1024]{0:T(1024)S(1)}, f32[1024]{0:T(1024)}, u32[]{:S(2)}) copy-start(f32[1024]{0:T(1024)} %param.10) | copy-start | bytes 12292
  6.4 9.0 %copy-start.11 = (f32[1024]{0:T(1024)S(1)}, f32[1024]{0:T(1024)}, u32[]{:S(2)}) copy-start(f32[1024]{0:T(1024)} %param.13) | copy-start | bytes 12292
  7.5 27.3 %all-to-all-start.1 = ((bf16[16,16,2048]{2,1,0:T(8,128)(2,1)}), bf16[16,16,2048]{2,1,0:T(8,128)(2,1)S(1)}, u32[]{:S(2)}, u32[]{:S(2)}) async-start(bf16[16,16,2048]{2,1,0:T(8,128)(2,1)} %broadcast_in_dim.9), calls=%async_computation.1 | async-start | bytes 2097152 | tf_op jit(solution)/shard_map/all_to_all | solution.py:319
  15.3 1.4 copy-start.1
  33.5 1.2 copy-start.13
  34.7 1.0 copy-start.15
  35.8 19.7 %collective-permute-start = (bf16[16,16,1536]{2,1,0:T(8,128)(2,1)S(1)}, bf16[16,16,1536]{2,1,0:T(8,128)(2,1)S(1)}, u32[]{:S(2)}, u32[]{:S(2)}) collective-permute-start(bf16[16,16,1536]{2,1,0:T(8,128)(2,1)S(1)} %slice.29.refs_0_), channel_id=1, source_target_pairs={{0,2},{1,3},{2,4},{3,5},{4,6},{5,7},{6,0},{7,1},{8,10},{9,11},{10,... | collective-permute-start | bytes 2359304 | tf_op jit(solution)/shard_map/ppermute | solution.py:326
  37.1 21.5 %collective-permute-start.1 = (bf16[16,16,1536]{2,1,0:T(8,128)(2,1)S(1)}, bf16[16,16,1536]{2,1,0:T(8,128)(2,1)}, u32[]{:S(2)}, u32[]{:S(2)}) collective-permute-start(bf16[16,16,1536]{2,1,0:T(8,128)(2,1)S(1)} %slice.29.refs_0_), channel_id=1, source_target_pairs={{0,6},{1,7},{2,0},{3,1},{4,2},{5,3},{6,4},{7,5},{8,14},{9,15},{10,... | collective-permute-start | bytes 2359304 | tf_op jit(solution)/shard_map/ppermute | solution.py:326
  38.5 44.9 %all-to-all-start.2 = ((bf16[128,48,128]{2,1,0:T(8,128)(2,1)}), bf16[128,48,128]{2,1,0:T(8,128)(2,1)S(1)}, u32[]{:S(2)}, u32[]{:S(2)}) async-start(bf16[128,48,128]{2,1,0:T(8,128)(2,1)} %get-tuple-element.18), calls=%async_computation.2 | async-start | bytes 3145728 | tf_op jit(solution)/shard_map/all_to_all | solution.py:350
  47.7 39.9 %copy-start.12 = (s32[48]{0:T(128)S(1)}, s32[48]{0:T(128)}, u32[]{:S(2)}) copy-start(s32[48]{0:T(128)} %len_ref.1) | copy-start | bytes 580
  47.7 35.7 %collective-permute-start.4 = (bf16[16,16,1536]{2,1,0:T(8,128)(2,1)S(1)}, bf16[16,16,1536]{2,1,0:T(8,128)(2,1)}, u32[]{:S(2)}, u32[]{:S(2)}) collective-permute-start(bf16[16,16,1536]{2,1,0:T(8,128)(2,1)S(1)} %slice.29.refs_0_), channel_id=1, source_target_pairs={{0,1},{1,0},{2,3},{3,2},{4,5},{5,4},{6,7},{7,6},{8,9},{9,8},{10,11... | collective-permute-start | bytes 2359304 | tf_op jit(solution)/shard_map/ppermute | solution.py:331
  55.6 25.4 %collective-permute-start.2 = (bf16[8,16,1536]{2,1,0:T(8,128)(2,1)S(1)}, bf16[8,16,1536]{2,1,0:T(8,128)(2,1)}, u32[]{:S(2)}, u32[]{:S(2)}) collective-permute-start(bf16[8,16,1536]{2,1,0:T(8,128)(2,1)S(1)} %slice.32), channel_id=1, source_target_pairs={{0,2},{1,3},{2,4},{3,5},{4,6},{5,7},{6,0},{7,1},{8,10},{9,11},{10,... | collective-permute-start | bytes 1179656 | tf_op jit(solution)/shard_map/ppermute | solution.py:326
  55.7 29.0 %collective-permute-start.5 = (bf16[16,16,1536]{2,1,0:T(8,128)(2,1)S(1)}, bf16[16,16,1536]{2,1,0:T(8,128)(2,1)}, u32[]{:S(2)}, u32[]{:S(2)}) collective-permute-start(bf16[16,16,1536]{2,1,0:T(8,128)(2,1)S(1)} %collective-permute-done.refs_1_), channel_id=1, source_target_pairs={{0,1},{1,0},{2,3},{3,2},{4,5},{5,4},{6,7},{7,6},{8,9},{9,8},{10,11... | collective-permute-start | bytes 2359304 | tf_op jit(solution)/shard_map/ppermute | solution.py:331
  58.6 27.7 %collective-permute-start.6 = (bf16[16,16,1536]{2,1,0:T(8,128)(2,1)}, bf16[16,16,1536]{2,1,0:T(8,128)(2,1)}, u32[]{:S(2)}, u32[]{:S(2)}) collective-permute-start(bf16[16,16,1536]{2,1,0:T(8,128)(2,1)} %collective-permute-done.1.refs_2_), channel_id=1, source_target_pairs={{0,1},{1,0},{2,3},{3,2},{4,5},{5,4},{6,7},{7,6},{8,9},{9,8},{10,11... | collective-permute-start | bytes 2359304 | tf_op jit(solution)/shard_map/ppermute | solution.py:331
  59.8 22.6 %collective-permute-start.3 = (bf16[8,16,1536]{2,1,0:T(8,128)(2,1)S(1)}, bf16[8,16,1536]{2,1,0:T(8,128)(2,1)}, u32[]{:S(2)}, u32[]{:S(2)}) collective-permute-start(bf16[8,16,1536]{2,1,0:T(8,128)(2,1)S(1)} %slice.33), channel_id=1, source_target_pairs={{0,6},{1,7},{2,0},{3,1},{4,2},{5,3},{6,4},{7,5},{8,14},{9,15},{10,... | collective-permute-start | bytes 1179656 | tf_op jit(solution)/shard_map/ppermute | solution.py:326
  80.9 6.7 %collective-permute-start.7 = (bf16[8,16,1536]{2,1,0:T(8,128)(2,1)}, bf16[8,16,1536]{2,1,0:T(8,128)(2,1)}, u32[]{:S(2)}, u32[]{:S(2)}) collective-permute-start(bf16[8,16,1536]{2,1,0:T(8,128)(2,1)} %collective-permute-done.2.refs_3_), channel_id=1, source_target_pairs={{0,1},{1,0},{2,3},{3,2},{4,5},{5,4},{6,7},{7,6},{8,9},{9,8},{10,11... | collective-permute-start | bytes 1179656 | tf_op jit(solution)/shard_map/ppermute | solution.py:331
  82.4 5.2 %collective-permute-start.8 = (bf16[8,16,1536]{2,1,0:T(8,128)(2,1)}, bf16[8,16,1536]{2,1,0:T(8,128)(2,1)}, u32[]{:S(2)}, u32[]{:S(2)}) collective-permute-start(bf16[8,16,1536]{2,1,0:T(8,128)(2,1)} %collective-permute-done.3.refs_4_), channel_id=1, source_target_pairs={{0,1},{1,0},{2,3},{3,2},{4,5},{5,4},{6,7},{7,6},{8,9},{9,8},{10,11... | collective-permute-start | bytes 1179656 | tf_op jit(solution)/shard_map/ppermute | solution.py:331
  83.4 22.9 %collective-permute-start.9 = (bf16[16,16,512]{2,1,0:T(8,128)(2,1)S(1)}, bf16[16,16,512]{2,1,0:T(8,128)(2,1)S(1)}, u32[]{:S(2)}, u32[]{:S(2)}) collective-permute-start(bf16[16,16,512]{2,1,0:T(8,128)(2,1)S(1)} %slice.28.refs_0_), channel_id=1, source_target_pairs={{0,2},{1,3},{2,4},{3,5},{4,6},{5,7},{6,0},{7,1},{8,10},{9,11},{10,... | collective-permute-start | bytes 786440 | tf_op jit(solution)/shard_map/ppermute | solution.py:326
  84.7 21.7 %collective-permute-start.10 = (bf16[16,16,512]{2,1,0:T(8,128)(2,1)S(1)}, bf16[16,16,512]{2,1,0:T(8,128)(2,1)S(1)}, u32[]{:S(2)}, u32[]{:S(2)}) collective-permute-start(bf16[16,16,512]{2,1,0:T(8,128)(2,1)S(1)} %slice.28.refs_0_), channel_id=1, source_target_pairs={{0,6},{1,7},{2,0},{3,1},{4,2},{5,3},{6,4},{7,5},{8,14},{9,15},{10,... | collective-permute-start | bytes 786440 | tf_op jit(solution)/shard_map/ppermute | solution.py:326
  86.2 20.1 %collective-permute-start.11 = (bf16[16,16,512]{2,1,0:T(8,128)(2,1)S(1)}, bf16[16,16,512]{2,1,0:T(8,128)(2,1)S(1)}, u32[]{:S(2)}, u32[]{:S(2)}) collective-permute-start(bf16[16,16,512]{2,1,0:T(8,128)(2,1)S(1)} %slice.28.refs_0_), channel_id=1, source_target_pairs={{0,4},{1,5},{2,6},{3,7},{4,0},{5,1},{6,2},{7,3},{8,12},{9,13},{10,... | collective-permute-start | bytes 786440 | tf_op jit(solution)/shard_map/ppermute | solution.py:326
  106.3 0.8 copy-start.4
  107.8 10.2 %copy-start.3 = (bf16[16,16,512]{2,1,0:T(8,128)(2,1)S(1)}, bf16[16,16,512]{2,1,0:T(8,128)(2,1)}, u32[]{:S(2)}) copy-start(bf16[16,16,512]{2,1,0:T(8,128)(2,1)} %copy-done.2) | copy-start | bytes 786436
  107.9 10.3 %copy-start.5 = (bf16[16,16,512]{2,1,0:T(8,128)(2,1)S(1)}, bf16[16,16,512]{2,1,0:T(8,128)(2,1)}, u32[]{:S(2)}) copy-start(bf16[16,16,512]{2,1,0:T(8,128)(2,1)} %copy-done.4) | copy-start | bytes 786436
  107.9 10.7 %copy-start.7 = (bf16[16,16,512]{2,1,0:T(8,128)(2,1)S(1)}, bf16[16,16,512]{2,1,0:T(8,128)(2,1)}, u32[]{:S(2)}) copy-start(bf16[16,16,512]{2,1,0:T(8,128)(2,1)} %copy-done.6) | copy-start | bytes 786436
  107.9 33.9 %all-to-all-start.3 = ((bf16[128,48,128]{2,1,0:T(8,128)(2,1)}), bf16[128,48,128]{2,1,0:T(8,128)(2,1)S(1)}, u32[]{:S(2)}, u32[]{:S(2)}) async-start(bf16[128,48,128]{2,1,0:T(8,128)(2,1)} %bitcast.7), calls=%async_computation.3 | async-start | bytes 3145728 | tf_op jit(solution)/shard_map/all_to_all | solution.py:350
  116.9 2.3 %collective-permute-start.12 = (bf16[16,16,512]{2,1,0:T(8,128)(2,1)S(1)}, bf16[16,16,512]{2,1,0:T(8,128)(2,1)S(1)}, u32[]{:S(2)}, u32[]{:S(2)}) collective-permute-start(bf16[16,16,512]{2,1,0:T(8,128)(2,1)S(1)} %slice.28.refs_0_), channel_id=1, source_target_pairs={{0,1},{1,0},{2,3},{3,2},{4,5},{5,4},{6,7},{7,6},{8,9},{9,8},{10,11... | collective-permute-start | bytes 786440 | tf_op jit(solution)/shard_map/ppermute | solution.py:331
  118.0 1.5 %collective-permute-start.13 = (bf16[16,16,512]{2,1,0:T(8,128)(2,1)S(1)}, bf16[16,16,512]{2,1,0:T(8,128)(2,1)S(1)}, u32[]{:S(2)}, u32[]{:S(2)}) collective-permute-start(bf16[16,16,512]{2,1,0:T(8,128)(2,1)S(1)} %copy-done.3), channel_id=1, source_target_pairs={{0,1},{1,0},{2,3},{3,2},{4,5},{5,4},{6,7},{7,6},{8,9},{9,8},{10,11... | collective-permute-start | bytes 786440 | tf_op jit(solution)/shard_map/ppermute | solution.py:331
  118.1 1.8 %collective-permute-start.14 = (bf16[16,16,512]{2,1,0:T(8,128)(2,1)S(1)}, bf16[16,16,512]{2,1,0:T(8,128)(2,1)S(1)}, u32[]{:S(2)}, u32[]{:S(2)}) collective-permute-start(bf16[16,16,512]{2,1,0:T(8,128)(2,1)S(1)} %copy-done.5), channel_id=1, source_target_pairs={{0,1},{1,0},{2,3},{3,2},{4,5},{5,4},{6,7},{7,6},{8,9},{9,8},{10,11... | collective-permute-start | bytes 786440 | tf_op jit(solution)/shard_map/ppermute | solution.py:331
  118.5 1.8 %collective-permute-start.15 = (bf16[16,16,512]{2,1,0:T(8,128)(2,1)S(1)}, bf16[16,16,512]{2,1,0:T(8,128)(2,1)S(1)}, u32[]{:S(2)}, u32[]{:S(2)}) collective-permute-start(bf16[16,16,512]{2,1,0:T(8,128)(2,1)S(1)} %copy-done.7), channel_id=1, source_target_pairs={{0,1},{1,0},{2,3},{3,2},{4,5},{5,4},{6,7},{7,6},{8,9},{9,8},{10,11... | collective-permute-start | bytes 786440 | tf_op jit(solution)/shard_map/ppermute | solution.py:331
  141.8 1.0 copy-start.9
  142.7 1.4 copy-start.14
  (3 other events, 2.1 us)

commit v5 on v4

--- a/solution.py
+++ b/solution.py
@@ -11,6 +11,7 @@
 LANES = 128
 CHUNK = 256
 TOGETHER = 3
+VMEM = 63 * 10**6
 LOG2E = 1.4426950408889634
 F32 = jnp.float32
 BF16 = jnp.bfloat16
@@ -46,6 +47,8 @@
     gain_t_hbm,
     w_qkv_hbm,
     w_o_hbm,
+    mixed_hbm,
+    send_hbm,
     mixed_ref,
     send_ref,
     frames_ref,
@@ -60,6 +63,8 @@
     frame_sem,
     qkv_sem,
     o_sem,
+    mixed_sem,
+    send_sem,
 ):
     rows, width = frames_ref.shape
     count = rows // tokens
@@ -78,6 +83,14 @@
     def fetch_frame(f):
         at = pl.ds(pl.multiple_of(f * tokens, tokens), tokens)
         return pltpu.make_async_copy(frames_hbm.at[at, :], frames_ref.at[at, :], frame_sem.at[f])
+
+    def give_mixed(f):
+        at = pl.ds(pl.multiple_of(f * tokens, tokens), tokens)
+        return pltpu.make_async_copy(mixed_ref.at[at, :], mixed_hbm.at[at, :], mixed_sem.at[f])
+
+    def give_send(f):
+        at = pl.ds(pl.multiple_of(f * 2 * groups, 2 * groups), 2 * groups)
+        return pltpu.make_async_copy(send_ref.at[:, at, :], send_hbm.at[:, at, :], send_sem.at[f])
 
     gains = (
         pltpu.make_async_copy(gain_s_hbm, gain_s_ref, gain_sem.at[0]),
@@ -87,9 +100,6 @@
         copy.start()
     for f in range(count):
         fetch_frame(f).start()
-    for c in range(parts):
-        fetch(c).start()
-    fetch_o.start()
     for copy in gains:
         copy.wait()
 
@@ -97,7 +107,13 @@
     def _(f):
         at = pl.ds(pl.multiple_of(f * tokens, tokens), tokens)
         fetch_frame(f).wait()
+        for c in range(parts // 4):
+            fetch(f * (parts // 4) + c).start()
         hidden[at, :] = normed(frames_ref[at, :].astype(F32), gain_s_ref[...]).astype(BF16)
+
+    for c in range(count * (parts // 4), parts):
+        fetch(c).start()
+    fetch_o.start()
 
     @pl.loop(0, parts, step=TOGETHER)
     def _(first):
@@ -125,23 +141,31 @@
         both = [inner[i * owners : (i + 1) * owners].reshape(owners, groups, LANES) for i in range(2)]
         rows_out = pl.ds(pl.multiple_of(f * 2 * groups, 2 * groups), 2 * groups)
         send_ref[:, rows_out, :] = jnp.concatenate(both, axis=1).astype(BF16)
+        give_mixed(f).start()
+        give_send(f).start()
+
+    for f in range(count):
+        give_mixed(f).wait()
+        give_send(f).wait()
 
 
 def spatial(frames, gain_s, gain_t, w_qkv, w_o):
     count, tokens, width = frames.shape
     rows = count * tokens
     parts = 3 * width // CHUNK
-    vmem = pl.BlockSpec(memory_space=pltpu.VMEM)
-    hbm = pl.BlockSpec(memory_space=pltpu.HBM)
+    blocks = (tokens // 2, count * 2 * width // LANES, LANES)
+    hbm = pl.BlockSpec(memory_space=pl.ANY)
     return pl.pallas_call(
         functools.partial(spatial_kernel, tokens),
         out_shape=(
             jax.ShapeDtypeStruct((rows, width), BF16),
-            jax.ShapeDtypeStruct((tokens // 2, count * 2 * width // LANES, LANES), BF16),
+            jax.ShapeDtypeStruct(blocks, BF16),
         ),
         in_specs=[hbm] * 5,
-        out_specs=(vmem, vmem),
+        out_specs=(hbm, hbm),
         scratch_shapes=[
+            pltpu.VMEM((rows, width), BF16),
+            pltpu.VMEM(blocks, BF16),
             pltpu.VMEM((rows, width), BF16),
             pltpu.VMEM((1, width), F32),
             pltpu.VMEM((1, width), F32),
@@ -154,8 +178,10 @@
             pltpu.SemaphoreType.DMA((count,)),
             pltpu.SemaphoreType.DMA((parts,)),
             pltpu.SemaphoreType.DMA,
+            pltpu.SemaphoreType.DMA((count,)),
+            pltpu.SemaphoreType.DMA((count,)),
         ],
-        compiler_params=pltpu.CompilerParams(vmem_limit_bytes=44 * 2**20),
+        compiler_params=pltpu.CompilerParams(vmem_limit_bytes=VMEM),
         cost_estimate=pl.CostEstimate(flops=16 * 10**9, bytes_accessed=14 * 2**20, transcendentals=0),
         name="spatial",
     )(frames.reshape(rows, width), gain_s.reshape(1, width), gain_t.reshape(1, width), w_qkv, w_o)
@@ -164,10 +190,20 @@
 def temporal_kernel(
     local_pos,
     len_ref,
-    recv_ref,
+    recv_hbm,
     *refs,
 ):
-    parts_in, (send_ref, w_qkv, hidden, qkv, heads, cap) = refs[:-6], refs[-6:]
+    parts_hbm, (send_hbm, *scratch) = refs[:-13], refs[-13:]
+    recv_ref, send_ref, whole, low, w_qkv, hidden, qkv, heads, cap, recv_sem, part_sem, send_sem = scratch
+    count = len(parts_hbm) // 2
+    parts_in = []
+    for side in range(2):
+        parts_in += [whole.at[3 * side + k] for k in range(3)] + [low.at[2 * side + k] for k in range(count - 3)]
+    fetch_recv = pltpu.make_async_copy(recv_hbm, recv_ref, recv_sem)
+    fetch_recv.start()
+    fetches = [
+        pltpu.make_async_copy(source, part, part_sem.at[k]) for k, (source, part) in enumerate(zip(parts_hbm, parts_in))
+    ]
     total = hidden.shape[0] // local_pos
     width = hidden.shape[1]
     parts = 3 * width // CHUNK
@@ -177,14 +213,14 @@
     span, seen = cap.shape[1:]
     back = total - seen
 
+    number = lax.broadcasted_iota(jnp.int32, (1, LANES), 1)
+
+    def add(e, ends):
+        return ends + jnp.where(number >= e, len_ref[e], 0)
+
+    ends = lax.fori_loop(0, len_ref.shape[0], add, jnp.zeros((1, LANES), jnp.int32))
     position = lax.broadcasted_iota(jnp.int32, (total, LANES), 0)
-
-    def first(e, carry):
-        end, begin = carry
-        end = end + len_ref[e]
-        return end, jnp.where(position >= end, end, begin)
-
-    _, begin = lax.fori_loop(0, len_ref.shape[0], first, (jnp.int32(0), jnp.zeros((total, LANES), jnp.int32)))
+    begin = jnp.max(jnp.where(ends <= position, ends, 0), axis=1, keepdims=True)
     lane = lax.broadcasted_iota(jnp.int32, (span, LANES), 1)
     for b in range(total // span):
         rows = slice(b * span, (b + 1) * span)
@@ -194,6 +230,9 @@
             cap[b, :, side * LANES : (side + 1) * LANES] = jnp.where(fine, jnp.inf, -1e30)
 
     step = 4 * groups
+    fetch_recv.wait()
+    for fetch in fetches[:count]:
+        fetch.start()
     for k in range(total // step):
         wide = recv_ref[pl.ds(k * step * block, step * block), :].astype(F32)
         wide = wide.reshape(step, local_pos, groups, LANES)
@@ -201,14 +240,23 @@
             at = i * total + k * step
             hidden[at : at + step, :] = wide[:, i].reshape(step, width).astype(BF16)
 
-    lines = w_qkv.shape[1]
-    put_rows(parts_in, (0, 1, 3, 2, 2), (0, 0, 0, 0, lines // 2), w_qkv)
-
-    @pl.loop(0, parts, step=TOGETHER)
-    def _(first):
-        for c in range(TOGETHER):
-            weights = w_qkv[first + c].reshape(width, CHUNK)
-            qkv[first + c] = jnp.dot(hidden[...], weights, preferred_element_type=F32).astype(BF16)
+    core = lax.rem(lax.axis_index("grp"), 2)
+    half = parts // 2
+    lines = whole.shape[1]
+    for turn in range(2):
+        side = core if turn == 0 else 1 - core
+        for fetch in fetches[turn * count : (turn + 1) * count]:
+            fetch.wait()
+        if turn == 0:
+            for fetch in fetches[count:]:
+                fetch.start()
+        put_rows(parts_in[turn * count : (turn + 1) * count], side, (0, 1, 3, 2, 2), (0, 0, 0, 0, lines // 2), w_qkv)
+
+        @pl.loop(0, half, step=TOGETHER)
+        def _(first, side=side):
+            for k in range(TOGETHER):
+                c = side * half + first + k
+                qkv[c] = jnp.dot(hidden[...], w_qkv[c], preferred_element_type=F32).astype(BF16)
 
     third = parts // 3
     per = CHUNK // LANES
@@ -226,13 +274,19 @@
                     qkv[c, at, cols], qkv[third + c, near, cols], qkv[2 * third + c, near, cols], scale, limit
                 )
 
+    gives = []
     for k in range(total // step):
         both = [
             heads[i * total + k * step : i * total + (k + 1) * step, :].astype(F32).reshape(step, groups, LANES)
             for i in range(local_pos)
         ]
         wide = jnp.stack(both, axis=1).reshape(step * block, LANES)
-        send_ref[pl.ds(k * step * block, step * block), :] = wide.astype(BF16)
+        at = pl.ds(k * step * block, step * block)
+        send_ref[at, :] = wide.astype(BF16)
+        gives.append(pltpu.make_async_copy(send_ref.at[at, :], send_hbm.at[at, :], send_sem.at[k]))
+        gives[k].start()
+    for give in gives:
+        give.wait()
 
 
 def temporal(episode_len, recv, weights, total, local_pos):
@@ -241,58 +295,108 @@
     tokens = total * local_pos
     parts = 3 * width // CHUNK
     span, seen = total // 2, 2 * LANES
-    vmem = pl.BlockSpec(memory_space=pltpu.VMEM)
+    hbm = pl.BlockSpec(memory_space=pl.ANY)
     return pl.pallas_call(
         functools.partial(temporal_kernel, local_pos),
         out_shape=jax.ShapeDtypeStruct(recv.shape, BF16),
-        in_specs=[pl.BlockSpec(memory_space=pltpu.SMEM)] + [vmem] * (1 + len(weights)),
-        out_specs=vmem,
+        in_specs=[pl.BlockSpec(memory_space=pltpu.SMEM)] + [hbm] * (1 + len(weights)),
+        out_specs=hbm,
         scratch_shapes=[
-            pltpu.VMEM((parts, lines, SIDE, rows, CHUNK), BF16),
+            pltpu.VMEM(recv.shape, BF16),
+            pltpu.VMEM(recv.shape, BF16),
+            pltpu.VMEM((6, lines, rows, cols), BF16),
+            pltpu.VMEM((4, lines // 2, rows, cols), BF16),
+            pltpu.VMEM((parts, width, CHUNK), BF16),
             pltpu.VMEM((tokens, width), BF16),
             pltpu.VMEM((parts, tokens, CHUNK), BF16),
             pltpu.VMEM((tokens, width), BF16),
             pltpu.VMEM((total // span, span, seen), F32),
+            pltpu.SemaphoreType.DMA,
+            pltpu.SemaphoreType.DMA((len(weights),)),
+            pltpu.SemaphoreType.DMA((total // 32,)),
         ],
-        compiler_params=pltpu.CompilerParams(vmem_limit_bytes=32 * 2**20),
+        compiler_params=pltpu.CompilerParams(vmem_limit_bytes=VMEM),
         cost_estimate=pl.CostEstimate(flops=16 * 10**9, bytes_accessed=14 * 2**20, transcendentals=0),
         name="temporal",
     )(episode_len, recv, *weights)
 
 
-def finish_kernel(tokens, mixed_ref, recv_ref, *refs):
-    parts_in, (out_ref, w_o, heads) = refs[:-3], refs[-3:]
+def finish_kernel(tokens, mixed_hbm, recv_hbm, *refs):
+    parts_hbm, (out_hbm, *scratch) = refs[:-11], refs[-11:]
+    mixed_ref, recv_ref, out_ref, parts_in, w_o, heads, mixed_sem, recv_sem, part_sem, out_sem = scratch
     rows, width = mixed_ref.shape
     count = rows // tokens
     groups = width // LANES
     owners = tokens // 2
-    put_rows(parts_in, (0, 1, 3, 2), (0, 0, 0, 0), w_o)
+
+    def slab(f):
+        return pl.ds(f * 2 * groups, 2 * groups)
+
+    def frame(f):
+        return pl.ds(f * tokens, tokens)
+
+    got = [
+        pltpu.make_async_copy(recv_hbm.at[:, slab(f), :], recv_ref.at[:, slab(f), :], recv_sem.at[f])
+        for f in range(count)
+    ]
+    had = [
+        pltpu.make_async_copy(mixed_hbm.at[frame(f), :], mixed_ref.at[frame(f), :], mixed_sem.at[f])
+        for f in range(count)
+    ]
+    fetches = [
+        pltpu.make_async_copy(source, parts_in.at[k], part_sem.at[k]) for k, source in enumerate(parts_hbm)
+    ]
+    gives = [
+        pltpu.make_async_copy(out_ref.at[frame(f), :], out_hbm.at[frame(f), :], out_sem.at[f]) for f in range(count)
+    ]
+    for copy in got[:1] + fetches + had[:1] + got[1:] + had[1:]:
+        copy.start()
     for f in range(count):
-        wide = recv_ref[:, f * 2 * groups : (f + 1) * 2 * groups, :].astype(F32)
+        got[f].wait()
+        wide = recv_ref[:, slab(f), :].astype(F32)
         wide = wide.reshape(owners, 2, groups, LANES)
         for i in range(2):
-            at = f * tokens + i * owners
-            heads[at : at + owners, :] = wide[:, i].reshape(owners, width).astype(BF16)
-    for c in range(width // CHUNK):
-        cols = pl.ds(c * CHUNK, CHUNK)
-        weights = w_o[c].reshape(width, CHUNK)
-        update = jnp.dot(heads[...], weights, preferred_element_type=F32).astype(BF16)
-        out_ref[:, cols] = (mixed_ref[:, cols].astype(F32) + update.astype(F32)).astype(BF16)
+            heads[i * owners : (i + 1) * owners, :] = wide[:, i].reshape(owners, width).astype(BF16)
+        if f == 0:
+            for copy in fetches:
+                copy.wait()
+            core = lax.rem(lax.axis_index("grp"), 2)
+            for turn in range(2):
+                mine = [parts_in.at[turn * SIDE + k] for k in range(SIDE)]
+                put_rows(mine, core if turn == 0 else 1 - core, (0, 1, 3, 2), (0, 0, 0, 0), w_o)
+        had[f].wait()
+        for c in range(width // CHUNK):
+            cols = pl.ds(c * CHUNK, CHUNK)
+            update = jnp.dot(heads[...], w_o[c], preferred_element_type=F32).astype(BF16)
+            out_ref[frame(f), cols] = (mixed_ref[frame(f), cols].astype(F32) + update.astype(F32)).astype(BF16)
+        gives[f].start()
+    for give in gives:
+        give.wait()
 
 
 def finish(mixed, recv, weights, tokens):
     lines, rows, cols = weights[0].shape
-    vmem = pl.BlockSpec(memory_space=pltpu.VMEM)
+    width = mixed.shape[1]
+    count = mixed.shape[0] // tokens
+    hbm = pl.BlockSpec(memory_space=pl.ANY)
     return pl.pallas_call(
         functools.partial(finish_kernel, tokens),
         out_shape=jax.ShapeDtypeStruct(mixed.shape, BF16),
-        in_specs=[vmem] * (2 + len(weights)),
-        out_specs=vmem,
+        in_specs=[hbm] * (2 + len(weights)),
+        out_specs=hbm,
         scratch_shapes=[
-            pltpu.VMEM((2 * cols // CHUNK, lines, SIDE, rows, CHUNK), BF16),
             pltpu.VMEM(mixed.shape, BF16),
+            pltpu.VMEM(recv.shape, BF16),
+            pltpu.VMEM(mixed.shape, BF16),
+            pltpu.VMEM((len(weights), lines, rows, cols), BF16),
+            pltpu.VMEM((2 * cols // CHUNK, width, CHUNK), BF16),
+            pltpu.VMEM((tokens, width), BF16),
+            pltpu.SemaphoreType.DMA((count,)),
+            pltpu.SemaphoreType.DMA((count,)),
+            pltpu.SemaphoreType.DMA((len(weights),)),
+            pltpu.SemaphoreType.DMA((count,)),
         ],
-        compiler_params=pltpu.CompilerParams(vmem_limit_bytes=24 * 2**20),
+        compiler_params=pltpu.CompilerParams(vmem_limit_bytes=VMEM),
         cost_estimate=pl.CostEstimate(flops=2 * 10**9, bytes_accessed=6 * 2**20, transcendentals=0),
         name="finish",
     )(mixed, recv, *weights)
@@ -331,18 +435,16 @@
     return lax.ppermute(part, AXES, [(k, k ^ 1) for k in range(count)])
 
 
-def put_rows(parts, shifts, lows, blocks):
+def put_rows(parts, side, shifts, lows, blocks):
     x = lax.axis_index("grp") // 2
-    core = lax.rem(lax.axis_index("grp"), 2)
     half = blocks.shape[0] // 2
-    count = len(shifts)
-    for k, part in enumerate(parts):
-        side = core if k < count else 1 - core
-        origin = lax.rem(x + SIDE - shifts[k % count], SIDE)
-        low = lows[k % count]
-        for line in range(part.shape[0]):
+    for part, shift, low in zip(parts, shifts, lows):
+        origin = lax.rem(x + SIDE - shift, SIDE)
+        lines, rows, _ = part.shape
+        for line in range(lines):
+            at = pl.ds(pl.multiple_of(((low + line) * SIDE + origin) * rows, rows), rows)
             for c in range(half):
-                blocks[side * half + c, low + line, origin] = part[line, :, c * CHUNK : (c + 1) * CHUNK]
+                blocks[side * half + c, at, :] = part[line, :, c * CHUNK : (c + 1) * CHUNK]
 
 
 def exchange(array, shards):
@@ -361,7 +463,8 @@
     own, own_o = plane[:, :, :cut], plane[:, :, cut:]
     left, right = along_x(own, 1), along_x(own, -1)
     lines = plane.shape[0]
-    mine = [own, left, right, along_x(left[: lines // 2], 1), along_x(right[lines // 2 :], -1)]
+    low, high, left, right = lax.optimization_barrier((left[: lines // 2], right[lines // 2 :], left, right))
+    mine = [own, left, right, along_x(low, 1), along_x(high, -1)]
     theirs = [from_sibling(part) for part in mine]
     recv = exchange(send, shards)
     recv, own_o = lax.optimization_barrier((recv, own_o))

time: 148 us -> 144 us (0.973)
  local copies, waits for them, and re-layouts: 12.8 us -> 6.61 us
  Pallas kernels: 38.8 us -> 40.8 us
    unnamed x32 -> x20, local copies, waits for them, and re-layouts: 8.14 us -> 1.18 us
    pallas_call x1, Pallas kernels: 3.34 us -> 5.84 us  [finish(): pl.pallas_call(functools.partial(finish_kernel, tokens), out_shape=jax.Sh...]
    ppermute x9, starting transfers between devices: 7.42 us -> 9.86 us  [from_sibling(): return lax.ppermute(part, AXES, [(k, k ^ 1) for k in range(count)])]
    ppermute x7, starting transfers between devices: 11.2 us -> 9.17 us  [along_x(): return lax.ppermute(part, AXES, pairs)]
  transfers between devices with their start and end apart: 19 -> 19, of which waited for: 7 -> 7; matrix products, arithmetic and copies ran while one was open for 1% -> 2% of each run, Pallas kernels for 24% -> 24%
where the time goes in v5:
time: 144 us; the launch traced here: 143 us
  waiting for transfers between devices  45.5 us (32%)
  starting transfers between devices  45 us (31%)
  Pallas kernels  40.8 us (28%)
  local copies, waits for them, and re-layouts  6.61 us (5%)
  blocking collectives  4.86 us (3%)
    ppermute x7, waiting for transfers between devices, along_x(): return lax.ppermute(part, AXES, pairs)  22.3 us
    all_to_all x2, waiting for transfers between devices, exchange(): return lax.all_to_all(blocks, AXES, split_axis=0, concat_axis=0, tiled=True)  21.3 us
    all_to_all x2, starting transfers between devices, exchange(): return lax.all_to_all(blocks, AXES, split_axis=0, concat_axis=0, tiled=True)  18.1 us
    pallas_call x1, Pallas kernels, spatial(): pl.pallas_call(functools.partial(spatial_kernel, tokens), out_shape=(jax....  17.5 us
    pallas_call x1, Pallas kernels, temporal(): pl.pallas_call(functools.partial(temporal_kernel, local_pos), out_shape=j...  17.5 us
    ppermute x9, starting transfers between devices, from_sibling(): return lax.ppermute(part, AXES, [(k, k ^ 1) for k in range(count)])  9.86 us
    ppermute x7, starting transfers between devices, along_x(): return lax.ppermute(part, AXES, pairs)  9.17 us
    all_to_all x1, starting transfers between devices, spread(): lax.all_to_all(copies, AXES, split_axis=0, concat_axis=0, tiled=True, axi...  7.85 us
  transfers between devices with their start and end apart: 19, of which 7 were waited for; matrix products, arithmetic and copies ran while one was open for 2% of the time, Pallas kernels for 24%

profile of v5, /device:TPU:1, one launch (start us, length us, event | category | flops | bytes accessed | tf_op | source)
XLA Modules:
  0.0 143.1 jit_solution(15681074824020592170)
XLA Ops:
  0.0 0.7 fusion.1
  0.7 0.8 fusion
  1.5 4.9 %all_to_all.31 = bf16[8,2,2048]{2,0,1:T(8,128)(2,1)S(1)} all-to-all(bf16[8,2,2048]{2,0,1:T(8,128)(2,1)S(1)} %bitcast.13), channel_id=1, replica_groups={{0,1},{2,3},{4,5},{6,7},{8,9},{10,11},{12,13},{14,15},{16,17},{18,19},{..., dimensions={1} | all-to-all | bytes 131072 | tf_op jit(solution)/shard_map/all_to_all | solution.py:416
  6.3 1.1 broadcast_in_dim.9
  7.5 7.9 %all-to-all-start.1 = ((bf16[16,16,2048]{2,1,0:T(8,128)(2,1)}), bf16[16,16,2048]{2,1,0:T(8,128)(2,1)S(1)}, u32[]{:S(2)}, u32[]{:S(2)}) async-start(bf16[16,16,2048]{2,1,0:T(8,128)(2,1)} %broadcast_in_dim.9), calls=%async_computation.1 | async-start | bytes 2097152 | tf_op jit(solution)/shard_map/all_to_all | solution.py:423
  15.3 17.5 %spatial.1 = (bf16[768,1024]{1,0:T(8,128)(2,1)}, bf16[128,48,128]{2,1,0:T(8,128)(2,1)}) custom-call(bf16[768,1024]{1,0:T(8,128)(2,1)} %bitcast.14, f32[1,1024]{1,0:T(1,128)} %bitcast.15, f32[1,1024]{1,0:T(1,128)} %bitcast.16, bf16[1024,3072]{1,0:T(8,128)(2,1)} %w_qkv_hbm.1, bf16[1024,1024]{1,0:T(8,128)(2,1)} %w_o_hbm.1), custom_call_target="tpu_custom_call" | custom-call | flops 16000000000 | bytes 14680064 | tf_op jit(solution)/shard_map/spatial/pallas_call | solution.py:158
  32.9 1.3 collective-permute-start
  34.2 1.5 %collective-permute-start.1 = (bf16[16,16,1536]{2,1,0:T(8,128)(2,1)S(1)}, bf16[16,16,1536]{2,1,0:T(8,128)(2,1)}, u32[]{:S(2)}, u32[]{:S(2)}) collective-permute-start(bf16[16,16,1536]{2,1,0:T(8,128)(2,1)S(1)} %slice.29.refs_0_), channel_id=1, source_target_pairs={{0,6},{1,7},{2,0},{3,1},{4,2},{5,3},{6,4},{7,5},{8,14},{9,15},{10,... | collective-permute-start | bytes 2359304 | tf_op jit(solution)/shard_map/ppermute | solution.py:430
  35.7 9.1 %all-to-all-start.2 = ((bf16[128,48,128]{2,1,0:T(8,128)(2,1)}), bf16[128,48,128]{2,1,0:T(8,128)(2,1)S(1)}, u32[]{:S(2)}, u32[]{:S(2)}) async-start(bf16[128,48,128]{2,1,0:T(8,128)(2,1)} %get-tuple-element.22), calls=%async_computation.2 | async-start | bytes 3145728 | tf_op jit(solution)/shard_map/all_to_all | solution.py:452
  44.8 1.1 collective-permute-start.4
  45.9 6.4 %collective-permute-done.refs_1_ = bf16[16,16,1536]{2,1,0:T(8,128)(2,1)} collective-permute-done((bf16[16,16,1536]{2,1,0:T(8,128)(2,1)S(1)}, bf16[16,16,1536]{2,1,0:T(8,128)(2,1)}, u32[]{:S(2)}, u32[]{:S(2)}) %collective-permute-start) | collective-permute-done | bytes 786464 | tf_op jit(solution)/shard_map/ppermute | solution.py:430
  52.4 1.0 slice.32
  53.4 1.0 slice.33
  54.5 5.1 %collective-permute-start.5 = (bf16[16,16,1536]{2,1,0:T(8,128)(2,1)}, bf16[16,16,1536]{2,1,0:T(8,128)(2,1)}, u32[]{:S(2)}, u32[]{:S(2)}) collective-permute-start(bf16[16,16,1536]{2,1,0:T(8,128)(2,1)} %collective-permute-done.refs_1_), channel_id=1, source_target_pairs={{0,1},{1,0},{2,3},{3,2},{4,5},{5,4},{6,7},{7,6},{8,9},{9,8},{10,11... | collective-permute-start | bytes 2359304 | tf_op jit(solution)/shard_map/ppermute | solution.py:435
  59.6 2.2 %collective-permute-start.3 = (bf16[8,16,1536]{2,1,0:T(8,128)(2,1)S(1)}, bf16[8,16,1536]{2,1,0:T(8,128)(2,1)}, u32[]{:S(2)}, u32[]{:S(2)}) collective-permute-start(bf16[8,16,1536]{2,1,0:T(8,128)(2,1)S(1)} %slice.33), channel_id=1, source_target_pairs={{0,6},{1,7},{2,0},{3,1},{4,2},{5,3},{6,4},{7,5},{8,14},{9,15},{10,... | collective-permute-start | bytes 1179656 | tf_op jit(solution)/shard_map/ppermute | solution.py:430
  61.8 15.9 %collective-permute-done.2.refs_3_ = bf16[8,16,1536]{2,1,0:T(8,128)(2,1)} collective-permute-done((bf16[8,16,1536]{2,1,0:T(8,128)(2,1)S(1)}, bf16[8,16,1536]{2,1,0:T(8,128)(2,1)}, u32[]{:S(2)}, u32[]{:S(2)}) %collective-permute-start.2) | collective-permute-done | bytes 393248 | tf_op jit(solution)/shard_map/ppermute | solution.py:430
  77.7 1.9 %collective-permute-start.7 = (bf16[8,16,1536]{2,1,0:T(8,128)(2,1)}, bf16[8,16,1536]{2,1,0:T(8,128)(2,1)}, u32[]{:S(2)}, u32[]{:S(2)}) collective-permute-start(bf16[8,16,1536]{2,1,0:T(8,128)(2,1)} %collective-permute-done.2.refs_3_), channel_id=1, source_target_pairs={{0,1},{1,0},{2,3},{3,2},{4,5},{5,4},{6,7},{7,6},{8,9},{9,8},{10,11... | collective-permute-start | bytes 1179656 | tf_op jit(solution)/shard_map/ppermute | solution.py:435
  79.5 0.7 slice.28.refs_0_
  80.3 1.3 collective-permute-start.9
  81.6 1.6 %collective-permute-start.10 = (bf16[16,16,512]{2,1,0:T(8,128)(2,1)}, bf16[16,16,512]{2,1,0:T(8,128)(2,1)S(1)}, u32[]{:S(2)}, u32[]{:S(2)}) collective-permute-start(bf16[16,16,512]{2,1,0:T(8,128)(2,1)} %slice.28.refs_0_), channel_id=1, source_target_pairs={{0,6},{1,7},{2,0},{3,1},{4,2},{5,3},{6,4},{7,5},{8,14},{9,15},{10,... | collective-permute-start | bytes 786440 | tf_op jit(solution)/shard_map/ppermute | solution.py:430
  83.1 1.4 collective-permute-start.11
  84.5 17.5 %temporal.1 = bf16[6144,128]{1,0:T(8,128)(2,1)} custom-call(s32[48]{0:T(128)} %len_ref.1, bf16[6144,128]{1,0:T(8,128)(2,1)} %bitcast.10, bf16[16,16,1536]{2,1,0:T(8,128)(2,1)} %copy-done.2, bf16[16,16,1536]{2,1,0:T(8,128)(2,1)} %collective-permute-done.refs_1_, bf16[16,16,1536]{2,1,0:T(8,128)(2,1)} %collective-permute-done.1.refs_2_, ...), custom_call_target="tpu_custom_call" | custom-call | flops 16000000000 | bytes 14680064 | tf_op jit(solution)/shard_map/temporal/pallas_call | solution.py:299
  102.0 9.0 %all-to-all-start.3 = ((bf16[128,48,128]{2,1,0:T(8,128)(2,1)}), bf16[128,48,128]{2,1,0:T(8,128)(2,1)S(1)}, u32[]{:S(2)}, u32[]{:S(2)}) async-start(bf16[128,48,128]{2,1,0:T(8,128)(2,1)} %bitcast.11), calls=%async_computation.3 | async-start | bytes 3145728 | tf_op jit(solution)/shard_map/all_to_all | solution.py:452
  111.0 1.1 collective-permute-start.12
  112.3 0.4 collective-permute-start.14
  112.8 0.5 collective-permute-done.12.refs_4_
  113.4 0.4 collective-permute-done.13.refs_5_
  113.7 0.7 collective-permute-done.14.refs_6_
  114.5 0.1 collective-permute-done.15.refs_7_
  114.6 21.3 %all-to-all-done.3.recv_hbm = bf16[128,48,128]{2,1,0:T(8,128)(2,1)S(1)} async-done(((bf16[128,48,128]{2,1,0:T(8,128)(2,1)}), bf16[128,48,128]{2,1,0:T(8,128)(2,1)S(1)}, u32[]{:S(2)}, u32[]{:S(2)}) %all-to-all-start.3) | async-done | bytes 1572896 | tf_op jit(solution)/shard_map/all_to_all | solution.py:452
  136.0 1.1 copy-done.1
  137.1 5.8 %finish.1 = bf16[768,1024]{1,0:T(8,128)(2,1)} custom-call(bf16[768,1024]{1,0:T(8,128)(2,1)} %get-tuple-element.20.mixed_hbm, bf16[128,48,128]{2,1,0:T(8,128)(2,1)} %copy-done.1, bf16[16,16,512]{2,1,0:T(8,128)(2,1)} %slice.28.refs_0_, bf16[16,16,512]{2,1,0:T(8,128)(2,1)} %copy-done.4, bf16[16,16,512]{2,1,0:T(8,128)(2,1)} %copy-done.5, ...), custom_call_target="tpu_custom_call" | custom-call | flops 2000000000 | bytes 6291456 | tf_op jit(solution)/shard_map/finish/pallas_call | solution.py:382
  (38 shorter events, 0.4 us)
Async XLA Ops:
  7.5 25.3 %all-to-all-start.1 = ((bf16[16,16,2048]{2,1,0:T(8,128)(2,1)}), bf16[16,16,2048]{2,1,0:T(8,128)(2,1)S(1)}, u32[]{:S(2)}, u32[]{:S(2)}) async-start(bf16[16,16,2048]{2,1,0:T(8,128)(2,1)} %broadcast_in_dim.9), calls=%async_computation.1 | async-start | bytes 2097152 | tf_op jit(solution)/shard_map/all_to_all | solution.py:423
  32.9 11.9 %copy-start.2 = (bf16[16,16,1536]{2,1,0:T(8,128)(2,1)}, bf16[16,16,1536]{2,1,0:T(8,128)(2,1)S(1)}, u32[]{:S(2)}) copy-start(bf16[16,16,1536]{2,1,0:T(8,128)(2,1)S(1)} %slice.29.refs_0_) | copy-start | bytes 2359300
  32.9 19.5 %collective-permute-start = (bf16[16,16,1536]{2,1,0:T(8,128)(2,1)S(1)}, bf16[16,16,1536]{2,1,0:T(8,128)(2,1)}, u32[]{:S(2)}, u32[]{:S(2)}) collective-permute-start(bf16[16,16,1536]{2,1,0:T(8,128)(2,1)S(1)} %slice.29.refs_0_), channel_id=1, source_target_pairs={{0,2},{1,3},{2,4},{3,5},{4,6},{5,7},{6,0},{7,1},{8,10},{9,11},{10,... | collective-permute-start | bytes 2359304 | tf_op jit(solution)/shard_map/ppermute | solution.py:430
  34.2 19.2 %collective-permute-start.1 = (bf16[16,16,1536]{2,1,0:T(8,128)(2,1)S(1)}, bf16[16,16,1536]{2,1,0:T(8,128)(2,1)}, u32[]{:S(2)}, u32[]{:S(2)}) collective-permute-start(bf16[16,16,1536]{2,1,0:T(8,128)(2,1)S(1)} %slice.29.refs_0_), channel_id=1, source_target_pairs={{0,6},{1,7},{2,0},{3,1},{4,2},{5,3},{6,4},{7,5},{8,14},{9,15},{10,... | collective-permute-start | bytes 2359304 | tf_op jit(solution)/shard_map/ppermute | solution.py:430
  35.7 44.6 %all-to-all-start.2 = ((bf16[128,48,128]{2,1,0:T(8,128)(2,1)}), bf16[128,48,128]{2,1,0:T(8,128)(2,1)S(1)}, u32[]{:S(2)}, u32[]{:S(2)}) async-start(bf16[128,48,128]{2,1,0:T(8,128)(2,1)} %get-tuple-element.22), calls=%async_computation.2 | async-start | bytes 3145728 | tf_op jit(solution)/shard_map/all_to_all | solution.py:452
  44.8 35.5 %collective-permute-start.4 = (bf16[16,16,1536]{2,1,0:T(8,128)(2,1)S(1)}, bf16[16,16,1536]{2,1,0:T(8,128)(2,1)}, u32[]{:S(2)}, u32[]{:S(2)}) collective-permute-start(bf16[16,16,1536]{2,1,0:T(8,128)(2,1)S(1)} %slice.29.refs_0_), channel_id=1, source_target_pairs={{0,1},{1,0},{2,3},{3,2},{4,5},{5,4},{6,7},{7,6},{8,9},{9,8},{10,11... | collective-permute-start | bytes 2359304 | tf_op jit(solution)/shard_map/ppermute | solution.py:435
  54.5 23.2 %collective-permute-start.2 = (bf16[8,16,1536]{2,1,0:T(8,128)(2,1)S(1)}, bf16[8,16,1536]{2,1,0:T(8,128)(2,1)}, u32[]{:S(2)}, u32[]{:S(2)}) collective-permute-start(bf16[8,16,1536]{2,1,0:T(8,128)(2,1)S(1)} %slice.32), channel_id=1, source_target_pairs={{0,2},{1,3},{2,4},{3,5},{4,6},{5,7},{6,0},{7,1},{8,10},{9,11},{10,... | collective-permute-start | bytes 1179656 | tf_op jit(solution)/shard_map/ppermute | solution.py:430
  54.5 27.0 %collective-permute-start.5 = (bf16[16,16,1536]{2,1,0:T(8,128)(2,1)}, bf16[16,16,1536]{2,1,0:T(8,128)(2,1)}, u32[]{:S(2)}, u32[]{:S(2)}) collective-permute-start(bf16[16,16,1536]{2,1,0:T(8,128)(2,1)} %collective-permute-done.refs_1_), channel_id=1, source_target_pairs={{0,1},{1,0},{2,3},{3,2},{4,5},{5,4},{6,7},{7,6},{8,9},{9,8},{10,11... | collective-permute-start | bytes 2359304 | tf_op jit(solution)/shard_map/ppermute | solution.py:435
  59.6 23.5 %collective-permute-start.6 = (bf16[16,16,1536]{2,1,0:T(8,128)(2,1)}, bf16[16,16,1536]{2,1,0:T(8,128)(2,1)}, u32[]{:S(2)}, u32[]{:S(2)}) collective-permute-start(bf16[16,16,1536]{2,1,0:T(8,128)(2,1)} %collective-permute-done.1.refs_2_), channel_id=1, source_target_pairs={{0,1},{1,0},{2,3},{3,2},{4,5},{5,4},{6,7},{7,6},{8,9},{9,8},{10,11... | collective-permute-start | bytes 2359304 | tf_op jit(solution)/shard_map/ppermute | solution.py:435
  59.6 19.9 %collective-permute-start.3 = (bf16[8,16,1536]{2,1,0:T(8,128)(2,1)S(1)}, bf16[8,16,1536]{2,1,0:T(8,128)(2,1)}, u32[]{:S(2)}, u32[]{:S(2)}) collective-permute-start(bf16[8,16,1536]{2,1,0:T(8,128)(2,1)S(1)} %slice.33), channel_id=1, source_target_pairs={{0,6},{1,7},{2,0},{3,1},{4,2},{5,3},{6,4},{7,5},{8,14},{9,15},{10,... | collective-permute-start | bytes 1179656 | tf_op jit(solution)/shard_map/ppermute | solution.py:430
  77.7 6.8 %collective-permute-start.7 = (bf16[8,16,1536]{2,1,0:T(8,128)(2,1)}, bf16[8,16,1536]{2,1,0:T(8,128)(2,1)}, u32[]{:S(2)}, u32[]{:S(2)}) collective-permute-start(bf16[8,16,1536]{2,1,0:T(8,128)(2,1)} %collective-permute-done.2.refs_3_), channel_id=1, source_target_pairs={{0,1},{1,0},{2,3},{3,2},{4,5},{5,4},{6,7},{7,6},{8,9},{9,8},{10,11... | collective-permute-start | bytes 1179656 | tf_op jit(solution)/shard_map/ppermute | solution.py:435
  79.5 4.9 %collective-permute-start.8 = (bf16[8,16,1536]{2,1,0:T(8,128)(2,1)}, bf16[8,16,1536]{2,1,0:T(8,128)(2,1)}, u32[]{:S(2)}, u32[]{:S(2)}) collective-permute-start(bf16[8,16,1536]{2,1,0:T(8,128)(2,1)} %collective-permute-done.3.refs_4_), channel_id=1, source_target_pairs={{0,1},{1,0},{2,3},{3,2},{4,5},{5,4},{6,7},{7,6},{8,9},{9,8},{10,11... | collective-permute-start | bytes 1179656 | tf_op jit(solution)/shard_map/ppermute | solution.py:435
  80.3 4.2 %copy-start = (bf16[128,48,128]{2,1,0:T(8,128)(2,1)}, bf16[128,48,128]{2,1,0:T(8,128)(2,1)S(1)}, u32[]{:S(2)}) copy-start(bf16[128,48,128]{2,1,0:T(8,128)(2,1)S(1)} %all-to-all-done.2) | copy-start | bytes 4718596
  80.3 21.7 %collective-permute-start.9 = (bf16[16,16,512]{2,1,0:T(8,128)(2,1)}, bf16[16,16,512]{2,1,0:T(8,128)(2,1)S(1)}, u32[]{:S(2)}, u32[]{:S(2)}) collective-permute-start(bf16[16,16,512]{2,1,0:T(8,128)(2,1)} %slice.28.refs_0_), channel_id=1, source_target_pairs={{0,2},{1,3},{2,4},{3,5},{4,6},{5,7},{6,0},{7,1},{8,10},{9,11},{10,... | collective-permute-start | bytes 786440 | tf_op jit(solution)/shard_map/ppermute | solution.py:430
  81.6 20.4 %collective-permute-start.10 = (bf16[16,16,512]{2,1,0:T(8,128)(2,1)}, bf16[16,16,512]{2,1,0:T(8,128)(2,1)S(1)}, u32[]{:S(2)}, u32[]{:S(2)}) collective-permute-start(bf16[16,16,512]{2,1,0:T(8,128)(2,1)} %slice.28.refs_0_), channel_id=1, source_target_pairs={{0,6},{1,7},{2,0},{3,1},{4,2},{5,3},{6,4},{7,5},{8,14},{9,15},{10,... | collective-permute-start | bytes 786440 | tf_op jit(solution)/shard_map/ppermute | solution.py:430
  83.1 18.9 %collective-permute-start.11 = (bf16[16,16,512]{2,1,0:T(8,128)(2,1)}, bf16[16,16,512]{2,1,0:T(8,128)(2,1)S(1)}, u32[]{:S(2)}, u32[]{:S(2)}) collective-permute-start(bf16[16,16,512]{2,1,0:T(8,128)(2,1)} %slice.28.refs_0_), channel_id=1, source_target_pairs={{0,4},{1,5},{2,6},{3,7},{4,0},{5,1},{6,2},{7,3},{8,12},{9,13},{10,... | collective-permute-start | bytes 786440 | tf_op jit(solution)/shard_map/ppermute | solution.py:430
  102.0 10.2 %copy-start.4 = (bf16[16,16,512]{2,1,0:T(8,128)(2,1)}, bf16[16,16,512]{2,1,0:T(8,128)(2,1)S(1)}, u32[]{:S(2)}) copy-start(bf16[16,16,512]{2,1,0:T(8,128)(2,1)S(1)} %collective-permute-done.9.refs_1_) | copy-start | bytes 786436
  102.0 10.3 %copy-start.5 = (bf16[16,16,512]{2,1,0:T(8,128)(2,1)}, bf16[16,16,512]{2,1,0:T(8,128)(2,1)S(1)}, u32[]{:S(2)}) copy-start(bf16[16,16,512]{2,1,0:T(8,128)(2,1)S(1)} %collective-permute-done.10.refs_2_) | copy-start | bytes 786436
  102.0 10.7 %copy-start.6 = (bf16[16,16,512]{2,1,0:T(8,128)(2,1)}, bf16[16,16,512]{2,1,0:T(8,128)(2,1)S(1)}, u32[]{:S(2)}) copy-start(bf16[16,16,512]{2,1,0:T(8,128)(2,1)S(1)} %collective-permute-done.11.refs_3_) | copy-start | bytes 786436
  102.0 9.0 %copy-start.3 = (bf16[16,16,512]{2,1,0:T(8,128)(2,1)S(1)}, bf16[16,16,512]{2,1,0:T(8,128)(2,1)}, u32[]{:S(2)}) copy-start(bf16[16,16,512]{2,1,0:T(8,128)(2,1)} %slice.28.refs_0_) | copy-start | bytes 786436
  102.0 33.9 %all-to-all-start.3 = ((bf16[128,48,128]{2,1,0:T(8,128)(2,1)}), bf16[128,48,128]{2,1,0:T(8,128)(2,1)S(1)}, u32[]{:S(2)}, u32[]{:S(2)}) async-start(bf16[128,48,128]{2,1,0:T(8,128)(2,1)} %bitcast.11), calls=%async_computation.3 | async-start | bytes 3145728 | tf_op jit(solution)/shard_map/all_to_all | solution.py:452
  111.0 2.3 %collective-permute-start.12 = (bf16[16,16,512]{2,1,0:T(8,128)(2,1)S(1)}, bf16[16,16,512]{2,1,0:T(8,128)(2,1)S(1)}, u32[]{:S(2)}, u32[]{:S(2)}) collective-permute-start(bf16[16,16,512]{2,1,0:T(8,128)(2,1)S(1)} %copy-done.3), channel_id=1, source_target_pairs={{0,1},{1,0},{2,3},{3,2},{4,5},{5,4},{6,7},{7,6},{8,9},{9,8},{10,11... | collective-permute-start | bytes 786440 | tf_op jit(solution)/shard_map/ppermute | solution.py:435
  112.2 1.5 %collective-permute-start.13 = (bf16[16,16,512]{2,1,0:T(8,128)(2,1)S(1)}, bf16[16,16,512]{2,1,0:T(8,128)(2,1)S(1)}, u32[]{:S(2)}, u32[]{:S(2)}) collective-permute-start(bf16[16,16,512]{2,1,0:T(8,128)(2,1)S(1)} %collective-permute-done.9.refs_1_), channel_id=1, source_target_pairs={{0,1},{1,0},{2,3},{3,2},{4,5},{5,4},{6,7},{7,6},{8,9},{9,8},{10,11... | collective-permute-start | bytes 786440 | tf_op jit(solution)/shard_map/ppermute | solution.py:435
  112.3 2.2 %collective-permute-start.14 = (bf16[16,16,512]{2,1,0:T(8,128)(2,1)S(1)}, bf16[16,16,512]{2,1,0:T(8,128)(2,1)S(1)}, u32[]{:S(2)}, u32[]{:S(2)}) collective-permute-start(bf16[16,16,512]{2,1,0:T(8,128)(2,1)S(1)} %collective-permute-done.10.refs_2_), channel_id=1, source_target_pairs={{0,1},{1,0},{2,3},{3,2},{4,5},{5,4},{6,7},{7,6},{8,9},{9,8},{10,11... | collective-permute-start | bytes 786440 | tf_op jit(solution)/shard_map/ppermute | solution.py:435
  112.7 1.9 %collective-permute-start.15 = (bf16[16,16,512]{2,1,0:T(8,128)(2,1)S(1)}, bf16[16,16,512]{2,1,0:T(8,128)(2,1)}, u32[]{:S(2)}, u32[]{:S(2)}) collective-permute-start(bf16[16,16,512]{2,1,0:T(8,128)(2,1)S(1)} %collective-permute-done.11.refs_3_), channel_id=1, source_target_pairs={{0,1},{1,0},{2,3},{3,2},{4,5},{5,4},{6,7},{7,6},{8,9},{9,8},{10,11... | collective-permute-start | bytes 786440 | tf_op jit(solution)/shard_map/ppermute | solution.py:435
  113.4 22.6 %copy-start.7 = (bf16[16,16,512]{2,1,0:T(8,128)(2,1)}, bf16[16,16,512]{2,1,0:T(8,128)(2,1)S(1)}, u32[]{:S(2)}) copy-start(bf16[16,16,512]{2,1,0:T(8,128)(2,1)S(1)} %collective-permute-done.12.refs_4_) | copy-start | bytes 786436
  113.7 22.2 %copy-start.8 = (bf16[16,16,512]{2,1,0:T(8,128)(2,1)}, bf16[16,16,512]{2,1,0:T(8,128)(2,1)S(1)}, u32[]{:S(2)}) copy-start(bf16[16,16,512]{2,1,0:T(8,128)(2,1)S(1)} %collective-permute-done.13.refs_5_) | copy-start | bytes 786436
  114.5 21.5 %copy-start.9 = (bf16[16,16,512]{2,1,0:T(8,128)(2,1)}, bf16[16,16,512]{2,1,0:T(8,128)(2,1)S(1)}, u32[]{:S(2)}) copy-start(bf16[16,16,512]{2,1,0:T(8,128)(2,1)S(1)} %collective-permute-done.14.refs_6_) | copy-start | bytes 786436
  136.0 1.2 copy-start.1

commit v6 on v5

--- a/solution.py
+++ b/solution.py
@@ -34,9 +34,9 @@
             scores = jnp.minimum(scores, cap)
         top = jnp.max(scores, axis=-1, keepdims=True)
         weights = jnp.exp2((scores - top) * (scale * LOG2E))
-        total = jnp.sum(weights, axis=-1, keepdims=True)
-        out = jnp.dot(weights.astype(BF16), v2, preferred_element_type=F32)
-        outs.append(out * (1.0 / total))
+        both = jnp.concatenate([v2, jnp.ones_like(v2)], axis=1)
+        out = jnp.dot(weights.astype(BF16), both, preferred_element_type=F32)
+        outs.append(out[:, :LANES] / out[:, LANES:])
     return jnp.where(lane < 64, outs[0], outs[1]).astype(BF16)
 
 
@@ -126,9 +126,8 @@
     third = parts // 3
     per = CHUNK // LANES
 
-    @pl.loop(0, count)
-    def _(f):
-        at = pl.ds(pl.multiple_of(f * tokens, tokens), tokens)
+    for f in range(count):
+        at = pl.ds(f * tokens, tokens)
         for pair in range(HEADS // 2):
             c, cols = pair // per, pl.ds((pair % per) * LANES, LANES)
             heads[:, pair * LANES : (pair + 1) * LANES] = head_pair(
@@ -263,8 +262,7 @@
 
     @pl.loop(0, local_pos)
     def _(i):
-        @pl.loop(0, total // span)
-        def _(b):
+        for b in range(total // span):
             at = pl.ds(pl.multiple_of(i * total + b * span, LANES // 2), span)
             near = pl.ds(pl.multiple_of(i * total + b * back, LANES), seen)
             limit = cap[b]
@@ -396,7 +394,7 @@
             pltpu.SemaphoreType.DMA((len(weights),)),
             pltpu.SemaphoreType.DMA((count,)),
         ],
-        compiler_params=pltpu.CompilerParams(vmem_limit_bytes=VMEM),
+        compiler_params=pltpu.CompilerParams(vmem_limit_bytes=VMEM - 2 * 2**20),
         cost_estimate=pl.CostEstimate(flops=2 * 10**9, bytes_accessed=6 * 2**20, transcendentals=0),
         name="finish",
     )(mixed, recv, *weights)

time: 144 us -> 140 us (0.972)
  Pallas kernels: 40.8 us -> 37 us
  starting transfers between devices: 45 us -> 48.2 us
  waiting for transfers between devices: 45.5 us -> 42.5 us
    ppermute x9, starting transfers between devices: 9.86 us -> 14.5 us  [from_sibling(): return lax.ppermute(part, AXES, [(k, k ^ 1) for k in range(count)])]
    ppermute x7, waiting for transfers between devices: 22.3 us -> 18.6 us  [along_x(): return lax.ppermute(part, AXES, pairs)]
    pallas_call x1, Pallas kernels: 17.5 us -> 15.6 us  [spatial(): pl.pallas_call(functools.partial(spatial_kernel, tokens), out_shape=(jax....]
    pallas_call x1, Pallas kernels: 17.5 us -> 15.6 us  [temporal(): pl.pallas_call(functools.partial(temporal_kernel, local_pos), out_shape=j...]
  transfers between devices with their start and end apart: 19 -> 19, of which waited for: 7 -> 8; matrix products, arithmetic and copies ran while one was open for 2% -> 2% of each run, Pallas kernels for 24% -> 22%
where the time goes in v6:
time: 140 us
  starting transfers between devices  48.2 us (34%)
  waiting for transfers between devices  42.5 us (30%)
  Pallas kernels  37 us (26%)
  local copies, waits for them, and re-layouts  6.61 us (5%)
  blocking collectives  4.86 us (3%)
    all_to_all x2, waiting for transfers between devices, exchange(): return lax.all_to_all(blocks, AXES, split_axis=0, concat_axis=0, tiled=True)  21.3 us
    ppermute x7, waiting for transfers between devices, along_x(): return lax.ppermute(part, AXES, pairs)  18.6 us
    all_to_all x2, starting transfers between devices, exchange(): return lax.all_to_all(blocks, AXES, split_axis=0, concat_axis=0, tiled=True)  16.8 us
    pallas_call x1, Pallas kernels, spatial(): pl.pallas_call(functools.partial(spatial_kernel, tokens), out_shape=(jax....  15.6 us
    pallas_call x1, Pallas kernels, temporal(): pl.pallas_call(functools.partial(temporal_kernel, local_pos), out_shape=j...  15.6 us
    ppermute x9, starting transfers between devices, from_sibling(): return lax.ppermute(part, AXES, [(k, k ^ 1) for k in range(count)])  14.5 us
    ppermute x7, starting transfers between devices, along_x(): return lax.ppermute(part, AXES, pairs)  9.03 us
    all_to_all x1, starting transfers between devices, spread(): lax.all_to_all(copies, AXES, split_axis=0, concat_axis=0, tiled=True, axi...  7.85 us
  transfers between devices with their start and end apart: 19, of which 8 were waited for; matrix products, arithmetic and copies ran while one was open for 2% of the time, Pallas kernels for 22%

profile of v6, /device:TPU:1, one launch (start us, length us, event | category | flops | bytes accessed | tf_op | source)
XLA Modules:
  0.0 139.6 jit_solution(15384998362489400009)
XLA Ops:
  0.0 0.7 fusion.1
  0.7 0.8 fusion
  1.5 4.9 %all_to_all.31 = bf16[8,2,2048]{2,0,1:T(8,128)(2,1)S(1)} all-to-all(bf16[8,2,2048]{2,0,1:T(8,128)(2,1)S(1)} %bitcast.13), channel_id=1, replica_groups={{0,1},{2,3},{4,5},{6,7},{8,9},{10,11},{12,13},{14,15},{16,17},{18,19},{..., dimensions={1} | all-to-all | bytes 131072 | tf_op jit(solution)/shard_map/all_to_all | solution.py:414
  6.3 1.1 broadcast_in_dim.9
  7.5 7.9 %all-to-all-start.1 = ((bf16[16,16,2048]{2,1,0:T(8,128)(2,1)}), bf16[16,16,2048]{2,1,0:T(8,128)(2,1)S(1)}, u32[]{:S(2)}, u32[]{:S(2)}) async-start(bf16[16,16,2048]{2,1,0:T(8,128)(2,1)} %broadcast_in_dim.9), calls=%async_computation.1 | async-start | bytes 2097152 | tf_op jit(solution)/shard_map/all_to_all | solution.py:421
  15.3 15.6 %spatial.1 = (bf16[768,1024]{1,0:T(8,128)(2,1)}, bf16[128,48,128]{2,1,0:T(8,128)(2,1)}) custom-call(bf16[768,1024]{1,0:T(8,128)(2,1)} %bitcast.14, f32[1,1024]{1,0:T(1,128)} %bitcast.15, f32[1,1024]{1,0:T(1,128)} %bitcast.16, bf16[1024,3072]{1,0:T(8,128)(2,1)} %w_qkv_hbm.1, bf16[1024,1024]{1,0:T(8,128)(2,1)} %w_o_hbm.1), custom_call_target="tpu_custom_call" | custom-call | flops 16000000000 | bytes 14680064 | tf_op jit(solution)/shard_map/spatial/pallas_call | solution.py:157
  30.9 0.8 all-to-all-done.1
  31.8 1.3 collective-permute-start
  33.0 1.5 %collective-permute-start.1 = (bf16[16,16,1536]{2,1,0:T(8,128)(2,1)S(1)}, bf16[16,16,1536]{2,1,0:T(8,128)(2,1)}, u32[]{:S(2)}, u32[]{:S(2)}) collective-permute-start(bf16[16,16,1536]{2,1,0:T(8,128)(2,1)S(1)} %slice.29.refs_0_), channel_id=1, source_target_pairs={{0,6},{1,7},{2,0},{3,1},{4,2},{5,3},{6,4},{7,5},{8,14},{9,15},{10,... | collective-permute-start | bytes 2359304 | tf_op jit(solution)/shard_map/ppermute | solution.py:428
  34.5 8.4 %all-to-all-start.2 = ((bf16[128,48,128]{2,1,0:T(8,128)(2,1)}), bf16[128,48,128]{2,1,0:T(8,128)(2,1)S(1)}, u32[]{:S(2)}, u32[]{:S(2)}) async-start(bf16[128,48,128]{2,1,0:T(8,128)(2,1)} %get-tuple-element.22), calls=%async_computation.2 | async-start | bytes 3145728 | tf_op jit(solution)/shard_map/all_to_all | solution.py:450
  42.9 1.1 collective-permute-start.4
  44.1 6.0 %collective-permute-done.refs_1_ = bf16[16,16,1536]{2,1,0:T(8,128)(2,1)} collective-permute-done((bf16[16,16,1536]{2,1,0:T(8,128)(2,1)S(1)}, bf16[16,16,1536]{2,1,0:T(8,128)(2,1)}, u32[]{:S(2)}, u32[]{:S(2)}) %collective-permute-start) | collective-permute-done | bytes 786464 | tf_op jit(solution)/shard_map/ppermute | solution.py:428
  50.1 1.0 slice.32
  51.1 1.0 slice.33
  52.3 8.5 %collective-permute-start.5 = (bf16[16,16,1536]{2,1,0:T(8,128)(2,1)}, bf16[16,16,1536]{2,1,0:T(8,128)(2,1)}, u32[]{:S(2)}, u32[]{:S(2)}) collective-permute-start(bf16[16,16,1536]{2,1,0:T(8,128)(2,1)} %collective-permute-done.refs_1_), channel_id=1, source_target_pairs={{0,1},{1,0},{2,3},{3,2},{4,5},{5,4},{6,7},{7,6},{8,9},{9,8},{10,11... | collective-permute-start | bytes 2359304 | tf_op jit(solution)/shard_map/ppermute | solution.py:433
  60.8 2.0 %collective-permute-start.3 = (bf16[8,16,1536]{2,1,0:T(8,128)(2,1)S(1)}, bf16[8,16,1536]{2,1,0:T(8,128)(2,1)}, u32[]{:S(2)}, u32[]{:S(2)}) collective-permute-start(bf16[8,16,1536]{2,1,0:T(8,128)(2,1)S(1)} %slice.33), channel_id=1, source_target_pairs={{0,6},{1,7},{2,0},{3,1},{4,2},{5,3},{6,4},{7,5},{8,14},{9,15},{10,... | collective-permute-start | bytes 1179656 | tf_op jit(solution)/shard_map/ppermute | solution.py:428
  62.8 12.6 %collective-permute-done.2.refs_3_ = bf16[8,16,1536]{2,1,0:T(8,128)(2,1)} collective-permute-done((bf16[8,16,1536]{2,1,0:T(8,128)(2,1)S(1)}, bf16[8,16,1536]{2,1,0:T(8,128)(2,1)}, u32[]{:S(2)}, u32[]{:S(2)}) %collective-permute-start.2) | collective-permute-done | bytes 393248 | tf_op jit(solution)/shard_map/ppermute | solution.py:428
  75.4 3.0 %collective-permute-start.7 = (bf16[8,16,1536]{2,1,0:T(8,128)(2,1)}, bf16[8,16,1536]{2,1,0:T(8,128)(2,1)}, u32[]{:S(2)}, u32[]{:S(2)}) collective-permute-start(bf16[8,16,1536]{2,1,0:T(8,128)(2,1)} %collective-permute-done.2.refs_3_), channel_id=1, source_target_pairs={{0,1},{1,0},{2,3},{3,2},{4,5},{5,4},{6,7},{7,6},{8,9},{9,8},{10,11... | collective-permute-start | bytes 1179656 | tf_op jit(solution)/shard_map/ppermute | solution.py:433
  78.4 0.7 slice.28.refs_0_
  79.1 1.5 %collective-permute-start.9 = (bf16[16,16,512]{2,1,0:T(8,128)(2,1)}, bf16[16,16,512]{2,1,0:T(8,128)(2,1)S(1)}, u32[]{:S(2)}, u32[]{:S(2)}) collective-permute-start(bf16[16,16,512]{2,1,0:T(8,128)(2,1)} %slice.28.refs_0_), channel_id=1, source_target_pairs={{0,2},{1,3},{2,4},{3,5},{4,6},{5,7},{6,0},{7,1},{8,10},{9,11},{10,... | collective-permute-start | bytes 786440 | tf_op jit(solution)/shard_map/ppermute | solution.py:428
  80.6 1.6 %collective-permute-start.10 = (bf16[16,16,512]{2,1,0:T(8,128)(2,1)}, bf16[16,16,512]{2,1,0:T(8,128)(2,1)S(1)}, u32[]{:S(2)}, u32[]{:S(2)}) collective-permute-start(bf16[16,16,512]{2,1,0:T(8,128)(2,1)} %slice.28.refs_0_), channel_id=1, source_target_pairs={{0,6},{1,7},{2,0},{3,1},{4,2},{5,3},{6,4},{7,5},{8,14},{9,15},{10,... | collective-permute-start | bytes 786440 | tf_op jit(solution)/shard_map/ppermute | solution.py:428
  82.2 1.2 collective-permute-start.11
  83.3 15.6 %temporal.1 = bf16[6144,128]{1,0:T(8,128)(2,1)} custom-call(s32[48]{0:T(128)} %len_ref.1, bf16[6144,128]{1,0:T(8,128)(2,1)} %bitcast.10, bf16[16,16,1536]{2,1,0:T(8,128)(2,1)} %copy-done.2, bf16[16,16,1536]{2,1,0:T(8,128)(2,1)} %collective-permute-done.refs_1_, bf16[16,16,1536]{2,1,0:T(8,128)(2,1)} %collective-permute-done.1.refs_2_, ...), custom_call_target="tpu_custom_call" | custom-call | flops 16000000000 | bytes 14680064 | tf_op jit(solution)/shard_map/temporal/pallas_call | solution.py:297
  99.0 8.5 %all-to-all-start.3 = ((bf16[128,48,128]{2,1,0:T(8,128)(2,1)}), bf16[128,48,128]{2,1,0:T(8,128)(2,1)S(1)}, u32[]{:S(2)}, u32[]{:S(2)}) async-start(bf16[128,48,128]{2,1,0:T(8,128)(2,1)} %bitcast.11), calls=%async_computation.3 | async-start | bytes 3145728 | tf_op jit(solution)/shard_map/all_to_all | solution.py:450
  107.5 1.1 collective-permute-start.12
  108.7 0.4 collective-permute-start.14
  109.3 0.5 collective-permute-done.12.refs_4_
  109.8 0.4 collective-permute-done.13.refs_5_
  110.2 0.7 collective-permute-done.14.refs_6_
  111.1 21.3 %all-to-all-done.3.recv_hbm = bf16[128,48,128]{2,1,0:T(8,128)(2,1)S(1)} async-done(((bf16[128,48,128]{2,1,0:T(8,128)(2,1)}), bf16[128,48,128]{2,1,0:T(8,128)(2,1)S(1)}, u32[]{:S(2)}, u32[]{:S(2)}) %all-to-all-start.3) | async-done | bytes 1572896 | tf_op jit(solution)/shard_map/all_to_all | solution.py:450
  132.4 1.1 copy-done.1
  133.5 5.8 %finish.1 = bf16[768,1024]{1,0:T(8,128)(2,1)} custom-call(bf16[768,1024]{1,0:T(8,128)(2,1)} %get-tuple-element.20.mixed_hbm, bf16[128,48,128]{2,1,0:T(8,128)(2,1)} %copy-done.1, bf16[16,16,512]{2,1,0:T(8,128)(2,1)} %slice.28.refs_0_, bf16[16,16,512]{2,1,0:T(8,128)(2,1)} %copy-done.4, bf16[16,16,512]{2,1,0:T(8,128)(2,1)} %copy-done.5, ...), custom_call_target="tpu_custom_call" | custom-call | flops 2000000000 | bytes 6291456 | tf_op jit(solution)/shard_map/finish/pallas_call | solution.py:380
  (38 shorter events, 0.5 us)
Async XLA Ops:
  7.5 24.2 %all-to-all-start.1 = ((bf16[16,16,2048]{2,1,0:T(8,128)(2,1)}), bf16[16,16,2048]{2,1,0:T(8,128)(2,1)S(1)}, u32[]{:S(2)}, u32[]{:S(2)}) async-start(bf16[16,16,2048]{2,1,0:T(8,128)(2,1)} %broadcast_in_dim.9), calls=%async_computation.1 | async-start | bytes 2097152 | tf_op jit(solution)/shard_map/all_to_all | solution.py:421
  31.8 11.2 %copy-start.2 = (bf16[16,16,1536]{2,1,0:T(8,128)(2,1)}, bf16[16,16,1536]{2,1,0:T(8,128)(2,1)S(1)}, u32[]{:S(2)}) copy-start(bf16[16,16,1536]{2,1,0:T(8,128)(2,1)S(1)} %slice.29.refs_0_) | copy-start | bytes 2359300
  31.8 18.3 %collective-permute-start = (bf16[16,16,1536]{2,1,0:T(8,128)(2,1)S(1)}, bf16[16,16,1536]{2,1,0:T(8,128)(2,1)}, u32[]{:S(2)}, u32[]{:S(2)}) collective-permute-start(bf16[16,16,1536]{2,1,0:T(8,128)(2,1)S(1)} %slice.29.refs_0_), channel_id=1, source_target_pairs={{0,2},{1,3},{2,4},{3,5},{4,6},{5,7},{6,0},{7,1},{8,10},{9,11},{10,... | collective-permute-start | bytes 2359304 | tf_op jit(solution)/shard_map/ppermute | solution.py:428
  33.0 18.1 %collective-permute-start.1 = (bf16[16,16,1536]{2,1,0:T(8,128)(2,1)S(1)}, bf16[16,16,1536]{2,1,0:T(8,128)(2,1)}, u32[]{:S(2)}, u32[]{:S(2)}) collective-permute-start(bf16[16,16,1536]{2,1,0:T(8,128)(2,1)S(1)} %slice.29.refs_0_), channel_id=1, source_target_pairs={{0,6},{1,7},{2,0},{3,1},{4,2},{5,3},{6,4},{7,5},{8,14},{9,15},{10,... | collective-permute-start | bytes 2359304 | tf_op jit(solution)/shard_map/ppermute | solution.py:428
  34.5 44.6 %all-to-all-start.2 = ((bf16[128,48,128]{2,1,0:T(8,128)(2,1)}), bf16[128,48,128]{2,1,0:T(8,128)(2,1)S(1)}, u32[]{:S(2)}, u32[]{:S(2)}) async-start(bf16[128,48,128]{2,1,0:T(8,128)(2,1)} %get-tuple-element.22), calls=%async_computation.2 | async-start | bytes 3145728 | tf_op jit(solution)/shard_map/all_to_all | solution.py:450
  42.9 36.2 %collective-permute-start.4 = (bf16[16,16,1536]{2,1,0:T(8,128)(2,1)S(1)}, bf16[16,16,1536]{2,1,0:T(8,128)(2,1)}, u32[]{:S(2)}, u32[]{:S(2)}) collective-permute-start(bf16[16,16,1536]{2,1,0:T(8,128)(2,1)S(1)} %slice.29.refs_0_), channel_id=1, source_target_pairs={{0,1},{1,0},{2,3},{3,2},{4,5},{5,4},{6,7},{7,6},{8,9},{9,8},{10,11... | collective-permute-start | bytes 2359304 | tf_op jit(solution)/shard_map/ppermute | solution.py:433
  52.2 23.2 %collective-permute-start.2 = (bf16[8,16,1536]{2,1,0:T(8,128)(2,1)S(1)}, bf16[8,16,1536]{2,1,0:T(8,128)(2,1)}, u32[]{:S(2)}, u32[]{:S(2)}) collective-permute-start(bf16[8,16,1536]{2,1,0:T(8,128)(2,1)S(1)} %slice.32), channel_id=1, source_target_pairs={{0,2},{1,3},{2,4},{3,5},{4,6},{5,7},{6,0},{7,1},{8,10},{9,11},{10,... | collective-permute-start | bytes 1179656 | tf_op jit(solution)/shard_map/ppermute | solution.py:428
  52.3 28.3 %collective-permute-start.5 = (bf16[16,16,1536]{2,1,0:T(8,128)(2,1)}, bf16[16,16,1536]{2,1,0:T(8,128)(2,1)}, u32[]{:S(2)}, u32[]{:S(2)}) collective-permute-start(bf16[16,16,1536]{2,1,0:T(8,128)(2,1)} %collective-permute-done.refs_1_), channel_id=1, source_target_pairs={{0,1},{1,0},{2,3},{3,2},{4,5},{5,4},{6,7},{7,6},{8,9},{9,8},{10,11... | collective-permute-start | bytes 2359304 | tf_op jit(solution)/shard_map/ppermute | solution.py:433
  60.8 21.4 %collective-permute-start.6 = (bf16[16,16,1536]{2,1,0:T(8,128)(2,1)}, bf16[16,16,1536]{2,1,0:T(8,128)(2,1)}, u32[]{:S(2)}, u32[]{:S(2)}) collective-permute-start(bf16[16,16,1536]{2,1,0:T(8,128)(2,1)} %collective-permute-done.1.refs_2_), channel_id=1, source_target_pairs={{0,1},{1,0},{2,3},{3,2},{4,5},{5,4},{6,7},{7,6},{8,9},{9,8},{10,11... | collective-permute-start | bytes 2359304 | tf_op jit(solution)/shard_map/ppermute | solution.py:433
  60.8 17.6 %collective-permute-start.3 = (bf16[8,16,1536]{2,1,0:T(8,128)(2,1)S(1)}, bf16[8,16,1536]{2,1,0:T(8,128)(2,1)}, u32[]{:S(2)}, u32[]{:S(2)}) collective-permute-start(bf16[8,16,1536]{2,1,0:T(8,128)(2,1)S(1)} %slice.33), channel_id=1, source_target_pairs={{0,6},{1,7},{2,0},{3,1},{4,2},{5,3},{6,4},{7,5},{8,14},{9,15},{10,... | collective-permute-start | bytes 1179656 | tf_op jit(solution)/shard_map/ppermute | solution.py:428
  75.4 7.9 %collective-permute-start.7 = (bf16[8,16,1536]{2,1,0:T(8,128)(2,1)}, bf16[8,16,1536]{2,1,0:T(8,128)(2,1)}, u32[]{:S(2)}, u32[]{:S(2)}) collective-permute-start(bf16[8,16,1536]{2,1,0:T(8,128)(2,1)} %collective-permute-done.2.refs_3_), channel_id=1, source_target_pairs={{0,1},{1,0},{2,3},{3,2},{4,5},{5,4},{6,7},{7,6},{8,9},{9,8},{10,11... | collective-permute-start | bytes 1179656 | tf_op jit(solution)/shard_map/ppermute | solution.py:433
  78.4 4.9 %collective-permute-start.8 = (bf16[8,16,1536]{2,1,0:T(8,128)(2,1)}, bf16[8,16,1536]{2,1,0:T(8,128)(2,1)}, u32[]{:S(2)}, u32[]{:S(2)}) collective-permute-start(bf16[8,16,1536]{2,1,0:T(8,128)(2,1)} %collective-permute-done.3.refs_4_), channel_id=1, source_target_pairs={{0,1},{1,0},{2,3},{3,2},{4,5},{5,4},{6,7},{7,6},{8,9},{9,8},{10,11... | collective-permute-start | bytes 1179656 | tf_op jit(solution)/shard_map/ppermute | solution.py:433
  79.1 4.2 %copy-start = (bf16[128,48,128]{2,1,0:T(8,128)(2,1)}, bf16[128,48,128]{2,1,0:T(8,128)(2,1)S(1)}, u32[]{:S(2)}) copy-start(bf16[128,48,128]{2,1,0:T(8,128)(2,1)S(1)} %all-to-all-done.2) | copy-start | bytes 4718596
  79.1 19.8 %collective-permute-start.9 = (bf16[16,16,512]{2,1,0:T(8,128)(2,1)}, bf16[16,16,512]{2,1,0:T(8,128)(2,1)S(1)}, u32[]{:S(2)}, u32[]{:S(2)}) collective-permute-start(bf16[16,16,512]{2,1,0:T(8,128)(2,1)} %slice.28.refs_0_), channel_id=1, source_target_pairs={{0,2},{1,3},{2,4},{3,5},{4,6},{5,7},{6,0},{7,1},{8,10},{9,11},{10,... | collective-permute-start | bytes 786440 | tf_op jit(solution)/shard_map/ppermute | solution.py:428
  80.6 18.4 %collective-permute-start.10 = (bf16[16,16,512]{2,1,0:T(8,128)(2,1)}, bf16[16,16,512]{2,1,0:T(8,128)(2,1)S(1)}, u32[]{:S(2)}, u32[]{:S(2)}) collective-permute-start(bf16[16,16,512]{2,1,0:T(8,128)(2,1)} %slice.28.refs_0_), channel_id=1, source_target_pairs={{0,6},{1,7},{2,0},{3,1},{4,2},{5,3},{6,4},{7,5},{8,14},{9,15},{10,... | collective-permute-start | bytes 786440 | tf_op jit(solution)/shard_map/ppermute | solution.py:428
  82.2 16.8 %collective-permute-start.11 = (bf16[16,16,512]{2,1,0:T(8,128)(2,1)}, bf16[16,16,512]{2,1,0:T(8,128)(2,1)S(1)}, u32[]{:S(2)}, u32[]{:S(2)}) collective-permute-start(bf16[16,16,512]{2,1,0:T(8,128)(2,1)} %slice.28.refs_0_), channel_id=1, source_target_pairs={{0,4},{1,5},{2,6},{3,7},{4,0},{5,1},{6,2},{7,3},{8,12},{9,13},{10,... | collective-permute-start | bytes 786440 | tf_op jit(solution)/shard_map/ppermute | solution.py:428
  99.0 9.7 %copy-start.4 = (bf16[16,16,512]{2,1,0:T(8,128)(2,1)}, bf16[16,16,512]{2,1,0:T(8,128)(2,1)S(1)}, u32[]{:S(2)}) copy-start(bf16[16,16,512]{2,1,0:T(8,128)(2,1)S(1)} %collective-permute-done.9.refs_1_) | copy-start | bytes 786436
  99.0 9.8 %copy-start.5 = (bf16[16,16,512]{2,1,0:T(8,128)(2,1)}, bf16[16,16,512]{2,1,0:T(8,128)(2,1)S(1)}, u32[]{:S(2)}) copy-start(bf16[16,16,512]{2,1,0:T(8,128)(2,1)S(1)} %collective-permute-done.10.refs_2_) | copy-start | bytes 786436
  99.0 10.2 %copy-start.6 = (bf16[16,16,512]{2,1,0:T(8,128)(2,1)}, bf16[16,16,512]{2,1,0:T(8,128)(2,1)S(1)}, u32[]{:S(2)}) copy-start(bf16[16,16,512]{2,1,0:T(8,128)(2,1)S(1)} %collective-permute-done.11.refs_3_) | copy-start | bytes 786436
  99.0 8.5 %copy-start.3 = (bf16[16,16,512]{2,1,0:T(8,128)(2,1)S(1)}, bf16[16,16,512]{2,1,0:T(8,128)(2,1)}, u32[]{:S(2)}) copy-start(bf16[16,16,512]{2,1,0:T(8,128)(2,1)} %slice.28.refs_0_) | copy-start | bytes 786436
  99.0 33.4 %all-to-all-start.3 = ((bf16[128,48,128]{2,1,0:T(8,128)(2,1)}), bf16[128,48,128]{2,1,0:T(8,128)(2,1)S(1)}, u32[]{:S(2)}, u32[]{:S(2)}) async-start(bf16[128,48,128]{2,1,0:T(8,128)(2,1)} %bitcast.11), calls=%async_computation.3 | async-start | bytes 3145728 | tf_op jit(solution)/shard_map/all_to_all | solution.py:450
  107.5 2.3 %collective-permute-start.12 = (bf16[16,16,512]{2,1,0:T(8,128)(2,1)S(1)}, bf16[16,16,512]{2,1,0:T(8,128)(2,1)S(1)}, u32[]{:S(2)}, u32[]{:S(2)}) collective-permute-start(bf16[16,16,512]{2,1,0:T(8,128)(2,1)S(1)} %copy-done.3), channel_id=1, source_target_pairs={{0,1},{1,0},{2,3},{3,2},{4,5},{5,4},{6,7},{7,6},{8,9},{9,8},{10,11... | collective-permute-start | bytes 786440 | tf_op jit(solution)/shard_map/ppermute | solution.py:433
  108.6 1.5 %collective-permute-start.13 = (bf16[16,16,512]{2,1,0:T(8,128)(2,1)S(1)}, bf16[16,16,512]{2,1,0:T(8,128)(2,1)S(1)}, u32[]{:S(2)}, u32[]{:S(2)}) collective-permute-start(bf16[16,16,512]{2,1,0:T(8,128)(2,1)S(1)} %collective-permute-done.9.refs_1_), channel_id=1, source_target_pairs={{0,1},{1,0},{2,3},{3,2},{4,5},{5,4},{6,7},{7,6},{8,9},{9,8},{10,11... | collective-permute-start | bytes 786440 | tf_op jit(solution)/shard_map/ppermute | solution.py:433
  108.7 2.2 %collective-permute-start.14 = (bf16[16,16,512]{2,1,0:T(8,128)(2,1)S(1)}, bf16[16,16,512]{2,1,0:T(8,128)(2,1)S(1)}, u32[]{:S(2)}, u32[]{:S(2)}) collective-permute-start(bf16[16,16,512]{2,1,0:T(8,128)(2,1)S(1)} %collective-permute-done.10.refs_2_), channel_id=1, source_target_pairs={{0,1},{1,0},{2,3},{3,2},{4,5},{5,4},{6,7},{7,6},{8,9},{9,8},{10,11... | collective-permute-start | bytes 786440 | tf_op jit(solution)/shard_map/ppermute | solution.py:433
  109.2 1.9 %collective-permute-start.15 = (bf16[16,16,512]{2,1,0:T(8,128)(2,1)S(1)}, bf16[16,16,512]{2,1,0:T(8,128)(2,1)}, u32[]{:S(2)}, u32[]{:S(2)}) collective-permute-start(bf16[16,16,512]{2,1,0:T(8,128)(2,1)S(1)} %collective-permute-done.11.refs_3_), channel_id=1, source_target_pairs={{0,1},{1,0},{2,3},{3,2},{4,5},{5,4},{6,7},{7,6},{8,9},{9,8},{10,11... | collective-permute-start | bytes 786440 | tf_op jit(solution)/shard_map/ppermute | solution.py:433
  109.8 22.6 %copy-start.7 = (bf16[16,16,512]{2,1,0:T(8,128)(2,1)}, bf16[16,16,512]{2,1,0:T(8,128)(2,1)S(1)}, u32[]{:S(2)}) copy-start(bf16[16,16,512]{2,1,0:T(8,128)(2,1)S(1)} %collective-permute-done.12.refs_4_) | copy-start | bytes 786436
  110.2 22.2 %copy-start.8 = (bf16[16,16,512]{2,1,0:T(8,128)(2,1)}, bf16[16,16,512]{2,1,0:T(8,128)(2,1)S(1)}, u32[]{:S(2)}) copy-start(bf16[16,16,512]{2,1,0:T(8,128)(2,1)S(1)} %collective-permute-done.13.refs_5_) | copy-start | bytes 786436
  110.9 21.5 %copy-start.9 = (bf16[16,16,512]{2,1,0:T(8,128)(2,1)}, bf16[16,16,512]{2,1,0:T(8,128)(2,1)S(1)}, u32[]{:S(2)}) copy-start(bf16[16,16,512]{2,1,0:T(8,128)(2,1)S(1)} %collective-permute-done.14.refs_6_) | copy-start | bytes 786436
  132.4 1.2 copy-start.1

commit v7 on v6

--- a/solution.py
+++ b/solution.py
@@ -251,11 +251,9 @@
                 fetch.start()
         put_rows(parts_in[turn * count : (turn + 1) * count], side, (0, 1, 3, 2, 2), (0, 0, 0, 0, lines // 2), w_qkv)
 
-        @pl.loop(0, half, step=TOGETHER)
-        def _(first, side=side):
-            for k in range(TOGETHER):
-                c = side * half + first + k
-                qkv[c] = jnp.dot(hidden[...], w_qkv[c], preferred_element_type=F32).astype(BF16)
+        for k in range(half):
+            c = side * half + k
+            qkv[c] = jnp.dot(hidden[...], w_qkv[c], preferred_element_type=F32).astype(BF16)
 
     third = parts // 3
     per = CHUNK // LANES
@@ -354,18 +352,18 @@
         wide = recv_ref[:, slab(f), :].astype(F32)
         wide = wide.reshape(owners, 2, groups, LANES)
         for i in range(2):
-            heads[i * owners : (i + 1) * owners, :] = wide[:, i].reshape(owners, width).astype(BF16)
-        if f == 0:
-            for copy in fetches:
-                copy.wait()
-            core = lax.rem(lax.axis_index("grp"), 2)
-            for turn in range(2):
-                mine = [parts_in.at[turn * SIDE + k] for k in range(SIDE)]
-                put_rows(mine, core if turn == 0 else 1 - core, (0, 1, 3, 2), (0, 0, 0, 0), w_o)
-        had[f].wait()
+            at = f * tokens + i * owners
+            heads[at : at + owners, :] = wide[:, i].reshape(owners, width).astype(BF16)
+    for copy in fetches + had:
+        copy.wait()
+    core = lax.rem(lax.axis_index("grp"), 2)
+    for turn in range(2):
+        mine = [parts_in.at[turn * SIDE + k] for k in range(SIDE)]
+        put_rows(mine, core if turn == 0 else 1 - core, (0, 1, 3, 2), (0, 0, 0, 0), w_o)
+    for f in range(count):
         for c in range(width // CHUNK):
             cols = pl.ds(c * CHUNK, CHUNK)
-            update = jnp.dot(heads[...], w_o[c], preferred_element_type=F32).astype(BF16)
+            update = jnp.dot(heads[frame(f), :], w_o[c], preferred_element_type=F32).astype(BF16)
             out_ref[frame(f), cols] = (mixed_ref[frame(f), cols].astype(F32) + update.astype(F32)).astype(BF16)
         gives[f].start()
     for give in gives:
@@ -388,13 +386,13 @@
             pltpu.VMEM(mixed.shape, BF16),
             pltpu.VMEM((len(weights), lines, rows, cols), BF16),
             pltpu.VMEM((2 * cols // CHUNK, width, CHUNK), BF16),
-            pltpu.VMEM((tokens, width), BF16),
+            pltpu.VMEM(mixed.shape, BF16),
             pltpu.SemaphoreType.DMA((count,)),
             pltpu.SemaphoreType.DMA((count,)),
             pltpu.SemaphoreType.DMA((len(weights),)),
             pltpu.SemaphoreType.DMA((count,)),
         ],
-        compiler_params=pltpu.CompilerParams(vmem_limit_bytes=VMEM - 2 * 2**20),
+        compiler_params=pltpu.CompilerParams(vmem_limit_bytes=VMEM),
         cost_estimate=pl.CostEstimate(flops=2 * 10**9, bytes_accessed=6 * 2**20, transcendentals=0),
         name="finish",
     )(mixed, recv, *weights)

time: 140 us -> 139 us (level)
  no operation moved by 1% of the time
where the time goes in v7:
time: 139 us
  starting transfers between devices  48.4 us (35%)
  waiting for transfers between devices  42.3 us (30%)
  Pallas kernels  36.3 us (26%)
  local copies, waits for them, and re-layouts  6.61 us (5%)
  blocking collectives  4.86 us (3%)
    all_to_all x2, waiting for transfers between devices, exchange(): return lax.all_to_all(blocks, AXES, split_axis=0, concat_axis=0, tiled=True)  21.3 us
    ppermute x7, waiting for transfers between devices, along_x(): return lax.ppermute(part, AXES, pairs)  18.6 us
    all_to_all x2, starting transfers between devices, exchange(): return lax.all_to_all(blocks, AXES, split_axis=0, concat_axis=0, tiled=True)  16.8 us
    pallas_call x1, Pallas kernels, spatial(): pl.pallas_call(functools.partial(spatial_kernel, tokens), out_shape=(jax....  15.6 us
    pallas_call x1, Pallas kernels, temporal(): pl.pallas_call(functools.partial(temporal_kernel, local_pos), out_shape=j...  15.2 us
    ppermute x9, starting transfers between devices, from_sibling(): return lax.ppermute(part, AXES, [(k, k ^ 1) for k in range(count)])  14.7 us
    ppermute x7, starting transfers between devices, along_x(): return lax.ppermute(part, AXES, pairs)  9.03 us
    all_to_all x1, starting transfers between devices, spread(): lax.all_to_all(copies, AXES, split_axis=0, concat_axis=0, tiled=True, axi...  7.85 us
  transfers between devices with their start and end apart: 19, of which 8 were waited for; matrix products, arithmetic and copies ran while one was open for 2% of the time, Pallas kernels for 22%

profile of v7, /device:TPU:1, one launch (start us, length us, event | category | flops | bytes accessed | tf_op | source)
XLA Modules:
  0.0 138.8 jit_solution(17142268589633693960)
XLA Ops:
  0.0 0.7 fusion.1
  0.7 0.8 fusion
  1.5 4.9 %all_to_all.31 = bf16[8,2,2048]{2,0,1:T(8,128)(2,1)S(1)} all-to-all(bf16[8,2,2048]{2,0,1:T(8,128)(2,1)S(1)} %bitcast.13), channel_id=1, replica_groups={{0,1},{2,3},{4,5},{6,7},{8,9},{10,11},{12,13},{14,15},{16,17},{18,19},{..., dimensions={1} | all-to-all | bytes 131072 | tf_op jit(solution)/shard_map/all_to_all | solution.py:412
  6.3 1.1 broadcast_in_dim.9
  7.5 7.9 %all-to-all-start.1 = ((bf16[16,16,2048]{2,1,0:T(8,128)(2,1)}), bf16[16,16,2048]{2,1,0:T(8,128)(2,1)S(1)}, u32[]{:S(2)}, u32[]{:S(2)}) async-start(bf16[16,16,2048]{2,1,0:T(8,128)(2,1)} %broadcast_in_dim.9), calls=%async_computation.1 | async-start | bytes 2097152 | tf_op jit(solution)/shard_map/all_to_all | solution.py:419
  15.3 15.6 %spatial.1 = (bf16[768,1024]{1,0:T(8,128)(2,1)}, bf16[128,48,128]{2,1,0:T(8,128)(2,1)}) custom-call(bf16[768,1024]{1,0:T(8,128)(2,1)} %bitcast.14, f32[1,1024]{1,0:T(1,128)} %bitcast.15, f32[1,1024]{1,0:T(1,128)} %bitcast.16, bf16[1024,3072]{1,0:T(8,128)(2,1)} %w_qkv_hbm.1, bf16[1024,1024]{1,0:T(8,128)(2,1)} %w_o_hbm.1), custom_call_target="tpu_custom_call" | custom-call | flops 16000000000 | bytes 14680064 | tf_op jit(solution)/shard_map/spatial/pallas_call | solution.py:157
  30.9 0.8 all-to-all-done.1
  31.8 1.3 collective-permute-start
  33.0 1.5 %collective-permute-start.1 = (bf16[16,16,1536]{2,1,0:T(8,128)(2,1)S(1)}, bf16[16,16,1536]{2,1,0:T(8,128)(2,1)}, u32[]{:S(2)}, u32[]{:S(2)}) collective-permute-start(bf16[16,16,1536]{2,1,0:T(8,128)(2,1)S(1)} %slice.29.refs_0_), channel_id=1, source_target_pairs={{0,6},{1,7},{2,0},{3,1},{4,2},{5,3},{6,4},{7,5},{8,14},{9,15},{10,... | collective-permute-start | bytes 2359304 | tf_op jit(solution)/shard_map/ppermute | solution.py:426
  34.5 8.4 %all-to-all-start.2 = ((bf16[128,48,128]{2,1,0:T(8,128)(2,1)}), bf16[128,48,128]{2,1,0:T(8,128)(2,1)S(1)}, u32[]{:S(2)}, u32[]{:S(2)}) async-start(bf16[128,48,128]{2,1,0:T(8,128)(2,1)} %get-tuple-element.22), calls=%async_computation.2 | async-start | bytes 3145728 | tf_op jit(solution)/shard_map/all_to_all | solution.py:448
  42.9 1.1 collective-permute-start.4
  44.1 6.0 %collective-permute-done.refs_1_ = bf16[16,16,1536]{2,1,0:T(8,128)(2,1)} collective-permute-done((bf16[16,16,1536]{2,1,0:T(8,128)(2,1)S(1)}, bf16[16,16,1536]{2,1,0:T(8,128)(2,1)}, u32[]{:S(2)}, u32[]{:S(2)}) %collective-permute-start) | collective-permute-done | bytes 786464 | tf_op jit(solution)/shard_map/ppermute | solution.py:426
  50.1 1.0 slice.32
  51.1 1.0 slice.33
  52.3 8.5 %collective-permute-start.5 = (bf16[16,16,1536]{2,1,0:T(8,128)(2,1)}, bf16[16,16,1536]{2,1,0:T(8,128)(2,1)}, u32[]{:S(2)}, u32[]{:S(2)}) collective-permute-start(bf16[16,16,1536]{2,1,0:T(8,128)(2,1)} %collective-permute-done.refs_1_), channel_id=1, source_target_pairs={{0,1},{1,0},{2,3},{3,2},{4,5},{5,4},{6,7},{7,6},{8,9},{9,8},{10,11... | collective-permute-start | bytes 2359304 | tf_op jit(solution)/shard_map/ppermute | solution.py:431
  60.8 2.0 %collective-permute-start.3 = (bf16[8,16,1536]{2,1,0:T(8,128)(2,1)S(1)}, bf16[8,16,1536]{2,1,0:T(8,128)(2,1)}, u32[]{:S(2)}, u32[]{:S(2)}) collective-permute-start(bf16[8,16,1536]{2,1,0:T(8,128)(2,1)S(1)} %slice.33), channel_id=1, source_target_pairs={{0,6},{1,7},{2,0},{3,1},{4,2},{5,3},{6,4},{7,5},{8,14},{9,15},{10,... | collective-permute-start | bytes 1179656 | tf_op jit(solution)/shard_map/ppermute | solution.py:426
  62.8 12.6 %collective-permute-done.2.refs_3_ = bf16[8,16,1536]{2,1,0:T(8,128)(2,1)} collective-permute-done((bf16[8,16,1536]{2,1,0:T(8,128)(2,1)S(1)}, bf16[8,16,1536]{2,1,0:T(8,128)(2,1)}, u32[]{:S(2)}, u32[]{:S(2)}) %collective-permute-start.2) | collective-permute-done | bytes 393248 | tf_op jit(solution)/shard_map/ppermute | solution.py:426
  75.4 3.0 %collective-permute-start.7 = (bf16[8,16,1536]{2,1,0:T(8,128)(2,1)}, bf16[8,16,1536]{2,1,0:T(8,128)(2,1)}, u32[]{:S(2)}, u32[]{:S(2)}) collective-permute-start(bf16[8,16,1536]{2,1,0:T(8,128)(2,1)} %collective-permute-done.2.refs_3_), channel_id=1, source_target_pairs={{0,1},{1,0},{2,3},{3,2},{4,5},{5,4},{6,7},{7,6},{8,9},{9,8},{10,11... | collective-permute-start | bytes 1179656 | tf_op jit(solution)/shard_map/ppermute | solution.py:431
  78.4 0.7 slice.28.refs_0_
  79.1 1.5 %collective-permute-start.9 = (bf16[16,16,512]{2,1,0:T(8,128)(2,1)}, bf16[16,16,512]{2,1,0:T(8,128)(2,1)S(1)}, u32[]{:S(2)}, u32[]{:S(2)}) collective-permute-start(bf16[16,16,512]{2,1,0:T(8,128)(2,1)} %slice.28.refs_0_), channel_id=1, source_target_pairs={{0,2},{1,3},{2,4},{3,5},{4,6},{5,7},{6,0},{7,1},{8,10},{9,11},{10,... | collective-permute-start | bytes 786440 | tf_op jit(solution)/shard_map/ppermute | solution.py:426
  80.6 1.6 %collective-permute-start.10 = (bf16[16,16,512]{2,1,0:T(8,128)(2,1)}, bf16[16,16,512]{2,1,0:T(8,128)(2,1)S(1)}, u32[]{:S(2)}, u32[]{:S(2)}) collective-permute-start(bf16[16,16,512]{2,1,0:T(8,128)(2,1)} %slice.28.refs_0_), channel_id=1, source_target_pairs={{0,6},{1,7},{2,0},{3,1},{4,2},{5,3},{6,4},{7,5},{8,14},{9,15},{10,... | collective-permute-start | bytes 786440 | tf_op jit(solution)/shard_map/ppermute | solution.py:426
  82.2 1.2 collective-permute-start.11
  83.3 15.2 %temporal.1 = bf16[6144,128]{1,0:T(8,128)(2,1)} custom-call(s32[48]{0:T(128)} %len_ref.1, bf16[6144,128]{1,0:T(8,128)(2,1)} %bitcast.10, bf16[16,16,1536]{2,1,0:T(8,128)(2,1)} %copy-done.2, bf16[16,16,1536]{2,1,0:T(8,128)(2,1)} %collective-permute-done.refs_1_, bf16[16,16,1536]{2,1,0:T(8,128)(2,1)} %collective-permute-done.1.refs_2_, ...), custom_call_target="tpu_custom_call" | custom-call | flops 16000000000 | bytes 14680064 | tf_op jit(solution)/shard_map/temporal/pallas_call | solution.py:295
  98.6 8.5 %all-to-all-start.3 = ((bf16[128,48,128]{2,1,0:T(8,128)(2,1)}), bf16[128,48,128]{2,1,0:T(8,128)(2,1)S(1)}, u32[]{:S(2)}, u32[]{:S(2)}) async-start(bf16[128,48,128]{2,1,0:T(8,128)(2,1)} %bitcast.11), calls=%async_computation.3 | async-start | bytes 3145728 | tf_op jit(solution)/shard_map/all_to_all | solution.py:448
  107.1 1.1 collective-permute-start.12
  108.3 0.4 collective-permute-start.14
  109.4 0.4 collective-permute-done.13.refs_5_
  109.8 0.4 collective-permute-done.14.refs_6_
  110.1 0.5 collective-permute-done.15.refs_7_
  110.6 21.3 %all-to-all-done.3.recv_hbm = bf16[128,48,128]{2,1,0:T(8,128)(2,1)S(1)} async-done(((bf16[128,48,128]{2,1,0:T(8,128)(2,1)}), bf16[128,48,128]{2,1,0:T(8,128)(2,1)S(1)}, u32[]{:S(2)}, u32[]{:S(2)}) %all-to-all-start.3) | async-done | bytes 1572896 | tf_op jit(solution)/shard_map/all_to_all | solution.py:448
  132.0 1.1 copy-done.1
  133.1 5.5 %finish.1 = bf16[768,1024]{1,0:T(8,128)(2,1)} custom-call(bf16[768,1024]{1,0:T(8,128)(2,1)} %get-tuple-element.20.mixed_hbm, bf16[128,48,128]{2,1,0:T(8,128)(2,1)} %copy-done.1, bf16[16,16,512]{2,1,0:T(8,128)(2,1)} %slice.28.refs_0_, bf16[16,16,512]{2,1,0:T(8,128)(2,1)} %copy-done.4, bf16[16,16,512]{2,1,0:T(8,128)(2,1)} %copy-done.5, ...), custom_call_target="tpu_custom_call" | custom-call | flops 2000000000 | bytes 6291456 | tf_op jit(solution)/shard_map/finish/pallas_call | solution.py:378
  (38 shorter events, 1.0 us)
Async XLA Ops:
  7.5 24.2 %all-to-all-start.1 = ((bf16[16,16,2048]{2,1,0:T(8,128)(2,1)}), bf16[16,16,2048]{2,1,0:T(8,128)(2,1)S(1)}, u32[]{:S(2)}, u32[]{:S(2)}) async-start(bf16[16,16,2048]{2,1,0:T(8,128)(2,1)} %broadcast_in_dim.9), calls=%async_computation.1 | async-start | bytes 2097152 | tf_op jit(solution)/shard_map/all_to_all | solution.py:419
  31.8 11.2 %copy-start.2 = (bf16[16,16,1536]{2,1,0:T(8,128)(2,1)}, bf16[16,16,1536]{2,1,0:T(8,128)(2,1)S(1)}, u32[]{:S(2)}) copy-start(bf16[16,16,1536]{2,1,0:T(8,128)(2,1)S(1)} %slice.29.refs_0_) | copy-start | bytes 2359300
  31.8 18.3 %collective-permute-start = (bf16[16,16,1536]{2,1,0:T(8,128)(2,1)S(1)}, bf16[16,16,1536]{2,1,0:T(8,128)(2,1)}, u32[]{:S(2)}, u32[]{:S(2)}) collective-permute-start(bf16[16,16,1536]{2,1,0:T(8,128)(2,1)S(1)} %slice.29.refs_0_), channel_id=1, source_target_pairs={{0,2},{1,3},{2,4},{3,5},{4,6},{5,7},{6,0},{7,1},{8,10},{9,11},{10,... | collective-permute-start | bytes 2359304 | tf_op jit(solution)/shard_map/ppermute | solution.py:426
  33.0 18.1 %collective-permute-start.1 = (bf16[16,16,1536]{2,1,0:T(8,128)(2,1)S(1)}, bf16[16,16,1536]{2,1,0:T(8,128)(2,1)}, u32[]{:S(2)}, u32[]{:S(2)}) collective-permute-start(bf16[16,16,1536]{2,1,0:T(8,128)(2,1)S(1)} %slice.29.refs_0_), channel_id=1, source_target_pairs={{0,6},{1,7},{2,0},{3,1},{4,2},{5,3},{6,4},{7,5},{8,14},{9,15},{10,... | collective-permute-start | bytes 2359304 | tf_op jit(solution)/shard_map/ppermute | solution.py:426
  34.5 44.6 %all-to-all-start.2 = ((bf16[128,48,128]{2,1,0:T(8,128)(2,1)}), bf16[128,48,128]{2,1,0:T(8,128)(2,1)S(1)}, u32[]{:S(2)}, u32[]{:S(2)}) async-start(bf16[128,48,128]{2,1,0:T(8,128)(2,1)} %get-tuple-element.22), calls=%async_computation.2 | async-start | bytes 3145728 | tf_op jit(solution)/shard_map/all_to_all | solution.py:448
  42.9 36.2 %collective-permute-start.4 = (bf16[16,16,1536]{2,1,0:T(8,128)(2,1)S(1)}, bf16[16,16,1536]{2,1,0:T(8,128)(2,1)}, u32[]{:S(2)}, u32[]{:S(2)}) collective-permute-start(bf16[16,16,1536]{2,1,0:T(8,128)(2,1)S(1)} %slice.29.refs_0_), channel_id=1, source_target_pairs={{0,1},{1,0},{2,3},{3,2},{4,5},{5,4},{6,7},{7,6},{8,9},{9,8},{10,11... | collective-permute-start | bytes 2359304 | tf_op jit(solution)/shard_map/ppermute | solution.py:431
  52.2 23.2 %collective-permute-start.2 = (bf16[8,16,1536]{2,1,0:T(8,128)(2,1)S(1)}, bf16[8,16,1536]{2,1,0:T(8,128)(2,1)}, u32[]{:S(2)}, u32[]{:S(2)}) collective-permute-start(bf16[8,16,1536]{2,1,0:T(8,128)(2,1)S(1)} %slice.32), channel_id=1, source_target_pairs={{0,2},{1,3},{2,4},{3,5},{4,6},{5,7},{6,0},{7,1},{8,10},{9,11},{10,... | collective-permute-start | bytes 1179656 | tf_op jit(solution)/shard_map/ppermute | solution.py:426
  52.3 28.3 %collective-permute-start.5 = (bf16[16,16,1536]{2,1,0:T(8,128)(2,1)}, bf16[16,16,1536]{2,1,0:T(8,128)(2,1)}, u32[]{:S(2)}, u32[]{:S(2)}) collective-permute-start(bf16[16,16,1536]{2,1,0:T(8,128)(2,1)} %collective-permute-done.refs_1_), channel_id=1, source_target_pairs={{0,1},{1,0},{2,3},{3,2},{4,5},{5,4},{6,7},{7,6},{8,9},{9,8},{10,11... | collective-permute-start | bytes 2359304 | tf_op jit(solution)/shard_map/ppermute | solution.py:431
  60.8 21.4 %collective-permute-start.6 = (bf16[16,16,1536]{2,1,0:T(8,128)(2,1)}, bf16[16,16,1536]{2,1,0:T(8,128)(2,1)}, u32[]{:S(2)}, u32[]{:S(2)}) collective-permute-start(bf16[16,16,1536]{2,1,0:T(8,128)(2,1)} %collective-permute-done.1.refs_2_), channel_id=1, source_target_pairs={{0,1},{1,0},{2,3},{3,2},{4,5},{5,4},{6,7},{7,6},{8,9},{9,8},{10,11... | collective-permute-start | bytes 2359304 | tf_op jit(solution)/shard_map/ppermute | solution.py:431
  60.8 17.6 %collective-permute-start.3 = (bf16[8,16,1536]{2,1,0:T(8,128)(2,1)S(1)}, bf16[8,16,1536]{2,1,0:T(8,128)(2,1)}, u32[]{:S(2)}, u32[]{:S(2)}) collective-permute-start(bf16[8,16,1536]{2,1,0:T(8,128)(2,1)S(1)} %slice.33), channel_id=1, source_target_pairs={{0,6},{1,7},{2,0},{3,1},{4,2},{5,3},{6,4},{7,5},{8,14},{9,15},{10,... | collective-permute-start | bytes 1179656 | tf_op jit(solution)/shard_map/ppermute | solution.py:426
  75.4 7.9 %collective-permute-start.7 = (bf16[8,16,1536]{2,1,0:T(8,128)(2,1)}, bf16[8,16,1536]{2,1,0:T(8,128)(2,1)}, u32[]{:S(2)}, u32[]{:S(2)}) collective-permute-start(bf16[8,16,1536]{2,1,0:T(8,128)(2,1)} %collective-permute-done.2.refs_3_), channel_id=1, source_target_pairs={{0,1},{1,0},{2,3},{3,2},{4,5},{5,4},{6,7},{7,6},{8,9},{9,8},{10,11... | collective-permute-start | bytes 1179656 | tf_op jit(solution)/shard_map/ppermute | solution.py:431
  78.4 4.9 %collective-permute-start.8 = (bf16[8,16,1536]{2,1,0:T(8,128)(2,1)}, bf16[8,16,1536]{2,1,0:T(8,128)(2,1)}, u32[]{:S(2)}, u32[]{:S(2)}) collective-permute-start(bf16[8,16,1536]{2,1,0:T(8,128)(2,1)} %collective-permute-done.3.refs_4_), channel_id=1, source_target_pairs={{0,1},{1,0},{2,3},{3,2},{4,5},{5,4},{6,7},{7,6},{8,9},{9,8},{10,11... | collective-permute-start | bytes 1179656 | tf_op jit(solution)/shard_map/ppermute | solution.py:431
  79.1 4.2 %copy-start = (bf16[128,48,128]{2,1,0:T(8,128)(2,1)}, bf16[128,48,128]{2,1,0:T(8,128)(2,1)S(1)}, u32[]{:S(2)}) copy-start(bf16[128,48,128]{2,1,0:T(8,128)(2,1)S(1)} %all-to-all-done.2) | copy-start | bytes 4718596
  79.1 19.4 %collective-permute-start.9 = (bf16[16,16,512]{2,1,0:T(8,128)(2,1)}, bf16[16,16,512]{2,1,0:T(8,128)(2,1)S(1)}, u32[]{:S(2)}, u32[]{:S(2)}) collective-permute-start(bf16[16,16,512]{2,1,0:T(8,128)(2,1)} %slice.28.refs_0_), channel_id=1, source_target_pairs={{0,2},{1,3},{2,4},{3,5},{4,6},{5,7},{6,0},{7,1},{8,10},{9,11},{10,... | collective-permute-start | bytes 786440 | tf_op jit(solution)/shard_map/ppermute | solution.py:426
  80.6 18.0 %collective-permute-start.10 = (bf16[16,16,512]{2,1,0:T(8,128)(2,1)}, bf16[16,16,512]{2,1,0:T(8,128)(2,1)S(1)}, u32[]{:S(2)}, u32[]{:S(2)}) collective-permute-start(bf16[16,16,512]{2,1,0:T(8,128)(2,1)} %slice.28.refs_0_), channel_id=1, source_target_pairs={{0,6},{1,7},{2,0},{3,1},{4,2},{5,3},{6,4},{7,5},{8,14},{9,15},{10,... | collective-permute-start | bytes 786440 | tf_op jit(solution)/shard_map/ppermute | solution.py:426
  82.2 16.4 %collective-permute-start.11 = (bf16[16,16,512]{2,1,0:T(8,128)(2,1)}, bf16[16,16,512]{2,1,0:T(8,128)(2,1)S(1)}, u32[]{:S(2)}, u32[]{:S(2)}) collective-permute-start(bf16[16,16,512]{2,1,0:T(8,128)(2,1)} %slice.28.refs_0_), channel_id=1, source_target_pairs={{0,4},{1,5},{2,6},{3,7},{4,0},{5,1},{6,2},{7,3},{8,12},{9,13},{10,... | collective-permute-start | bytes 786440 | tf_op jit(solution)/shard_map/ppermute | solution.py:426
  98.5 9.7 %copy-start.4 = (bf16[16,16,512]{2,1,0:T(8,128)(2,1)}, bf16[16,16,512]{2,1,0:T(8,128)(2,1)S(1)}, u32[]{:S(2)}) copy-start(bf16[16,16,512]{2,1,0:T(8,128)(2,1)S(1)} %collective-permute-done.9.refs_1_) | copy-start | bytes 786436
  98.6 9.8 %copy-start.5 = (bf16[16,16,512]{2,1,0:T(8,128)(2,1)}, bf16[16,16,512]{2,1,0:T(8,128)(2,1)S(1)}, u32[]{:S(2)}) copy-start(bf16[16,16,512]{2,1,0:T(8,128)(2,1)S(1)} %collective-permute-done.10.refs_2_) | copy-start | bytes 786436
  98.6 10.2 %copy-start.6 = (bf16[16,16,512]{2,1,0:T(8,128)(2,1)}, bf16[16,16,512]{2,1,0:T(8,128)(2,1)S(1)}, u32[]{:S(2)}) copy-start(bf16[16,16,512]{2,1,0:T(8,128)(2,1)S(1)} %collective-permute-done.11.refs_3_) | copy-start | bytes 786436
  98.6 8.5 %copy-start.3 = (bf16[16,16,512]{2,1,0:T(8,128)(2,1)S(1)}, bf16[16,16,512]{2,1,0:T(8,128)(2,1)}, u32[]{:S(2)}) copy-start(bf16[16,16,512]{2,1,0:T(8,128)(2,1)} %slice.28.refs_0_) | copy-start | bytes 786436
  98.6 33.4 %all-to-all-start.3 = ((bf16[128,48,128]{2,1,0:T(8,128)(2,1)}), bf16[128,48,128]{2,1,0:T(8,128)(2,1)S(1)}, u32[]{:S(2)}, u32[]{:S(2)}) async-start(bf16[128,48,128]{2,1,0:T(8,128)(2,1)} %bitcast.11), calls=%async_computation.3 | async-start | bytes 3145728 | tf_op jit(solution)/shard_map/all_to_all | solution.py:448
  107.1 2.3 %collective-permute-start.12 = (bf16[16,16,512]{2,1,0:T(8,128)(2,1)S(1)}, bf16[16,16,512]{2,1,0:T(8,128)(2,1)S(1)}, u32[]{:S(2)}, u32[]{:S(2)}) collective-permute-start(bf16[16,16,512]{2,1,0:T(8,128)(2,1)S(1)} %copy-done.3), channel_id=1, source_target_pairs={{0,1},{1,0},{2,3},{3,2},{4,5},{5,4},{6,7},{7,6},{8,9},{9,8},{10,11... | collective-permute-start | bytes 786440 | tf_op jit(solution)/shard_map/ppermute | solution.py:431
  108.2 1.5 %collective-permute-start.13 = (bf16[16,16,512]{2,1,0:T(8,128)(2,1)S(1)}, bf16[16,16,512]{2,1,0:T(8,128)(2,1)S(1)}, u32[]{:S(2)}, u32[]{:S(2)}) collective-permute-start(bf16[16,16,512]{2,1,0:T(8,128)(2,1)S(1)} %collective-permute-done.9.refs_1_), channel_id=1, source_target_pairs={{0,1},{1,0},{2,3},{3,2},{4,5},{5,4},{6,7},{7,6},{8,9},{9,8},{10,11... | collective-permute-start | bytes 786440 | tf_op jit(solution)/shard_map/ppermute | solution.py:431
  108.3 1.8 %collective-permute-start.14 = (bf16[16,16,512]{2,1,0:T(8,128)(2,1)S(1)}, bf16[16,16,512]{2,1,0:T(8,128)(2,1)S(1)}, u32[]{:S(2)}, u32[]{:S(2)}) collective-permute-start(bf16[16,16,512]{2,1,0:T(8,128)(2,1)S(1)} %collective-permute-done.10.refs_2_), channel_id=1, source_target_pairs={{0,1},{1,0},{2,3},{3,2},{4,5},{5,4},{6,7},{7,6},{8,9},{9,8},{10,11... | collective-permute-start | bytes 786440 | tf_op jit(solution)/shard_map/ppermute | solution.py:431
  108.7 1.9 %collective-permute-start.15 = (bf16[16,16,512]{2,1,0:T(8,128)(2,1)S(1)}, bf16[16,16,512]{2,1,0:T(8,128)(2,1)}, u32[]{:S(2)}, u32[]{:S(2)}) collective-permute-start(bf16[16,16,512]{2,1,0:T(8,128)(2,1)S(1)} %collective-permute-done.11.refs_3_), channel_id=1, source_target_pairs={{0,1},{1,0},{2,3},{3,2},{4,5},{5,4},{6,7},{7,6},{8,9},{9,8},{10,11... | collective-permute-start | bytes 786440 | tf_op jit(solution)/shard_map/ppermute | solution.py:431
  109.4 22.6 %copy-start.7 = (bf16[16,16,512]{2,1,0:T(8,128)(2,1)}, bf16[16,16,512]{2,1,0:T(8,128)(2,1)S(1)}, u32[]{:S(2)}) copy-start(bf16[16,16,512]{2,1,0:T(8,128)(2,1)S(1)} %collective-permute-done.12.refs_4_) | copy-start | bytes 786436
  109.8 22.2 %copy-start.8 = (bf16[16,16,512]{2,1,0:T(8,128)(2,1)}, bf16[16,16,512]{2,1,0:T(8,128)(2,1)S(1)}, u32[]{:S(2)}) copy-start(bf16[16,16,512]{2,1,0:T(8,128)(2,1)S(1)} %collective-permute-done.13.refs_5_) | copy-start | bytes 786436
  110.1 21.9 %copy-start.9 = (bf16[16,16,512]{2,1,0:T(8,128)(2,1)}, bf16[16,16,512]{2,1,0:T(8,128)(2,1)S(1)}, u32[]{:S(2)}) copy-start(bf16[16,16,512]{2,1,0:T(8,128)(2,1)S(1)} %collective-permute-done.14.refs_6_) | copy-start | bytes 786436
  132.0 1.2 copy-start.1
